TPU v7x, 256 devices: a whole 4x4x8 slice. The times are simulated.
256 devices in a mesh: ta: 4 (over z_hi), ha: 8 (over x, core), wa: 8 (over y, z_lo).
Axes of the slice: x: 4, y: 4, z: 8 (z_hi: 4, z_lo: 2; z = z_hi * 2 + z_lo), core: 2. Of those that a mesh axis runs over, the one named last changes fastest.
Arguments:
- clip: bfloat16 [8, 32, 128, 256], P('ta', 'ha', 'wa'), may hold values from -6 to 6
- conv_weight: bfloat16 [6912, 256], replicated, may hold values from -0.078125 to 0.078125
- down_weight: bfloat16 [6912, 256], replicated, may hold values from -0.078125 to 0.078125
- out_cotangent: bfloat16 [4, 16, 64, 256], P('ta', 'ha', 'wa'), may hold values from -6 to 6
Outputs:
- grad_clip: bfloat16 [8, 32, 128, 256], P('ta', 'ha', 'wa')
- grad_conv: float32 [6912, 256], P(('ha', 'wa'), 'ta')
- grad_down: float32 [6912, 256], P(('ha', 'wa'), 'ta')
All inputs are finite; a program needn't handle non-finite values.
Results may differ from a plain program's by a relative error of at most 0.014.
Values may be sent and summed in bfloat16 or wider, within the bound.
No kernel may reach another device: no remote copies, remote signals or barrier semaphores. Data moves between devices by JAX's collectives and lax.ppermute only.
A program may use at most 64 MiB of HBM per device.

v0:
```python
import jax
import jax.numpy as jnp
from jax import lax
from jax.sharding import PartitionSpec as P


def from_behind(x, axis, by):
    count = lax.axis_size(axis)
    pairs = [(i, i + by) for i in range(count) if 0 <= i + by < count]
    return lax.ppermute(x, axis, pairs)


def padded(block, sides, width):
    for axis, dim in sides:
        count = lax.axis_size(axis)
        forward = [(i, i + 1) for i in range(count - 1)]
        backward = [(target, source) for source, target in forward]
        low = lax.ppermute(
            lax.slice_in_dim(block, block.shape[dim] - width, None, axis=dim), axis, forward
        )
        high = lax.ppermute(lax.slice_in_dim(block, 0, width, axis=dim), axis, backward)
        block = jnp.concatenate([low, block, high], axis=dim)
    return block


def extend_past(values):
    earlier = from_behind(values[-2:], "ta", 1)
    return jnp.concatenate([earlier, values], axis=0)


def extend_next(values, frames):
    later = from_behind(values[:frames], "ta", -1)
    return jnp.concatenate([values, later], axis=0)


def with_rims(values):
    return padded(values, (("ha", 1), ("wa", 2)), 1)


def convolve(inputs, kernel, specs, padding, lhs_step, rhs_step):
    return lax.conv_general_dilated(
        inputs,
        kernel,
        (1, 1, 1),
        padding,
        lhs_dilation=lhs_step,
        rhs_dilation=rhs_step,
        dimension_numbers=specs,
        preferred_element_type=jnp.float32,
    )


def local(clip, conv_weight, down_weight, out_cotangent):
    channels = clip.shape[-1]
    share = channels // lax.axis_size("ta")
    first_kernel = conv_weight.reshape(3, 3, 3, channels, channels)
    down_kernel = down_weight.reshape(3, 3, 3, channels, channels)
    coarse_t, coarse_h, coarse_w = (
        out_cotangent.shape[0],
        out_cotangent.shape[1],
        out_cotangent.shape[2],
    )
    unit = (1, 1, 1)
    valid = [(0, 0), (0, 0), (0, 0)]
    forward_specs = ("NDHWC", "DHWIO", "NDHWC")
    back_specs = ("NDHWC", "DHWOI", "NDHWC")
    weight_specs = ("CDHWN", "IDHWO", "DHWNC")
    padded_clip = with_rims(extend_past(clip))
    pre_act = convolve(padded_clip[None], first_kernel, forward_specs, valid, unit, unit)[0]
    activation = jax.nn.silu(pre_act).astype(jnp.bfloat16)
    padded_act = with_rims(extend_past(activation))
    act_window = padded_act[: 2 * coarse_t + 1, : 2 * coarse_h + 1, : 2 * coarse_w + 1]
    clip_blocks, act_blocks = (
        lax.all_gather(padded_clip[None], "ta", axis=0, tiled=True),
        lax.all_gather(act_window[None], "ta", axis=0, tiled=True),
    )
    coarse_ext = with_rims(extend_next(out_cotangent, 1))[:, 1:, 1:]
    flipped_down = down_kernel[::-1, ::-1, ::-1]
    grad_act = convolve(
        coarse_ext[None], flipped_down, back_specs, [(0, 1), (1, 0), (1, 0)], (2, 2, 2), unit
    )[0]
    sigma = jax.nn.sigmoid(pre_act)
    grad_pre = (grad_act * sigma * (1.0 + pre_act * (1.0 - sigma))).astype(jnp.bfloat16)
    padded_grad = with_rims(extend_next(grad_pre, 2))
    flipped_first = first_kernel[::-1, ::-1, ::-1]
    grad_clip = convolve(padded_grad[None], flipped_first, back_specs, valid, unit, unit)[0].astype(
        jnp.bfloat16
    )
    start = lax.axis_index("ta") * share
    cot_all = lax.all_gather(out_cotangent[None], "ta", axis=0, tiled=True)
    grad_all = lax.all_gather(grad_pre[None], "ta", axis=0, tiled=True)
    cot_blocks = lax.dynamic_slice_in_dim(cot_all, start, share, 4)
    grad_blocks = lax.dynamic_slice_in_dim(grad_all, start, share, 4)
    grad_down = convolve(act_blocks, cot_blocks, weight_specs, valid, unit, (2, 2, 2))
    grad_conv = convolve(clip_blocks, grad_blocks, weight_specs, valid, unit, unit)
    terms = (grad_conv.reshape(27 * channels, share), grad_down.reshape(27 * channels, share))
    totals = (
        lax.psum_scatter(terms[0], ("ha", "wa"), scatter_dimension=0, tiled=True),
        lax.psum_scatter(terms[1], ("ha", "wa"), scatter_dimension=0, tiled=True),
    )
    return (grad_clip, totals[0], totals[1])


def solution(mesh):
    return jax.shard_map(
        local,
        mesh=mesh,
        in_specs=(P("ta", "ha", "wa", None), P(), P(), P("ta", "ha", "wa", None)),
        out_specs=(P("ta", "ha", "wa", None), P(("ha", "wa"), "ta"), P(("ha", "wa"), "ta")),
        check_vma=False,
    )
```

profile of v0, /device:TPU:1, one launch (start us, length us, event | category | flops | bytes accessed | tf_op | source)
XLA Modules:
  0.0 725.1 jit_solution(650782564747855269)
XLA Ops:
  7.2 0.0 copy-start
  7.2 0.0 all-reduce.5.cloned.1.call-start
  7.2 6.6 collective-permute-start.4
  13.8 1.3 collective-permute-start
  15.1 16.0 %all-gather.2 = bf16[4,2,8,256]{3,2,1,0:T(8,128)(2,1)} all-gather(bf16[1,2,8,256]{3,2,1,0:T(8,128)(2,1)} %param.7), channel_id=4, replica_groups=mesh['ta'=4,'ha'=8,'wa'=8] {'ta'}, dimensions={0}, use_global_device_ids=true | all-gather | bytes 40960 | tf_op jit(solution)/shard_map/all_gather | solution.py:90
  31.1 0.8 constant_dynamic-slice_fusion.2
  31.9 0.7 constant_dynamic-update-slice_fusion.1
  32.6 0.7 constant_dynamic-update-slice_fusion
  33.3 6.0 collective-permute-start.2
  39.4 3.0 collective-permute-start.1
  42.4 0.8 constant_dynamic-update-slice_fusion.3
  43.3 0.8 constant_dynamic-update-slice_fusion.2
  44.1 1.9 collective-permute-start.6
  46.0 3.6 collective-permute-start.5
  49.7 1.3 collective-permute-start.3
  51.1 1.3 collective-permute-start.8
  52.4 4.6 collective-permute-start.7
  57.1 0.9 collective-permute-done.7
  57.9 0.2 pad_maximum_fusion
  58.1 0.1 copy.96
  58.2 0.1 pad.clone
  58.5 0.9 add_divide_fusion
  59.4 0.1 copy.64
  59.5 0.1 copy.73
  59.6 0.1 copy.71
  59.7 20.7 %all-gather = bf16[16,6,18,256]{3,2,1,0:T(8,128)(2,1)S(1)} all-gather(bf16[4,6,18,256]{3,2,1,0:T(8,128)(2,1)S(1)} %get-tuple-element.14), channel_id=2, replica_groups=mesh['ta'=4,'ha'=8,'wa'=8] {'ta'}, dimensions={0}, use_global_device_ids=true | all-gather | bytes 1105920 | tf_op jit(solution)/shard_map/all_gather | solution.py:74
  80.4 1.3 fusion.23
  81.8 0.7 multiply_convert_fusion
  82.5 3.7 collective-permute-start.14
  86.2 11.2 %all_gather.13 = bf16[4,2,4,16,256]{4,3,2,1,0:T(8,128)(2,1)S(1)} all-gather(bf16[1,2,4,16,256]{4,3,2,1,0:T(8,128)(2,1)S(1)} %copy.75), channel_id=1, replica_groups=mesh['ta'=4,'ha'=8,'wa'=8] {'ta'}, dimensions={0}, use_global_device_ids=true | all-gather | bytes 327680 | tf_op jit(solution)/shard_map/all_gather | solution.py:91
  97.4 7.0 collective-permute-start.16
  104.4 4.0 collective-permute-start.15
  108.4 0.1 constant_dynamic-slice_fusion.3
  108.5 0.9 collective-permute-done.15
  109.4 0.6 pad_maximum_fusion.12
  110.0 6.4 collective-permute-start.17
  116.4 2.5 fusion.3
  118.9 2.6 copy.78
  121.5 4.1 reshape.21
  125.6 1.0 pad_maximum_fusion.1
  126.5 17.1 %all-gather.1 = bf16[12,5,17,256]{3,2,1,0:T(8,128)(2,1)S(1)} all-gather(bf16[3,5,17,256]{3,2,1,0:T(8,128)(2,1)S(1)} %pad_maximum_fusion.1), channel_id=3, replica_groups=mesh['ta'=4,'ha'=8,'wa'=8] {'ta'}, dimensions={0}, use_global_device_ids=true | all-gather | bytes 652800 | tf_op jit(solution)/shard_map/all_gather | solution.py:75
  143.7 0.5 fusion.5
  144.2 2.7 copy.81
  146.9 4.0 reshape.22
  150.9 0.0 all-reduce.5.cloned.1.call-update
  150.9 0.0 copy-start.11
  150.9 1.3 collective-permute-start.9
  152.2 4.8 collective-permute-done.9
  157.0 0.8 pad_maximum_fusion.11
  157.8 3.6 collective-permute-start.11
  161.4 5.3 collective-permute-start.10
  166.8 0.1 collective-permute-done.11
  166.8 0.9 collective-permute-done.10
  167.8 1.4 pad_maximum_fusion.18
  169.2 1.3 collective-permute-start.13
  170.5 5.5 collective-permute-start.12
  176.0 0.6 dynamic-slice.1
  177.2 1.1 maximum_bitcast_fusion
  178.2 0.1 copy.97
  178.4 0.1 pad.2.clone
  178.6 1.3 fusion
  180.0 0.6 copy.82
  180.6 536.1 %all-reduce.5.cloned.1.call-done = (f32[6912,64]{0,1:T(8,128)}, f32[6912,64]{0,1:T(8,128)}) async-done(((f32[6912,64]{0,1:T(8,128)}, f32[6912,64]{0,1:T(8,128)}), (f32[6912,64]{0,1:T(8,128)}, f32[6912,64]{0,1:T(8,128)})) %all-reduce.5.cloned.1.call-update) | async-done | bytes 3538960
  716.7 1.6 constant_dynamic-slice_fusion
  (51 shorter events, 0.4 us)
Async XLA Ops:
  7.2 51.3 %copy-start = (bf16[6912,256]{1,0:T(8,128)(2,1)S(1)}, bf16[6912,256]{1,0:T(8,128)(2,1)}, u32[]{:S(2)}) copy-start(bf16[6912,256]{1,0:T(8,128)(2,1)} %param.5) | copy-start | bytes 10616836
  7.2 709.5 %all-reduce.5.cloned.1.call-start = ((), (), s32[]{:S(2)}) async-start(), calls=%async_computation | async-start | bytes 7077888
  7.2 35.2 %collective-permute-start.4 = (bf16[2,4,16,256]{3,2,1,0:T(8,128)(2,1)}, bf16[2,4,16,256]{3,2,1,0:T(8,128)(2,1)}, u32[]{:S(2)}, u32[]{:S(2)}) collective-permute-start(bf16[2,4,16,256]{3,2,1,0:T(8,128)(2,1)} %param.4), channel_id=1, source_target_pairs={{0,64},{64,128},{128,192},{1,65},{65,129},{129,193},{2,66},{66,130... | collective-permute-start | bytes 196616 | tf_op jit(solution)/shard_map/ppermute | solution.py:10
  13.8 18.8 %collective-permute-start = (bf16[1,2,8,256]{3,2,1,0:T(8,128)(2,1)}, bf16[1,2,8,256]{3,2,1,0:T(8,128)(2,1)}, u32[]{:S(2)}, u32[]{:S(2)}) collective-permute-start(bf16[1,2,8,256]{3,2,1,0:T(8,128)(2,1)} %param.7), channel_id=1, source_target_pairs={{64,0},{128,64},{192,128},{65,1},{129,65},{193,129},{66,2},{130,66... | collective-permute-start | bytes 24584 | tf_op jit(solution)/shard_map/ppermute | solution.py:10
  31.1 27.3 %copy-start.10 = (pred[8,3]{0,1:T(4,128)(4,1)S(1)}, pred[8,3]{0,1:T(4,128)(4,1)}, u32[]{:S(2)}) copy-start(pred[8,3]{0,1:T(4,128)(4,1)} %constant.26) | copy-start | bytes 76
  33.3 16.4 %collective-permute-start.2 = (bf16[2,1,8,256]{3,2,1,0:T(8,128)(2,1)S(1)}, bf16[2,1,8,256]{3,2,1,0:T(8,128)(2,1)S(1)}, u32[]{:S(2)}, u32[]{:S(2)}) collective-permute-start(bf16[2,1,8,256]{3,2,1,0:T(8,128)(2,1)S(1)} %get-tuple-element.31), channel_id=1, source_target_pairs={{8,0},{16,8},{24,16},{32,24},{40,32},{48,40},{56,48},{9,1},{17,9},... | collective-permute-start | bytes 24584 | tf_op jit(solution)/shard_map/ppermute | solution.py:21
  39.4 10.3 %collective-permute-start.1 = (bf16[2,1,8,256]{3,2,1,0:T(8,128)(2,1)S(1)}, bf16[2,1,8,256]{3,2,1,0:T(8,128)(2,1)S(1)}, u32[]{:S(2)}, u32[]{:S(2)}) collective-permute-start(bf16[2,1,8,256]{3,2,1,0:T(8,128)(2,1)S(1)} %get-tuple-element.30), channel_id=1, source_target_pairs={{0,8},{8,16},{16,24},{24,32},{32,40},{40,48},{48,56},{1,9},{9,17},... | collective-permute-start | bytes 24584 | tf_op jit(solution)/shard_map/ppermute | solution.py:18
  44.1 6.9 collective-permute-start.6
  46.0 5.0 collective-permute-start.5
  49.7 7.3 %collective-permute-start.3 = (bf16[2,4,1,256]{3,2,1,0:T(2,128)(2,1)S(1)}, bf16[2,4,1,256]{3,2,1,0:T(2,128)(2,1)S(1)}, u32[]{:S(2)}, u32[]{:S(2)}) collective-permute-start(bf16[2,4,1,256]{3,2,1,0:T(2,128)(2,1)S(1)} %pad_maximum_fusion.22), channel_id=1, source_target_pairs={{1,0},{2,1},{3,2},{4,3},{5,4},{6,5},{7,6},{9,8},{10,9},{11,10},{12... | collective-permute-start | bytes 12296 | tf_op jit(solution)/shard_map/ppermute | solution.py:21
  51.1 6.0 collective-permute-start.8
  52.4 5.6 collective-permute-start.7
  58.5 22.0 %copy-start.8 = (bf16[6912,256]{1,0:T(8,128)(2,1)S(1)}, bf16[6912,256]{1,0:T(8,128)(2,1)}, u32[]{:S(2)}) copy-start(bf16[6912,256]{1,0:T(8,128)(2,1)} %param.6) | copy-start | bytes 10616836
  82.5 33.9 %copy-start.1 = (bf16[2,4,16,256]{3,2,1,0:T(8,128)(2,1)}, bf16[2,4,16,256]{3,2,1,0:T(8,128)(2,1)S(1)}, u32[]{:S(2)}) copy-start(bf16[2,4,16,256]{3,2,1,0:T(8,128)(2,1)S(1)} %get-tuple-element.24) | copy-start | bytes 196612
  82.5 14.9 %collective-permute-start.14 = (bf16[2,4,16,256]{3,2,1,0:T(8,128)(2,1)S(1)}, bf16[2,4,16,256]{3,2,1,0:T(8,128)(2,1)S(1)}, u32[]{:S(2)}, u32[]{:S(2)}) collective-permute-start(bf16[2,4,16,256]{3,2,1,0:T(8,128)(2,1)S(1)} %get-tuple-element.24), channel_id=1, source_target_pairs={{0,64},{64,128},{128,192},{1,65},{65,129},{129,193},{2,66},{66,130... | collective-permute-start | bytes 196616 | tf_op jit(solution)/shard_map/ppermute | solution.py:10
  97.4 19.0 %copy-start.2 = (bf16[2,4,16,256]{3,2,1,0:T(8,128)(2,1)}, bf16[2,4,16,256]{3,2,1,0:T(8,128)(2,1)S(1)}, u32[]{:S(2)}) copy-start(bf16[2,4,16,256]{3,2,1,0:T(8,128)(2,1)S(1)} %collective-permute-done.14) | copy-start | bytes 196612
  97.4 11.1 %collective-permute-start.16 = (bf16[4,1,16,256]{3,2,1,0:T(8,128)(2,1)S(1)}, bf16[4,1,16,256]{3,2,1,0:T(8,128)(2,1)S(1)}, u32[]{:S(2)}, u32[]{:S(2)}) collective-permute-start(bf16[4,1,16,256]{3,2,1,0:T(8,128)(2,1)S(1)} %get-tuple-element.23), channel_id=1, source_target_pairs={{8,0},{16,8},{24,16},{32,24},{40,32},{48,40},{56,48},{9,1},{17,9},... | collective-permute-start | bytes 98312 | tf_op jit(solution)/shard_map/ppermute | solution.py:21
  104.4 5.0 collective-permute-start.15
  108.5 7.9 %copy-start.6 = (bf16[4,1,16,256]{3,2,1,0:T(8,128)(2,1)}, bf16[4,1,16,256]{3,2,1,0:T(8,128)(2,1)S(1)}, u32[]{:S(2)}) copy-start(bf16[4,1,16,256]{3,2,1,0:T(8,128)(2,1)S(1)} %collective-permute-done.16) | copy-start | bytes 98308
  109.4 7.0 copy-start.7
  110.0 15.6 %collective-permute-start.17 = (bf16[4,6,1,256]{3,2,1,0:T(2,128)(2,1)}, bf16[4,6,1,256]{3,2,1,0:T(2,128)(2,1)}, u32[]{:S(2)}, u32[]{:S(2)}) collective-permute-start(bf16[4,6,1,256]{3,2,1,0:T(2,128)(2,1)} %pad_maximum_fusion.12), channel_id=1, source_target_pairs={{0,1},{1,2},{2,3},{3,4},{4,5},{5,6},{6,7},{8,9},{9,10},{10,11},{11... | collective-permute-start | bytes 36872 | tf_op jit(solution)/shard_map/ppermute | solution.py:18
  150.9 25.2 %copy-start.9 = (u32[256]{0:T(256)S(1)}, u32[256]{0:T(256)}, u32[]{:S(2)}) copy-start(u32[256]{0:T(256)} %constant.30) | copy-start | bytes 3076
  150.9 27.7 %copy-start.11 = (pred[8,3]{0,1:T(4,128)(4,1)S(1)}, pred[8,3]{0,1:T(4,128)(4,1)}, u32[]{:S(2)}) copy-start(pred[8,3]{0,1:T(4,128)(4,1)} %constant.26) | copy-start | bytes 76
  150.9 6.1 collective-permute-start.9
  157.0 10.8 %copy-start.3 = (bf16[2,4,16,256]{3,2,1,0:T(8,128)(2,1)}, bf16[2,4,16,256]{3,2,1,0:T(8,128)(2,1)S(1)}, u32[]{:S(2)}) copy-start(bf16[2,4,16,256]{3,2,1,0:T(8,128)(2,1)S(1)} %collective-permute-done.9) | copy-start | bytes 196612
  157.8 9.0 %collective-permute-start.11 = (bf16[4,1,16,256]{3,2,1,0:T(8,128)(2,1)S(1)}, bf16[4,1,16,256]{3,2,1,0:T(8,128)(2,1)S(1)}, u32[]{:S(2)}, u32[]{:S(2)}) collective-permute-start(bf16[4,1,16,256]{3,2,1,0:T(8,128)(2,1)S(1)} %get-tuple-element.27), channel_id=1, source_target_pairs={{8,0},{16,8},{24,16},{32,24},{40,32},{48,40},{56,48},{9,1},{17,9},... | collective-permute-start | bytes 98312 | tf_op jit(solution)/shard_map/ppermute | solution.py:21
  161.4 6.3 collective-permute-start.10
  166.8 2.4 copy-start.4
  167.8 1.5 copy-start.5
  169.2 7.9 %collective-permute-start.13 = (bf16[4,6,1,256]{3,2,1,0:T(2,128)(2,1)}, bf16[4,6,1,256]{3,2,1,0:T(2,128)(2,1)}, u32[]{:S(2)}, u32[]{:S(2)}) collective-permute-start(bf16[4,6,1,256]{3,2,1,0:T(2,128)(2,1)} %get-tuple-element.19), channel_id=1, source_target_pairs={{1,0},{2,1},{3,2},{4,3},{5,4},{6,5},{7,6},{9,8},{10,9},{11,10},{12... | collective-permute-start | bytes 36872 | tf_op jit(solution)/shard_map/ppermute | solution.py:21
  170.5 6.6 collective-permute-start.12
Sparse Core Ops, SparseCore 0:
  151.0 565.6 all-reduce.4
where the time goes:
time: 733 us; the launch traced here: 725 us
  waiting for transfers between devices  544 us (74%)
  starting transfers between devices  67.8 us (9%)
  blocking collectives  65.1 us (9%)
  local copies, waits for them, and re-layouts  21.2 us (3%)
  between operations  15.1 us (2%)
    unnamed x2, waiting for transfers between devices  536 us
    ppermute x7, starting transfers between devices, padded(): lax.ppermute(lax.slice_in_dim(block, block.shape[dim] - width, None, axis...  32.5 us
    ppermute x7, starting transfers between devices, padded(): lax.ppermute(lax.slice_in_dim(block, 0, width, axis=dim), axis, backward)  22.4 us
    all_gather x1, blocking collectives, local(): lax.all_gather(padded_clip[None], 'ta', axis=0, tiled=True)  20.7 us
    all_gather x1, blocking collectives, local(): lax.all_gather(act_window[None], 'ta', axis=0, tiled=True)  17.1 us
    all_gather x1, blocking collectives, local(): cot_all = lax.all_gather(out_cotangent[None], 'ta', axis=0, tiled=True)  16 us
  transfers between devices with their start and end apart: 19, of which 6 were waited for; matrix products, arithmetic and copies ran while one was open for 3% of the time, Pallas kernels for 0%

commit v1 on v0

v1 whole, which is shorter than its diff:
```python
import jax
import jax.numpy as jnp
from jax import lax
from jax.sharding import PartitionSpec as P


def from_next(x, axis):
    count = lax.axis_size(axis)
    got = lax.ppermute(x, axis, [((i + 1) % count, i) for i in range(count)])
    return jnp.where(lax.axis_index(axis) == count - 1, jnp.zeros_like(got), got)


def from_previous(x, axis):
    count = lax.axis_size(axis)
    got = lax.ppermute(x, axis, [(i, (i + 1) % count) for i in range(count)])
    return jnp.where(lax.axis_index(axis) == 0, jnp.zeros_like(got), got)


def convolve(inputs, kernel, specs, padding, lhs_step, rhs_step):
    return lax.conv_general_dilated(
        inputs,
        kernel,
        (1, 1, 1),
        padding,
        lhs_dilation=lhs_step,
        rhs_dilation=rhs_step,
        dimension_numbers=specs,
        preferred_element_type=jnp.float32,
    )


def extend(clip, cot, dim, axis):
    clip_edge = lax.slice_in_dim(clip, 0, 2, axis=dim)
    cot_edge = lax.slice_in_dim(cot, 0, 1, axis=dim)
    channels = clip.shape[-1]
    rows = clip_edge.size // channels
    packed = jnp.concatenate(
        [clip_edge.reshape(rows, channels), cot_edge.reshape(-1, channels)], axis=0
    )
    packed = from_next(packed, axis)
    return (
        jnp.concatenate([clip, packed[:rows].reshape(clip_edge.shape)], axis=dim),
        jnp.concatenate([cot, packed[rows:].reshape(cot_edge.shape)], axis=dim),
    )


def owned(axis, length):
    place, count = lax.axis_index(axis), lax.axis_size(axis)
    spot = jnp.arange(length)
    return ((spot > 0) | (place == 0)) & ((spot < length - 1) | (place < count - 1))


def local(clip, conv_weight, down_weight, out_cotangent):
    frames, rows, columns, channels = clip.shape
    ta, ha, wa = lax.axis_size("ta"), lax.axis_size("ha"), lax.axis_size("wa")
    share = channels // ta
    first_kernel = conv_weight.reshape(3, 3, 3, channels, channels)
    down_kernel = down_weight.reshape(3, 3, 3, channels, channels)
    unit = (1, 1, 1)
    forward_specs = ("NDHWC", "DHWIO", "NDHWC")
    back_specs = ("NDHWC", "DHWOI", "NDHWC")
    weight_specs = ("CDHWN", "IDHWO", "DHWNC")
    here = frames * rows * columns
    packed = jnp.concatenate(
        [clip.reshape(here, channels), out_cotangent.reshape(-1, channels)], axis=0
    )
    packed = lax.all_gather(packed, "ta", axis=0, tiled=False)
    clips = packed[:, :here].reshape(ta * frames, rows, columns, channels)
    cots = packed[:, here:].reshape((-1,) + out_cotangent.shape[1:])
    clips, cots = extend(clips, cots, 1, "ha")
    clips, cots = extend(clips, cots, 2, "wa")
    pre_act = convolve(
        clips[None], first_kernel, forward_specs, [(2, 0), (1, 0), (1, 0)], unit, unit
    )[0]
    own = (owned("ha", rows + 1)[:, None] & owned("wa", columns + 1)[None, :])[None, :, :, None]
    activation = jnp.where(own, jax.nn.silu(pre_act), 0.0).astype(jnp.bfloat16)
    flipped_down = down_kernel[::-1, ::-1, ::-1]
    grad_act = convolve(
        cots[None], flipped_down, back_specs, [(0, 3), (1, 1), (1, 1)], (2, 2, 2), unit
    )[0]
    sigma = jax.nn.sigmoid(pre_act)
    grad_pre = grad_act * sigma * (1.0 + pre_act * (1.0 - sigma))
    grad_pre = jnp.where(own, grad_pre, 0.0).astype(jnp.bfloat16)
    place = lax.axis_index("ta")
    later = jnp.pad(grad_pre, ((0, 2), (0, 0), (0, 0), (0, 0)))
    later = lax.dynamic_slice_in_dim(later, place * frames, frames + 2, 0)
    flipped_first = first_kernel[::-1, ::-1, ::-1]
    grad_clip = convolve(
        later[None], flipped_first, back_specs, [(0, 0), (1, 2), (1, 2)], unit, unit
    )[0]
    start = place * share
    cot_share = lax.dynamic_slice_in_dim(cots, start, share, 3)
    grad_share = lax.dynamic_slice_in_dim(grad_pre, start, share, 3)
    grad_down = convolve(
        activation[None, :-1], cot_share[None], weight_specs, [(2, 0), (1, 1), (1, 1)], unit, (2, 2, 2)
    )
    grad_conv = convolve(
        clips[None], grad_share[None], weight_specs, [(2, 0), (1, 0), (1, 0)], unit, unit
    )
    both = jnp.concatenate(
        [grad_conv.reshape(27 * channels, share), grad_down.reshape(27 * channels, share)], axis=1
    )
    part = 27 * channels // (ha * wa)
    both = both.reshape(ha // 2, 2, wa, part, 2 * share)
    core = lax.axis_index("ha") % 2
    mine = lax.dynamic_index_in_dim(both, core, 1, keepdims=False)
    other = lax.dynamic_index_in_dim(both, 1 - core, 1, keepdims=False).astype(jnp.bfloat16)
    other = lax.ppermute(other, "ha", [(i, i ^ 1) for i in range(ha)])
    pair = (mine + other.astype(jnp.float32)).astype(jnp.bfloat16)
    groups = [[h * wa + w for h in range(c, ha, 2) for w in range(wa)] for c in range(2)]
    pair = pair.reshape(ha * wa // 2 * part, 2 * share)
    spread = lax.all_to_all(pair, ("ha", "wa"), 0, 0, axis_index_groups=groups, tiled=True)
    total = jnp.sum(spread.reshape(ha * wa // 2, part, 2 * share).astype(jnp.float32), axis=0)
    past = from_previous(grad_clip[:, :, columns:], "wa")
    grad_clip = grad_clip[:, :, :columns]
    grad_clip = grad_clip.at[:, :, :2].add(past)
    past = from_previous(grad_clip[:, rows:], "ha")
    grad_clip = grad_clip[:, :rows].at[:, :2].add(past)
    return (grad_clip.astype(jnp.bfloat16), total[:, :share], total[:, share:])


def solution(mesh):
    return jax.shard_map(
        local,
        mesh=mesh,
        in_specs=(P("ta", "ha", "wa", None), P(), P(), P("ta", "ha", "wa", None)),
        out_specs=(P("ta", "ha", "wa", None), P(("ha", "wa"), "ta"), P(("ha", "wa"), "ta")),
        check_vma=False,
    )
```

time: 733 us -> 147 us (0.20)
  waiting for transfers between devices: 544 us -> 14.4 us
  starting transfers between devices: 67.8 us -> 17.8 us
  blocking collectives: 65.1 us -> 16.6 us
  local copies, waits for them, and re-layouts: 21.2 us -> 55.6 us
  matrix products: 6.55 us -> 22.6 us
  between operations: 15.1 us -> 0.92 us
  other arithmetic: 5.8 us -> 17.7 us
    unnamed x2 -> x0, waiting for transfers between devices: 536 us -> none
    ppermute x18 -> x5, starting transfers between devices: 67.8 us -> 10.2 us  [the longest x2 6.68 us: from_next(): got = lax.ppermute(x, axis, [((i + 1) % count, i) for i in range(count)])]
    all_gather x4 -> x1, blocking collectives: 65.1 us -> 16.6 us  [local(): packed = lax.all_gather(packed, 'ta', axis=0, tiled=False)]
    conv_general_dilated x5, matrix products: 6.55 us -> 22.6 us  [convolve(): lax.conv_general_dilated(inputs, kernel, (1, 1, 1), padding, lhs_dilation...]
    concatenate x2 -> x4, local copies, waits for them, and re-layouts: 1.54 us -> 16.5 us  [the longest x3 15.9 us: local(): jnp.concatenate([grad_conv.reshape(27 * channels, share), grad_down.resha...]
    all_to_all x0 -> x1, starting transfers between devices: none -> 7.54 us  [local(): lax.all_to_all(pair, ('ha', 'wa'), 0, 0, axis_index_groups=groups, tiled=...]
  transfers between devices with their start and end apart: 19 -> 6, of which waited for: 6 -> 4; matrix products, arithmetic and copies ran while one was open for 3% -> 9% of each run, Pallas kernels for 0% -> 0%
where the time goes in v1:
time: 147 us; the launch traced here: 145 us
  local copies, waits for them, and re-layouts  55.6 us (38%)
  matrix products  22.6 us (15%)
  starting transfers between devices  17.8 us (12%)
  other arithmetic  17.7 us (12%)
  blocking collectives  16.6 us (11%)
  waiting for transfers between devices  14.4 us (10%)
    conv_general_dilated x5, matrix products, convolve(): lax.conv_general_dilated(inputs, kernel, (1, 1, 1), padding, lhs_dilation...  22.6 us
    all_gather x1, blocking collectives, local(): packed = lax.all_gather(packed, 'ta', axis=0, tiled=False)  16.6 us
    concatenate x3, local copies, waits for them, and re-layouts, local(): jnp.concatenate([grad_conv.reshape(27 * channels, share), grad_down.resha...  15.9 us
    ppermute x2, waiting for transfers between devices, from_previous(): got = lax.ppermute(x, axis, [(i, (i + 1) % count) for i in range(count)])  11.6 us
    unnamed x30, local copies, waits for them, and re-layouts  9.42 us
    all_to_all x1, starting transfers between devices, local(): lax.all_to_all(pair, ('ha', 'wa'), 0, 0, axis_index_groups=groups, tiled=...  7.54 us
    conv_general_dilated x8, local copies, waits for them, and re-layouts, convolve(): lax.conv_general_dilated(inputs, kernel, (1, 1, 1), padding, lhs_dilation...  7.11 us
    ppermute x2, starting transfers between devices, from_next(): got = lax.ppermute(x, axis, [((i + 1) % count, i) for i in range(count)])  6.68 us
  transfers between devices with their start and end apart: 6, of which 4 were waited for; matrix products, arithmetic and copies ran while one was open for 9% of the time, Pallas kernels for 0%

profile of v1, /device:TPU:1, one launch (start us, length us, event | category | flops | bytes accessed | tf_op | source)
XLA Modules:
  0.0 145.5 jit_solution(14011240594937561268)
XLA Ops:
  0.6 1.0 pad_maximum_fusion.2
  1.7 16.6 %all-gather = bf16[576,256]{1,0:T(8,128)(2,1)S(1)} all-gather(bf16[144,256]{1,0:T(8,128)(2,1)S(1)} %pad_maximum_fusion.2), channel_id=2, replica_groups=mesh['ta'=4,'ha'=8,'wa'=8] {'ta'}, dimensions={0}, use_global_device_ids=true | all-gather | bytes 368640 | tf_op jit(solution)/shard_map/all_gather | solution.py:67
  18.3 0.7 copy-done.2
  19.0 0.7 pad_maximum_fusion.1
  19.7 3.3 %collective-permute-start = (bf16[288,256]{1,0:T(8,128)(2,1)}, bf16[288,256]{1,0:T(8,128)(2,1)}, u32[]{:S(2)}, u32[]{:S(2)}) collective-permute-start(bf16[288,256]{1,0:T(8,128)(2,1)} %pad_maximum_fusion.1), channel_id=1, source_target_pairs={{8,0},{16,8},{24,16},{32,24},{40,32},{48,40},{56,48},{0,56},{9,1},... | collective-permute-start | bytes 442376 | tf_op jit(solution)/shard_map/ppermute | solution.py:9
  23.0 0.6 copy_dynamic-update-slice_fusion
  23.6 0.5 or_and_fusion
  24.1 0.5 or_and_fusion.1
  24.7 2.6 %collective-permute-done = bf16[288,256]{1,0:T(8,128)(2,1)} collective-permute-done((bf16[288,256]{1,0:T(8,128)(2,1)}, bf16[288,256]{1,0:T(8,128)(2,1)}, u32[]{:S(2)}, u32[]{:S(2)}) %collective-permute-start) | collective-permute-done | bytes 147488 | tf_op jit(solution)/shard_map/ppermute | solution.py:9
  27.2 0.9 broadcast_select_fusion
  28.2 0.7 slice.139
  28.8 0.6 copy_dynamic-update-slice_fusion.1
  29.4 0.7 slice.140
  30.1 1.6 %pad_maximum_fusion.5 = bf16[8,6,2,256]{3,2,1,0:T(2,128)(2,1)} fusion(bf16[8,2,16,256]{3,2,1,0:T(8,128)(2,1)} %bitcast.84, bf16[8,4,16,256]{3,2,1,0:T(8,128)(2,1)} %bitcast.81), kind=kLoop, calls=%fused_computation.59 | loop fusion | flops 98304 | bytes 442368 | tf_op jit(solution)/shard_map/concatenate | solution.py:42
  31.7 1.4 reshape.190
  33.2 1.4 pad_maximum_fusion.4
  34.6 3.4 %collective-permute-start.1 = (bf16[108,256]{1,0:T(8,128)(2,1)}, bf16[108,256]{1,0:T(8,128)(2,1)}, u32[]{:S(2)}, u32[]{:S(2)}) collective-permute-start(bf16[108,256]{1,0:T(8,128)(2,1)} %pad_maximum_fusion.4), channel_id=1, source_target_pairs={{1,0},{2,1},{3,2},{4,3},{5,4},{6,5},{7,6},{0,7},{9,8},{10,9},{11,1... | collective-permute-start | bytes 165896 | tf_op jit(solution)/shard_map/ppermute | solution.py:9
  38.0 1.3 broadcast_and_fusion
  39.3 0.3 collective-permute-done.1
  39.5 0.8 broadcast_select_fusion.1
  40.4 0.6 slice.142
  41.0 1.4 reshape.194
  42.4 2.0 %fusion.29 = (bf16[1,8,6,18,256]{4,3,2,1,0:T(8,128)(2,1)}, bf16[8,6,1,18,256]{4,3,1,0,2:T(8,128)(2,1)S(1)}) fusion(bf16[8,6,2,256]{3,2,1,0:T(2,128)(2,1)} %reshape.194, bf16[8,2,16,256]{3,2,1,0:T(8,128)(2,1)} %bitcast.85, bf16[8,4,16,256]{3,2,1,0:T(8,128)(2,1)} %bitcast.82), kind=kLoop, calls=%fused_computation.41 | loop fusion | flops 1327104 | bytes 1327104 | tf_op jit(solution)/shard_map/broadcast_in_dim | solution.py:73
  44.4 0.1 copy.131
  44.6 0.1 copy.109
  44.7 0.1 slice.143
  44.8 0.2 copy-done.11
  45.1 3.6 %convolution_select_fusion = f32[8,5,8,3,256]{4,2,3,1,0:T(8,128)S(1)} fusion(bf16[3,3,3,256,256]{4,3,2,1,0:T(8,128)(2,1)S(1)} %bitcast.76, bf16[8,6,1,7,2,256]{5,3,4,1,0,2:T(8,128)(2,1)S(1)} %slice.143, bf16[8,6,1,8,3,256]{5,3,4,1,0,2:T(8,128)(2,1)S(1)} %copy.109, pred[8,3]{0,1:T(4,128)(4,1)S(1)} %copy-done.11), kind=kOutput, calls=%fused_computation.6 | convolution fusion | flops 2777726976 | bytes 5455896 | tf_op jit(solution)/shard_map/conv_general_dilated | solution.py:20
  48.7 1.3 copy.110
  50.0 0.8 fusion.35
  50.8 2.0 %slice_bitcast_fusion = f32[8,5,17,256]{3,0,2,1:T(8,128)} fusion(f32[8,5,1,24,256]{4,0,3,1,2:T(8,128)} %bitcast.78), kind=kLoop, calls=%fused_computation.22 | loop fusion | bytes 1392640 | tf_op jit(solution)/shard_map/squeeze | solution.py:72
  52.8 1.4 fusion.38
  54.3 5.7 %fusion.32 = f32[1,8,5,17,256]{4,0,3,2,1:T(1,128)S(1)} fusion(bf16[3,3,3,256,256]{4,3,2,1,0:T(8,128)(2,1)} %bitcast.93, bf16[1,4,3,9,256]{4,1,3,2,0:T(4,128)(2,1)S(1)} %fusion.35), kind=kOutput, calls=%fused_computation.48 | convolution fusion | flops 229376000 | bytes 4290560 | tf_op jit(solution)/shard_map/conv_general_dilated | solution.py:20
  60.0 1.1 add_divide_fusion
  61.1 0.8 copy-done.5
  61.9 0.1 dynamic-slice_bitcast_fusion
  62.0 9.4 %fusion.9 = f32[3,3,3,256,64]{3,4,2,1,0:T(8,128)S(1)} fusion(bf16[1,8,6,18,256]{4,3,2,1,0:T(8,128)(2,1)S(1)} %copy-done.6, bf16[1,8,5,17,64]{4,1,3,2,0:T(8,128)(2,1)S(1)} %dynamic-slice_bitcast_fusion), kind=kOutput, calls=%fused_computation.15 | convolution fusion | flops 481689600 | bytes 2298880 | tf_op jit(solution)/shard_map/conv_general_dilated | solution.py:20
  71.4 2.7 %copy.117 = f32[3,3,3,256,64]{3,2,1,0,4:T(4,128)} copy(f32[3,3,3,256,64]{3,4,2,1,0:T(8,128)S(1)} %fusion.9) | data formatting | bytes 3538944 | tf_op jit(solution)/shard_map/conv_general_dilated | solution.py:20
  74.1 6.4 %concatenate.40 = f32[4,2,8,108,64]{3,2,1,0,4:T(8,128)} reshape(f32[3,3,3,256,64]{3,2,1,0,4:T(4,128)} %copy.117) | data formatting | bytes 3538944 | tf_op jit(solution)/shard_map/concatenate | solution.py:100
  80.5 3.3 %constant_dynamic-update-slice_fusion.1 = f32[4,2,8,108,128]{3,2,1,0,4:T(8,128)} fusion(f32[4,2,8,108,64]{3,2,1,0,4:T(8,128)} %concatenate.40), kind=kLoop, calls=%fused_computation.71 | loop fusion | bytes 3866624
  83.8 0.2 fusion.26
  84.0 2.6 %fusion.17 = f32[3,3,3,256,64]{3,4,2,1,0:T(8,128)S(1)} fusion(bf16[1,7,5,17,256]{4,1,3,2,0:T(8,128)(2,1)S(1)} %fusion.26, bf16[1,4,3,9,64]{4,1,3,2,0:T(4,128)(2,1)S(1)} %copy-done.8), kind=kOutput, calls=%fused_computation.29 | convolution fusion | flops 57344000 | bytes 2087936 | tf_op jit(solution)/shard_map/conv_general_dilated | solution.py:20
  86.6 2.7 %copy.120 = f32[3,3,3,256,64]{3,2,1,0,4:T(4,128)} copy(f32[3,3,3,256,64]{3,4,2,1,0:T(8,128)S(1)} %fusion.17) | data formatting | bytes 3538944 | tf_op jit(solution)/shard_map/conv_general_dilated | solution.py:20
  89.3 6.4 %concatenate.41 = f32[4,2,8,108,64]{3,2,1,0,4:T(8,128)} reshape(f32[3,3,3,256,64]{3,2,1,0,4:T(4,128)} %copy.120) | data formatting | bytes 3538944 | tf_op jit(solution)/shard_map/concatenate | solution.py:100
  95.7 3.1 %constant_dynamic-update-slice_fusion = f32[4,2,8,108,128]{3,2,1,0,4:T(8,128)} fusion(f32[4,2,8,108,128]{3,2,1,0,4:T(8,128)} %constant_dynamic-update-slice_fusion.1, f32[4,2,8,108,64]{3,2,1,0,4:T(8,128)} %concatenate.41), kind=kLoop, calls=%fused_computation.70 | loop fusion | bytes 4194304 | tf_op jit(solution)/shard_map/concatenate | solution.py:100
  98.8 2.8 %fusion.2 = bf16[4,8,108,128]{2,1,0,3:T(8,128)(2,1)} fusion(f32[4,2,8,108,128]{3,2,1,0,4:T(8,128)} %constant_dynamic-update-slice_fusion, s32[]{:T(128)S(6)} %select_n.74), kind=kLoop, calls=%fused_computation.8 | loop fusion | bytes 1769476 | tf_op jit(solution)/shard_map/convert_element_type | solution.py:107
  101.6 3.0 %copy.122 = bf16[4,8,108,128]{3,1,2,0:T(8,128)(2,1)} copy(bf16[4,8,108,128]{2,1,0,3:T(8,128)(2,1)} %fusion.2) | data formatting | bytes 1769472 | tf_op jit(solution)/shard_map/convert_element_type | solution.py:107
  104.6 3.1 %constant_dynamic-slice_fusion = f32[4,1,8,108,128]{3,2,1,0,4:T(8,128)} fusion(f32[4,2,8,108,128]{3,2,1,0,4:T(8,128)} %constant_dynamic-update-slice_fusion, s32[]{:T(128)S(6)} %select_n.73), kind=kLoop, calls=%fused_computation.72 | loop fusion | bytes 3538948 | tf_op jit(solution)/shard_map/jit(dynamic_index_in_dim)/dynamic_slice | solution.py:106
  107.7 3.2 %copy.121 = f32[4,1,8,108,128]{4,2,3,1,0:T(8,128)} copy(f32[4,1,8,108,128]{3,2,1,0,4:T(8,128)} %constant_dynamic-slice_fusion) | data formatting | bytes 3538944 | tf_op jit(solution)/shard_map/jit(dynamic_index_in_dim)/dynamic_slice | solution.py:106
  110.9 1.9 %copy_bitcast_fusion = bf16[32,108,128]{2,0,1:T(8,128)(2,1)S(1)} fusion(f32[4,1,8,108,128]{4,2,3,1,0:T(8,128)} %copy.121, bf16[4,8,108,128]{3,1,2,0:T(8,128)(2,1)} %collective-permute-done.4), kind=kLoop, calls=%fused_computation.14 | loop fusion | flops 1327104 | bytes 3538944 | tf_op jit(solution)/shard_map/all_to_all | solution.py:112
  112.8 1.3 copy.124
  114.1 7.5 %all-to-all-start = ((bf16[32,108,128]{2,1,0:T(8,128)(2,1)}), bf16[32,108,128]{2,1,0:T(8,128)(2,1)}, u32[]{:S(2)}, u32[]{:S(2)}) async-start(bf16[32,108,128]{2,1,0:T(8,128)(2,1)} %copy.124), calls=%async_computation | async-start | bytes 1835008 | tf_op jit(solution)/shard_map/all_to_all | solution.py:112
  121.7 1.1 fusion.31
  123.0 1.2 convolution_select_fusion.1
  124.2 0.2 copy.113
  124.5 1.2 collective-permute-start.2
  125.8 10.3 %collective-permute-done.2 = f32[2,6,2,256]{3,0,2,1:T(2,128)S(1)} collective-permute-done((f32[2,6,2,256]{3,0,2,1:T(2,128)S(1)}, f32[2,6,2,256]{3,0,2,1:T(2,128)S(1)}, u32[]{:S(2)}, u32[]{:S(2)}) %collective-permute-start.2) | collective-permute-done | bytes 24608 | tf_op jit(solution)/shard_map/ppermute | solution.py:15
  136.1 2.3 %collective-permute-start.3 = (f32[2,2,16,256]{3,0,2,1:T(2,128)S(1)}, f32[2,2,16,256]{3,0,2,1:T(2,128)S(1)}, u32[]{:S(2)}, u32[]{:S(2)}) collective-permute-start(f32[2,2,16,256]{3,0,2,1:T(2,128)S(1)} %slice.152), channel_id=1, source_target_pairs={{0,8},{8,16},{16,24},{24,32},{32,40},{40,48},{48,56},{56,0},{1,9},... | collective-permute-start | bytes 196616 | tf_op jit(solution)/shard_map/ppermute | solution.py:15
  138.4 1.3 collective-permute-done.3
  139.8 0.6 copy.125
  140.4 1.3 convert_reduce_fusion
  141.7 0.7 fusion.46
  142.4 1.5 %copy.126 = f32[108,64]{0,1:T(8,128)} copy(f32[108,64]{1,0:T(8,128)} %get-tuple-element.47) | data formatting | bytes 55296
  143.9 1.5 %copy.127 = f32[108,64]{0,1:T(8,128)} copy(f32[108,64]{1,0:T(8,128)} %get-tuple-element.46) | data formatting | bytes 55296
  (46 shorter events, 0.5 us)
Async XLA Ops:
  0.6 44.2 %copy-start = (bf16[6912,256]{1,0:T(8,128)(2,1)S(1)}, bf16[6912,256]{1,0:T(8,128)(2,1)}, u32[]{:S(2)}) copy-start(bf16[6912,256]{1,0:T(8,128)(2,1)} %param.9) | copy-start | bytes 10616836
  18.3 0.7 copy-start.2
  19.7 7.5 %collective-permute-start = (bf16[288,256]{1,0:T(8,128)(2,1)}, bf16[288,256]{1,0:T(8,128)(2,1)}, u32[]{:S(2)}, u32[]{:S(2)}) collective-permute-start(bf16[288,256]{1,0:T(8,128)(2,1)} %pad_maximum_fusion.1), channel_id=1, source_target_pairs={{8,0},{16,8},{24,16},{32,24},{40,32},{48,40},{56,48},{0,56},{9,1},... | collective-permute-start | bytes 442376 | tf_op jit(solution)/shard_map/ppermute | solution.py:9
  34.6 4.9 %collective-permute-start.1 = (bf16[108,256]{1,0:T(8,128)(2,1)}, bf16[108,256]{1,0:T(8,128)(2,1)}, u32[]{:S(2)}, u32[]{:S(2)}) collective-permute-start(bf16[108,256]{1,0:T(8,128)(2,1)} %pad_maximum_fusion.4), channel_id=1, source_target_pairs={{1,0},{2,1},{3,2},{4,3},{5,4},{6,5},{7,6},{0,7},{9,8},{10,9},{11,1... | collective-permute-start | bytes 165896 | tf_op jit(solution)/shard_map/ppermute | solution.py:9
  40.4 0.6 copy-start.7
  44.4 0.7 copy-start.11
  45.1 4.9 %slice-start = ((bf16[108,256]{1,0:T(8,128)(2,1)}), bf16[12,256]{1,0:T(8,128)(2,1)S(1)}, s32[]{:S(2)}) async-start(bf16[108,256]{1,0:T(8,128)(2,1)} %copy-done.7), calls=%async_computation.1 | async-start | bytes 16384 | tf_op jit(solution)/shard_map/slice | solution.py:43
  54.3 5.7 %copy-start.1 = (f32[8,5,8,3,256]{4,0,3,2,1:T(8,128)S(1)}, f32[8,5,8,3,256]{4,0,3,2,1:T(8,128)}, u32[]{:S(2)}) copy-start(f32[8,5,8,3,256]{4,0,3,2,1:T(8,128)} %copy.110) | copy-start | bytes 2949124
  54.3 5.7 %copy-start.9 = (pred[5,17]{1,0:T(8,128)(4,1)S(1)}, pred[5,17]{1,0:T(8,128)(4,1)}, u32[]{:S(2)}) copy-start(pred[5,17]{1,0:T(8,128)(4,1)} %broadcast_and_fusion) | copy-start | bytes 259
  60.0 2.0 %copy-start.6 = (bf16[1,8,6,18,256]{4,3,2,1,0:T(8,128)(2,1)S(1)}, bf16[1,8,6,18,256]{4,3,2,1,0:T(8,128)(2,1)}, u32[]{:S(2)}) copy-start(bf16[1,8,6,18,256]{4,3,2,1,0:T(8,128)(2,1)} %get-tuple-element.44) | copy-start | bytes 1327108
  61.1 0.8 copy-start.5
  80.5 3.3 %copy-start.3 = (f32[8,5,17,256]{3,0,2,1:T(8,128)S(1)}, f32[8,5,17,256]{3,0,2,1:T(8,128)}, u32[]{:S(2)}) copy-start(f32[8,5,17,256]{3,0,2,1:T(8,128)} %get-tuple-element.42) | copy-start | bytes 2088964
  80.5 3.3 %copy-start.4 = (f32[8,5,17,256]{3,0,2,1:T(8,128)S(1)}, f32[8,5,17,256]{3,0,2,1:T(8,128)}, u32[]{:S(2)}) copy-start(f32[8,5,17,256]{3,0,2,1:T(8,128)} %slice_bitcast_fusion) | copy-start | bytes 2088964
  80.5 3.5 %copy-start.8 = (bf16[1,4,3,9,64]{4,1,3,2,0:T(4,128)(2,1)S(1)}, bf16[1,4,3,9,64]{4,1,3,2,0:T(4,128)(2,1)}, u32[]{:S(2)}) copy-start(bf16[1,4,3,9,64]{4,1,3,2,0:T(4,128)(2,1)} %fusion.38) | copy-start | bytes 41476
  104.6 6.3 %collective-permute-start.4 = (bf16[4,8,108,128]{3,1,2,0:T(8,128)(2,1)}, bf16[4,8,108,128]{3,1,2,0:T(8,128)(2,1)}, u32[]{:S(2)}, u32[]{:S(2)}) collective-permute-start(bf16[4,8,108,128]{3,1,2,0:T(8,128)(2,1)} %copy.122), channel_id=1, source_target_pairs={{0,8},{8,0},{16,24},{24,16},{32,40},{40,32},{48,56},{56,48},{1,9},... | collective-permute-start | bytes 2654216 | tf_op jit(solution)/shard_map/ppermute | solution.py:108
  114.1 8.8 %copy-start.10 = (pred[8,3]{0,1:T(4,128)(4,1)S(1)}, pred[8,3]{0,1:T(4,128)(4,1)}, u32[]{:S(2)}) copy-start(pred[8,3]{0,1:T(4,128)(4,1)} %constant.124) | copy-start | bytes 76
  114.1 26.3 %all-to-all-start = ((bf16[32,108,128]{2,1,0:T(8,128)(2,1)}), bf16[32,108,128]{2,1,0:T(8,128)(2,1)}, u32[]{:S(2)}, u32[]{:S(2)}) async-start(bf16[32,108,128]{2,1,0:T(8,128)(2,1)} %copy.124), calls=%async_computation | async-start | bytes 1835008 | tf_op jit(solution)/shard_map/all_to_all | solution.py:112
  124.5 11.5 %collective-permute-start.2 = (f32[2,6,2,256]{3,0,2,1:T(2,128)S(1)}, f32[2,6,2,256]{3,0,2,1:T(2,128)S(1)}, u32[]{:S(2)}, u32[]{:S(2)}) collective-permute-start(f32[2,6,2,256]{3,0,2,1:T(2,128)S(1)} %slice.149), channel_id=1, source_target_pairs={{0,1},{1,2},{2,3},{3,4},{4,5},{5,6},{6,7},{7,0},{8,9},{9,10},{10,1... | collective-permute-start | bytes 73736 | tf_op jit(solution)/shard_map/ppermute | solution.py:15
  136.1 3.6 %collective-permute-start.3 = (f32[2,2,16,256]{3,0,2,1:T(2,128)S(1)}, f32[2,2,16,256]{3,0,2,1:T(2,128)S(1)}, u32[]{:S(2)}, u32[]{:S(2)}) collective-permute-start(f32[2,2,16,256]{3,0,2,1:T(2,128)S(1)} %slice.152), channel_id=1, source_target_pairs={{0,8},{8,16},{16,24},{24,32},{32,40},{40,48},{48,56},{56,0},{1,9},... | collective-permute-start | bytes 196616 | tf_op jit(solution)/shard_map/ppermute | solution.py:15

commit v2 on v0

v2 whole, which is shorter than its diff:
```python
import jax
import jax.numpy as jnp
from jax import lax
from jax.experimental import pallas as pl
from jax.experimental.pallas import tpu as pltpu
from jax.sharding import PartitionSpec as P

F, R, W, C = 2, 4, 16, 256
TA, HA, WA = 4, 8, 8
T = TA * F
HEAD = 2 * F * W + (R // 2) * (W // 2)
BLOCK = F * R * W + (R // 2) * (W // 2)
SHARE = C // TA
PART = 27 * C // (HA * WA)
SLOT = 112
PEERS = HA * WA // 2
TAPS = [(a, b, c) for a in range(3) for b in range(3) for c in range(3)]
BF16, F32 = jnp.bfloat16, jnp.float32
VMEM_BYTES = 48 * 1024 * 1024


def iota(shape, dim):
    return lax.broadcasted_iota(jnp.int32, shape, dim)


def onehot(hit):
    return jnp.where(hit, 1.0, 0.0).astype(F32).astype(BF16)


def dot(x, y):
    return jnp.dot(x, y, preferred_element_type=F32)


def dot_t(x, y):
    return lax.dot_general(x, y, (((1,), (1,)), ((), ())), preferred_element_type=F32)


def column(order):
    return jnp.where(order < W // 2, 2 * order, 2 * (order - W // 2) + 1)


def frame_rows(g_ref, h_ref, t):
    s, f = t // F, t % F
    low = 2 * W * f
    return [
        g_ref[s, low : low + 2 * W],
        g_ref[s, HEAD + low : HEAD + low + 2 * W],
        h_ref[s, low : low + 2 * W],
    ]


def edge_kernel(g_ref, h_ref, out_ref):
    cot = 2 * F * W
    m, n = iota((16, 128), 0), iota((16, 128), 1)
    source = jnp.where(m < 12, (m // 2) * W + m % 2, jnp.where(m < 14, 96 + (m - 12) * 8, 112))
    pick = onehot((n == source) & (m < 15))
    for t in range(T):
        s = t // F
        rows = frame_rows(g_ref, h_ref, t) + [g_ref[s, cot : cot + 16], h_ref[s, cot : cot + 16]]
        out_ref[t] = dot(pick, jnp.concatenate(rows, axis=0)).astype(BF16)


def main_kernel(
    at_ref, g_ref, h_ref, w_ref, k1_ref, kd_ref, mine_ref, other_ref, later_ref,
    k1, kd, xb, cu, pre, act, gp, tt, sem1, semd,
):
    ta, last_h, last_w = at_ref[0], at_ref[1] == HA - 1, at_ref[2] == WA - 1
    core = lax.rem(at_ref[1], 2)
    cot = 2 * F * W
    step = 3 * C
    copies1 = [
        pltpu.make_async_copy(k1_ref.at[pl.ds(i * step, step)], k1.at[pl.ds(i * step, step)], sem1.at[i])
        for i in range(9)
    ]
    copiesd = [
        pltpu.make_async_copy(kd_ref.at[pl.ds(i * step, step)], kd.at[pl.ds(i * step, step)], semd.at[i])
        for i in range(9)
    ]
    for copy in copies1 + copiesd:
        copy.start()

    m, n = iota((576, 112), 0), iota((576, 112), 1)
    tap, place = m // 64, m % 64
    b, c, k, col = tap // 3, tap % 3, place // W, column(place % W)
    row, v = k + b, col + c
    source = jnp.where(v < W, row * W + v, 96 + row * 2 + v - W)
    out_h = last_h & (((b == 0) & (k == 3)) | ((b == 2) & (k == 2)))
    out_w = last_w & (((c == 0) & (col == 15)) | ((c == 2) & (col == 14)))
    pick = onehot((n == source) & jnp.logical_not(out_h | out_w))
    for i in range(9):
        xb[i, 0:2] = jnp.zeros((2, 64, C), BF16)
    for t in range(T):
        rows = jnp.concatenate(frame_rows(g_ref, h_ref, t) + [w_ref[t]], axis=0)
        built = dot(pick, rows).astype(BF16)
        for i in range(9):
            xb[i, t + 2] = built[i * 64 : (i + 1) * 64]

    m, n = iota((144, 48), 0), iota((144, 48), 1)
    tap, place = m // 16, m % 16
    b, c, kk, mm = tap // 3, tap % 3, place // 8, place % 8
    r, q = kk + jnp.where(b < 2, 1, 0), mm + jnp.where(c < 2, 1, 0)
    source = jnp.where(q == 8, 44 + r, r * 8 + q)
    out_h = last_h & (b == 0) & (kk == 1)
    out_w = last_w & (c == 0) & (mm == 7)
    pick = onehot((n == source) & jnp.logical_not(out_h | out_w))
    for i in range(9):
        cu[i, TA] = jnp.zeros((16, C), BF16)
    for j in range(TA):
        rows = jnp.concatenate(
            [g_ref[j, cot : cot + 16], h_ref[j, cot : cot + 16], w_ref[2 * j]], axis=0
        )
        built = dot(pick, rows).astype(BF16)
        for i in range(9):
            cu[i, j] = built[i * 16 : (i + 1) * 16]

    for i, (a, b, c) in enumerate(TAPS):
        if i % 3 == 0:
            copies1[i // 3].wait()
        x = xb[b * 3 + c, a : a + T].reshape(T * 64, C)
        y = dot(x, k1[i * C : (i + 1) * C])
        if i == 0:
            pre[...] = y
        else:
            pre[...] += y

    for copy in copiesd:
        copy.wait()
    for te in range(2):
        for ke in range(2):
            for ce in range(2):
                total = None
                for i, (a, b, c) in enumerate(TAPS):
                    if (a == 1, b == 1, c == 1) != (te == 1, ke == 1, ce == 1):
                        continue
                    ja = 1 if a < 2 else 0
                    y = dot_t(cu[b * 3 + c, ja : ja + 4].reshape(64, C), kd[i * C : (i + 1) * C])
                    total = y if total is None else total + y
                for j in range(4):
                    for kk in range(2):
                        t, k = 2 * j + te, 2 * kk + ke
                        spot = t * 64 + k * W + ce * 8
                        x = pre[spot : spot + 8]
                        s = 1.0 / (1.0 + jnp.exp(-x))
                        at = (j * 2 + kk) * 8
                        g = total[at : at + 8]
                        act[te * 4 + ke * 2 + ce, at : at + 8] = x * s
                        pre[spot : spot + 8] = g * s * (1.0 + x * (1.0 - s))
    gp[0:2] = jnp.zeros((2, 64, C), BF16)
    gp[2 : T + 2] = pre[...].astype(BF16).reshape(T, 64, C)
    gp[T + 2 : T + 4] = jnp.zeros((2, 64, C), BF16)
    later_ref[...] = gp[pl.ds(2 + F * ta, F + 2)]

    share = onehot(iota((SHARE, C), 1) == iota((SHARE, C), 0) + ta * SHARE)
    left = jnp.concatenate(
        [
            dot_t(share, gp[2 - a : 2 - a + T + 2].reshape((T + 2) * 64, C)).astype(BF16)
            for a in range(3)
        ],
        axis=0,
    )
    for bc in range(9):
        y = dot(left, xb[bc].reshape((T + 2) * 64, C)).astype(BF16)
        for a in range(3):
            tt[a * 9 + bc, 0:SHARE] = y[a * SHARE : (a + 1) * SHARE]
    for bc in range(9):
        for ja in range(2):
            cots = dot_t(share, cu[bc, ja : ja + 4].reshape(64, C)).astype(BF16)
            for a in (0, 1) if ja == 1 else (2,):
                kind = (4 if a == 1 else 0) + (2 if bc // 3 == 1 else 0) + (1 if bc % 3 == 1 else 0)
                tt[a * 9 + bc, SHARE:] = dot(cots, act[kind].astype(BF16)).astype(BF16)

    m, n = iota((SLOT, C), 0), iota((SLOT, C), 1)
    for x in range(HA // 2):
        for w in range(WA):
            pair = []
            for cc in range(2):
                first = ((x * 2 + cc) * WA + w) * PART
                tap, off = first // C, first % C
                y = dot_t(onehot((n == m + off) & (m < PART)), tt[tap])
                if off + PART > C:
                    y += dot_t(onehot((n == m + off - C) & (m < PART)), tt[tap + 1])
                pair.append(y)
            spot = (x * WA + w) * SLOT
            mine_ref[spot : spot + SLOT] = jnp.where(core == 0, pair[0], pair[1]).astype(BF16)
            other_ref[spot : spot + SLOT] = jnp.where(core == 0, pair[1], pair[0]).astype(BF16)


WIDE = 144


def clip_kernel(at_ref, later_ref, k1_ref, main_ref, spill_ref, k1, yb, acc, sem):
    last_h, last_w = at_ref[1] == HA - 1, at_ref[2] == WA - 1
    step = 3 * C
    copies = [
        pltpu.make_async_copy(k1_ref.at[pl.ds(i * step, step)], k1.at[pl.ds(i * step, step)], sem.at[i])
        for i in range(9)
    ]
    for copy in copies:
        copy.start()
    for i in range(9):
        b, c = i // 3, i % 3
        m, n = iota((WIDE, 64), 0), iota((WIDE, 64), 1)
        past = m >= 96
        h = jnp.where(past, (m - 96) // 8, m // W)
        v = jnp.where(past, W + (m - 96) % 8, m % W)
        k, col = n // W, column(n % W)
        hit = (h == k + b) & (v == col + c) & (v < W + 2)
        if b != 1:
            hit = hit & jnp.logical_not(last_h & (k == (3 if b == 0 else 2)))
        if c != 1:
            hit = hit & jnp.logical_not(last_w & (col == (15 if c == 0 else 14)))
        pick = onehot(hit)
        for t in range(F + 2):
            yb[i, t] = dot(pick, later_ref[t]).astype(BF16)
    for i, (a, b, c) in enumerate(TAPS):
        if i % 3 == 0:
            copies[i // 3].wait()
        y = dot_t(yb[b * 3 + c, 2 - a : 2 - a + F].reshape(F * WIDE, C), k1[i * C : (i + 1) * C])
        if i == 0:
            acc[...] = y
        else:
            acc[...] += y
    for f in range(F):
        main_ref[f] = acc[f * WIDE : f * WIDE + 96]
        spill_ref[f] = acc[f * WIDE + 96 : (f + 1) * WIDE]


def sum_kernel(parts_ref, conv_ref, down_ref):
    total = parts_ref[0].astype(F32)
    for i in range(1, PEERS):
        total += parts_ref[i].astype(F32)
    conv_ref[...] = total[:PART, :SHARE]
    down_ref[...] = total[:PART, SHARE:]


def whole():
    return pl.BlockSpec(memory_space=pltpu.VMEM)


def call(kernel, outs, specs, scratch, flops, name):
    return pl.pallas_call(
        kernel,
        out_shape=outs,
        in_specs=specs,
        out_specs=jax.tree.map(lambda _: whole(), outs),
        scratch_shapes=scratch,
        compiler_params=pltpu.CompilerParams(vmem_limit_bytes=VMEM_BYTES),
        cost_estimate=pl.CostEstimate(flops=flops, bytes_accessed=8_000_000, transcendentals=0),
        name=name,
    )


def shape(dims, dtype=BF16):
    return jax.ShapeDtypeStruct(dims, dtype)


def shift(x, axis, by):
    count = lax.axis_size(axis)
    return lax.ppermute(x, axis, [(i, (i + by) % count) for i in range(count)])


def local(clip, conv_weight, down_weight, out_cotangent):
    smem, anywhere = pl.BlockSpec(memory_space=pltpu.SMEM), pl.BlockSpec(memory_space=pl.ANY)
    at = jnp.stack([lax.axis_index(a) for a in ("ta", "ha", "wa")]).astype(jnp.int32)
    head = clip[:, :2].reshape(2 * F * W, C)
    tail = clip[:, 2:].reshape(2 * F * W, C)
    packed = jnp.concatenate([head, out_cotangent.reshape(-1, C), tail], axis=0)
    g = lax.all_gather(packed, "ta", axis=0, tiled=False)
    h = shift(g[:, :HEAD], "ha", -1)
    w = call(edge_kernel, shape((T, 16, C)), [whole()] * 2, [], 10**7, "edge")(g, h)
    w = shift(w, "wa", -1)
    mine, other, later = call(
        main_kernel,
        [shape((PEERS * SLOT, 2 * SHARE)), shape((PEERS * SLOT, 2 * SHARE)), shape((F + 2, 64, C))],
        [smem, whole(), whole(), whole(), anywhere, anywhere],
        [
            pltpu.VMEM((27 * C, C), BF16),
            pltpu.VMEM((27 * C, C), BF16),
            pltpu.VMEM((9, T + 2, 64, C), BF16),
            pltpu.VMEM((9, TA + 1, 16, C), BF16),
            pltpu.VMEM((T * 64, C), F32),
            pltpu.VMEM((8, 64, C), F32),
            pltpu.VMEM((T + 4, 64, C), BF16),
            pltpu.VMEM((27, 2 * SHARE, C), BF16),
            pltpu.SemaphoreType.DMA((9,)),
            pltpu.SemaphoreType.DMA((9,)),
        ],
        5 * 10**9,
        "main",
    )(at, g, h, w, conv_weight, down_weight)
    other = lax.ppermute(other, "ha", [(i, i ^ 1) for i in range(HA)])
    grad_clip, spill = call(
        clip_kernel,
        [shape((F, 96, C), F32), shape((F, 48, C), F32)],
        [smem, whole(), anywhere],
        [
            pltpu.VMEM((27 * C, C), BF16),
            pltpu.VMEM((9, F + 2, WIDE, C), BF16),
            pltpu.VMEM((F * WIDE, C), F32),
            pltpu.SemaphoreType.DMA((9,)),
        ],
        10**9,
        "clip",
    )(at, later, conv_weight)
    spill = shift(spill, "wa", 1)
    pair = (mine.astype(F32) + other.astype(F32)).astype(BF16)
    groups = [[i * WA + w for i in range(c, HA, 2) for w in range(WA)] for c in range(2)]
    parts = lax.all_to_all(pair, ("ha", "wa"), 0, 0, axis_index_groups=groups, tiled=True)
    grad_conv, grad_down = call(
        sum_kernel, [shape((PART, SHARE), F32), shape((PART, SHARE), F32)], [whole()], [], 10**6, "sum"
    )(parts.reshape(PEERS, SLOT, 2 * SHARE))
    grad_clip = grad_clip.reshape(F, 6, W, C)
    spill = spill.reshape(F, 6, 8, C)
    grad_clip = jnp.concatenate([grad_clip[:, :, :8] + spill, grad_clip[:, :, 8:]], axis=2)
    past = shift(grad_clip[:, R:], "ha", 1)
    grad_clip = jnp.concatenate([grad_clip[:, :2] + past, grad_clip[:, 2:R]], axis=1).astype(BF16)
    return (grad_clip, grad_conv, grad_down)


def solution(mesh):
    return jax.shard_map(
        local,
        mesh=mesh,
        in_specs=(P("ta", "ha", "wa", None), P(), P(), P("ta", "ha", "wa", None)),
        out_specs=(P("ta", "ha", "wa", None), P(("ha", "wa"), "ta"), P(("ha", "wa"), "ta")),
        check_vma=False,
    )
```

time: 733 us -> 81.4 us (0.11); the launches traced: 725 us -> 81 us
  waiting for transfers between devices: 544 us -> 15.5 us
  starting transfers between devices: 67.8 us -> 18.7 us
  blocking collectives: 65.1 us -> 16.5 us
  Pallas kernels: 0 us -> 20.8 us
  local copies, waits for them, and re-layouts: 21.2 us -> 6.2 us
  between operations: 15.1 us -> 0.7 us
    unnamed x2 -> x0, waiting for transfers between devices: 536 us -> none
    ppermute x18 -> x5, starting transfers between devices: 67.8 us -> 10.6 us  [the longest x4 10.6 us: shift(): return lax.ppermute(x, axis, [(i, (i + by) % count) for i in range(count)])]
    all_gather x4 -> x1, blocking collectives: 65.1 us -> 16.5 us  [local(): g = lax.all_gather(packed, 'ta', axis=0, tiled=False)]
    pallas_call x0 -> x4, Pallas kernels: none -> 20.8 us  [the longest x1 14.5 us: local(): call(main_kernel, [shape((PEERS * SLOT, 2 * SHARE)), shape((PEERS * SLOT,...]
    all_to_all x0 -> x1, starting transfers between devices: none -> 8.1 us  [local(): lax.all_to_all(pair, ('ha', 'wa'), 0, 0, axis_index_groups=groups, tiled=...]
    reshape x2 -> x0, local copies, waits for them, and re-layouts: 8.08 us -> none  [the longest x1 4.05 us: local(): grad_conv.reshape(27 * channels, share)]
    ppermute x18 -> x5, waiting for transfers between devices: 7.6 us -> 15.5 us  [the longest x4 13 us: shift(): return lax.ppermute(x, axis, [(i, (i + by) % count) for i in range(count)])]
  transfers between devices with their start and end apart: 19 -> 6, of which waited for: 6 -> 5; matrix products, arithmetic and copies ran while one was open for 3% -> 1% of each run, Pallas kernels for 0% -> 7%
where the time goes in v2:
time: 81.4 us; the launch traced here: 81 us
  Pallas kernels  20.8 us (26%)
  starting transfers between devices  18.7 us (23%)
  blocking collectives  16.5 us (20%)
  waiting for transfers between devices  15.5 us (19%)
  local copies, waits for them, and re-layouts  6.2 us (8%)
  other arithmetic  2.62 us (3%)
    all_gather x1, blocking collectives, local(): g = lax.all_gather(packed, 'ta', axis=0, tiled=False)  16.5 us
    pallas_call x1, Pallas kernels, local(): call(main_kernel, [shape((PEERS * SLOT, 2 * SHARE)), shape((PEERS * SLOT,...  14.5 us
    ppermute x4, waiting for transfers between devices, shift(): return lax.ppermute(x, axis, [(i, (i + by) % count) for i in range(count)])  13 us
    ppermute x4, starting transfers between devices, shift(): return lax.ppermute(x, axis, [(i, (i + by) % count) for i in range(count)])  10.6 us
    all_to_all x1, starting transfers between devices, local(): lax.all_to_all(pair, ('ha', 'wa'), 0, 0, axis_index_groups=groups, tiled=...  8.1 us
    pallas_call x1, Pallas kernels, local(): call(clip_kernel, [shape((F, 96, C), F32), shape((F, 48, C), F32)], [smem...  5.93 us
    unnamed x6, local copies, waits for them, and re-layouts  5.4 us
    ppermute x1, waiting for transfers between devices, local(): other = lax.ppermute(other, 'ha', [(i, i ^ 1) for i in range(HA)])  2.46 us
  transfers between devices with their start and end apart: 6, of which 5 were waited for; matrix products, arithmetic and copies ran while one was open for 1% of the time, Pallas kernels for 7%

profile of v2, /device:TPU:1, one launch (start us, length us, event | category | flops | bytes accessed | tf_op | source)
XLA Modules:
  0.0 81.0 jit_solution(9782677812070992252)
XLA Ops:
  0.6 0.8 fusion.5
  1.4 0.7 pad_maximum_fusion
  2.1 16.5 %all-gather = bf16[576,256]{1,0:T(8,128)(2,1)S(1)} all-gather(bf16[144,256]{1,0:T(8,128)(2,1)S(1)} %pad_maximum_fusion), channel_id=2, replica_groups=mesh['ta'=4,'ha'=8,'wa'=8] {'ta'}, dimensions={0}, use_global_device_ids=true | all-gather | bytes 368640 | tf_op jit(solution)/shard_map/all_gather | solution.py:268
  18.6 3.3 %collective-permute-start = (bf16[4,80,256]{2,1,0:T(8,128)(2,1)S(1)}, bf16[4,80,256]{2,1,0:T(8,128)(2,1)S(1)}, u32[]{:S(2)}, u32[]{:S(2)}) collective-permute-start(bf16[4,80,256]{2,1,0:T(8,128)(2,1)S(1)} %slice.33), channel_id=1, source_target_pairs={{0,56},{8,0},{16,8},{24,16},{32,24},{40,32},{48,40},{56,48},{1,57}... | collective-permute-start | bytes 491528 | tf_op jit(solution)/shard_map/ppermute | solution.py:259
  21.9 4.1 %collective-permute-done.h_ref = bf16[4,80,256]{2,1,0:T(8,128)(2,1)S(1)} collective-permute-done((bf16[4,80,256]{2,1,0:T(8,128)(2,1)S(1)}, bf16[4,80,256]{2,1,0:T(8,128)(2,1)S(1)}, u32[]{:S(2)}, u32[]{:S(2)}) %collective-permute-start) | collective-permute-done | bytes 163872 | tf_op jit(solution)/shard_map/ppermute | solution.py:259
  26.0 0.2 edge.1
  26.2 3.4 %collective-permute-start.1 = (bf16[8,16,256]{2,1,0:T(8,128)(2,1)S(1)}, bf16[8,16,256]{2,1,0:T(8,128)(2,1)S(1)}, u32[]{:S(2)}, u32[]{:S(2)}) collective-permute-start(bf16[8,16,256]{2,1,0:T(8,128)(2,1)S(1)} %edge.1), channel_id=1, source_target_pairs={{0,7},{1,0},{2,1},{3,2},{4,3},{5,4},{6,5},{7,6},{8,15},{9,8},{10,9... | collective-permute-start | bytes 196616 | tf_op jit(solution)/shard_map/ppermute | solution.py:259
  29.6 0.1 pad_add_fusion.at_ref
  29.7 1.3 %collective-permute-done.1.w_ref = bf16[8,16,256]{2,1,0:T(8,128)(2,1)S(1)} collective-permute-done((bf16[8,16,256]{2,1,0:T(8,128)(2,1)S(1)}, bf16[8,16,256]{2,1,0:T(8,128)(2,1)S(1)}, u32[]{:S(2)}, u32[]{:S(2)}) %collective-permute-start.1) | collective-permute-done | bytes 65568 | tf_op jit(solution)/shard_map/ppermute | solution.py:259
  31.0 0.0 copy-start
  31.0 2.0 %copy-done = bf16[6912,256]{1,0:T(8,128)(2,1)S(1)} copy-done((bf16[6912,256]{1,0:T(8,128)(2,1)S(1)}, bf16[6912,256]{1,0:T(8,128)(2,1)}, u32[]{:S(2)}) %copy-start) | copy-done | bytes 3538968
  33.0 14.5 %main.1 = (bf16[3584,128]{1,0:T(8,128)(2,1)S(1)}, bf16[3584,128]{1,0:T(8,128)(2,1)S(1)}, bf16[4,64,256]{2,1,0:T(8,128)(2,1)S(1)}) custom-call(s32[3]{0:T(128)S(1)} %pad_add_fusion.at_ref, bf16[4,144,256]{2,1,0:T(8,128)(2,1)S(1)} %bitcast.13, bf16[4,80,256]{2,1,0:T(8,128)(2,1)S(1)} %collective-permute-done.h_ref, ...), custom_call_target="tpu_custom_call" | custom-call | flops 5000000000 | bytes 8000000 | tf_op jit(solution)/shard_map/main/pallas_call | solution.py:272
  47.5 0.1 collective-permute-start.4
  47.6 2.5 %collective-permute-done.4 = bf16[3584,128]{1,0:T(8,128)(2,1)S(1)} collective-permute-done((bf16[3584,128]{1,0:T(8,128)(2,1)S(1)}, bf16[3584,128]{1,0:T(8,128)(2,1)S(1)}, u32[]{:S(2)}, u32[]{:S(2)}) %collective-permute-start.4) | collective-permute-done | bytes 917536 | tf_op jit(solution)/shard_map/ppermute | solution.py:291
  50.1 1.2 %add_convert_fusion = bf16[3584,128]{1,0:T(8,128)(2,1)} fusion(bf16[3584,128]{1,0:T(8,128)(2,1)S(1)} %collective-permute-done.4, bf16[3584,128]{1,0:T(8,128)(2,1)S(1)} %get-tuple-element.13), kind=kLoop, calls=%fused_computation | loop fusion | flops 1835008 | bytes 2752512 | tf_op jit(solution)/shard_map/convert_element_type | solution.py:306
  51.2 8.1 %all-to-all-start = ((bf16[32,112,128]{2,1,0:T(8,128)(2,1)}), bf16[32,112,128]{2,1,0:T(8,128)(2,1)S(1)}, u32[]{:S(2)}, u32[]{:S(2)}) async-start(bf16[32,112,128]{2,1,0:T(8,128)(2,1)} %bitcast.9), calls=%async_computation | async-start | bytes 1835008 | tf_op jit(solution)/shard_map/all_to_all | solution.py:308
  59.3 0.0 copy-start.1
  59.3 2.0 %copy-done.1 = bf16[6912,256]{1,0:T(8,128)(2,1)S(1)} copy-done((bf16[6912,256]{1,0:T(8,128)(2,1)S(1)}, bf16[6912,256]{1,0:T(8,128)(2,1)}, u32[]{:S(2)}) %copy-start.1) | copy-done | bytes 3538968
  61.3 5.9 %clip.1 = (f32[2,96,256]{2,1,0:T(8,128)S(1)}, f32[2,48,256]{2,1,0:T(8,128)S(1)}) custom-call(s32[3]{0:T(128)S(1)} %pad_add_fusion.at_ref, bf16[4,64,256]{2,1,0:T(8,128)(2,1)S(1)} %get-tuple-element.10.later_ref, bf16[6912,256]{1,0:T(8,128)(2,1)S(1)} %copy-done.1), custom_call_target="tpu_custom_call" | custom-call | flops 1000000000 | bytes 8000000 | tf_op jit(solution)/shard_map/clip/pallas_call | solution.py:292
  67.3 1.1 %collective-permute-start.2 = (f32[2,48,256]{2,1,0:T(8,128)S(1)}, f32[2,48,256]{2,1,0:T(8,128)S(1)}, u32[]{:S(2)}, u32[]{:S(2)}) collective-permute-start(f32[2,48,256]{2,1,0:T(8,128)S(1)} %get-tuple-element.12), channel_id=1, source_target_pairs={{0,1},{1,2},{2,3},{3,4},{4,5},{5,6},{6,7},{7,0},{8,9},{9,10},{10,1... | collective-permute-start | bytes 294920 | tf_op jit(solution)/shard_map/ppermute | solution.py:259
  68.4 6.3 %collective-permute-done.2 = f32[2,48,256]{2,1,0:T(8,128)S(1)} collective-permute-done((f32[2,48,256]{2,1,0:T(8,128)S(1)}, f32[2,48,256]{2,1,0:T(8,128)S(1)}, u32[]{:S(2)}, u32[]{:S(2)}) %collective-permute-start.2) | collective-permute-done | bytes 98336 | tf_op jit(solution)/shard_map/ppermute | solution.py:259
  74.8 2.7 %collective-permute-start.3 = (f32[2,2,16,256]{3,2,1,0:T(8,128)S(1)}, f32[2,2,16,256]{3,2,1,0:T(8,128)S(1)}, u32[]{:S(2)}, u32[]{:S(2)}) collective-permute-start(f32[2,2,16,256]{3,2,1,0:T(8,128)S(1)} %fusion), channel_id=1, source_target_pairs={{0,8},{8,16},{16,24},{24,32},{32,40},{40,48},{48,56},{56,0},{1,9},... | collective-permute-start | bytes 196616 | tf_op jit(solution)/shard_map/ppermute | solution.py:259
  77.5 1.3 %collective-permute-done.3 = f32[2,2,16,256]{3,2,1,0:T(8,128)S(1)} collective-permute-done((f32[2,2,16,256]{3,2,1,0:T(8,128)S(1)}, f32[2,2,16,256]{3,2,1,0:T(8,128)S(1)}, u32[]{:S(2)}, u32[]{:S(2)}) %collective-permute-start.3) | collective-permute-done | bytes 65568 | tf_op jit(solution)/shard_map/ppermute | solution.py:259
  78.8 0.6 pad_maximum_fusion.2
  79.4 0.0 all-to-all-done.parts_ref
  79.4 0.2 sum.1
  79.6 0.7 copy.7
  80.3 0.7 copy.8
  (5 shorter events, 0.1 us)
Async XLA Ops:
  18.6 7.4 %collective-permute-start = (bf16[4,80,256]{2,1,0:T(8,128)(2,1)S(1)}, bf16[4,80,256]{2,1,0:T(8,128)(2,1)S(1)}, u32[]{:S(2)}, u32[]{:S(2)}) collective-permute-start(bf16[4,80,256]{2,1,0:T(8,128)(2,1)S(1)} %slice.33), channel_id=1, source_target_pairs={{0,56},{8,0},{16,8},{24,16},{32,24},{40,32},{48,40},{56,48},{1,57}... | collective-permute-start | bytes 491528 | tf_op jit(solution)/shard_map/ppermute | solution.py:259
  26.2 4.8 %collective-permute-start.1 = (bf16[8,16,256]{2,1,0:T(8,128)(2,1)S(1)}, bf16[8,16,256]{2,1,0:T(8,128)(2,1)S(1)}, u32[]{:S(2)}, u32[]{:S(2)}) collective-permute-start(bf16[8,16,256]{2,1,0:T(8,128)(2,1)S(1)} %edge.1), channel_id=1, source_target_pairs={{0,7},{1,0},{2,1},{3,2},{4,3},{5,4},{6,5},{7,6},{8,15},{9,8},{10,9... | collective-permute-start | bytes 196616 | tf_op jit(solution)/shard_map/ppermute | solution.py:259
  31.0 2.0 %copy-start = (bf16[6912,256]{1,0:T(8,128)(2,1)S(1)}, bf16[6912,256]{1,0:T(8,128)(2,1)}, u32[]{:S(2)}) copy-start(bf16[6912,256]{1,0:T(8,128)(2,1)} %k1_ref.3) | copy-start | bytes 10616836
  47.5 2.6 %collective-permute-start.4 = (bf16[3584,128]{1,0:T(8,128)(2,1)S(1)}, bf16[3584,128]{1,0:T(8,128)(2,1)S(1)}, u32[]{:S(2)}, u32[]{:S(2)}) collective-permute-start(bf16[3584,128]{1,0:T(8,128)(2,1)S(1)} %get-tuple-element.14), channel_id=1, source_target_pairs={{0,8},{8,0},{16,24},{24,16},{32,40},{40,32},{48,56},{56,48},{1,9},... | collective-permute-start | bytes 2752520 | tf_op jit(solution)/shard_map/ppermute | solution.py:291
  51.2 28.2 %all-to-all-start = ((bf16[32,112,128]{2,1,0:T(8,128)(2,1)}), bf16[32,112,128]{2,1,0:T(8,128)(2,1)S(1)}, u32[]{:S(2)}, u32[]{:S(2)}) async-start(bf16[32,112,128]{2,1,0:T(8,128)(2,1)} %bitcast.9), calls=%async_computation | async-start | bytes 1835008 | tf_op jit(solution)/shard_map/all_to_all | solution.py:308
  59.3 2.0 %copy-start.1 = (bf16[6912,256]{1,0:T(8,128)(2,1)S(1)}, bf16[6912,256]{1,0:T(8,128)(2,1)}, u32[]{:S(2)}) copy-start(bf16[6912,256]{1,0:T(8,128)(2,1)} %k1_ref.3) | copy-start | bytes 10616836
  67.3 7.5 %collective-permute-start.2 = (f32[2,48,256]{2,1,0:T(8,128)S(1)}, f32[2,48,256]{2,1,0:T(8,128)S(1)}, u32[]{:S(2)}, u32[]{:S(2)}) collective-permute-start(f32[2,48,256]{2,1,0:T(8,128)S(1)} %get-tuple-element.12), channel_id=1, source_target_pairs={{0,1},{1,2},{2,3},{3,4},{4,5},{5,6},{6,7},{7,0},{8,9},{9,10},{10,1... | collective-permute-start | bytes 294920 | tf_op jit(solution)/shard_map/ppermute | solution.py:259
  74.8 4.0 %collective-permute-start.3 = (f32[2,2,16,256]{3,2,1,0:T(8,128)S(1)}, f32[2,2,16,256]{3,2,1,0:T(8,128)S(1)}, u32[]{:S(2)}, u32[]{:S(2)}) collective-permute-start(f32[2,2,16,256]{3,2,1,0:T(8,128)S(1)} %fusion), channel_id=1, source_target_pairs={{0,8},{8,16},{16,24},{24,32},{32,40},{40,48},{48,56},{56,0},{1,9},... | collective-permute-start | bytes 196616 | tf_op jit(solution)/shard_map/ppermute | solution.py:259

commit v3 on v2

--- a/solution.py
+++ b/solution.py
@@ -16,7 +16,7 @@
 PEERS = HA * WA // 2
 TAPS = [(a, b, c) for a in range(3) for b in range(3) for c in range(3)]
 BF16, F32 = jnp.bfloat16, jnp.float32
-VMEM_BYTES = 48 * 1024 * 1024
+VMEM_BYTES = 28 * 1024 * 1024
 
 
 def iota(shape, dim):
@@ -60,25 +60,43 @@
         out_ref[t] = dot(pick, jnp.concatenate(rows, axis=0)).astype(BF16)
 
 
-def main_kernel(
-    at_ref, g_ref, h_ref, w_ref, k1_ref, kd_ref, mine_ref, other_ref, later_ref,
-    k1, kd, xb, cu, pre, act, gp, tt, sem1, semd,
-):
-    ta, last_h, last_w = at_ref[0], at_ref[1] == HA - 1, at_ref[2] == WA - 1
-    core = lax.rem(at_ref[1], 2)
-    cot = 2 * F * W
+def pack_kernel(clip_ref, cot_ref, out_ref, sems):
+    half = 2 * W
+    copies = []
+    for f in range(F):
+        for part in range(2):
+            for k in range(2):
+                spot = part * HEAD + f * half + k * W
+                copies.append((clip_ref.at[f, 2 * part + k], out_ref.at[pl.ds(spot, W)]))
+    copies.append((cot_ref, out_ref.at[pl.ds(2 * F * W, 16)]))
+    copies = [pltpu.make_async_copy(x, y, sems.at[i]) for i, (x, y) in enumerate(copies)]
+    for copy in copies:
+        copy.start()
+    for copy in copies:
+        copy.wait()
+
+
+TABLE = 2 * C // 4 + C + SLOT
+
+
+def load_kernel(at_ref, after_ref, k1_ref, kd_ref, k1, kd, table_ref, sems):
     step = 3 * C
-    copies1 = [
-        pltpu.make_async_copy(k1_ref.at[pl.ds(i * step, step)], k1.at[pl.ds(i * step, step)], sem1.at[i])
-        for i in range(9)
-    ]
-    copiesd = [
-        pltpu.make_async_copy(kd_ref.at[pl.ds(i * step, step)], kd.at[pl.ds(i * step, step)], semd.at[i])
-        for i in range(9)
-    ]
-    for copy in copies1 + copiesd:
+    copies = []
+    for x, y in ((k1_ref, k1), (kd_ref, kd)):
+        for i in range(9):
+            part = pl.ds(i * step, step)
+            copies.append(pltpu.make_async_copy(x.at[part], y.at[part], sems.at[len(copies)]))
+    for copy in copies:
         copy.start()
-
+    m, n = iota((TABLE, C), 0), iota((TABLE, C), 1)
+    for r in range(4):
+        table_ref[r] = onehot(n == m + (4 * r - C // 2))
+    for copy in copies:
+        copy.wait()
+
+
+def window_pick(at_ref):
+    last_h, last_w = at_ref[1] == HA - 1, at_ref[2] == WA - 1
     m, n = iota((576, 112), 0), iota((576, 112), 1)
     tap, place = m // 64, m % 64
     b, c, k, col = tap // 3, tap % 3, place // W, column(place % W)
@@ -86,14 +104,50 @@
     source = jnp.where(v < W, row * W + v, 96 + row * 2 + v - W)
     out_h = last_h & (((b == 0) & (k == 3)) | ((b == 2) & (k == 2)))
     out_w = last_w & (((c == 0) & (col == 15)) | ((c == 2) & (col == 14)))
-    pick = onehot((n == source) & jnp.logical_not(out_h | out_w))
+    return onehot((n == source) & jnp.logical_not(out_h | out_w))
+
+
+def early_kernel(at_ref, g_ref, h_ref, k1, xb, pre, edge_ref):
+    pick = window_pick(at_ref)
+    edge_ref[...] = pick[:, 96:]
+    own = pick[:, :96]
     for i in range(9):
         xb[i, 0:2] = jnp.zeros((2, 64, C), BF16)
     for t in range(T):
-        rows = jnp.concatenate(frame_rows(g_ref, h_ref, t) + [w_ref[t]], axis=0)
-        built = dot(pick, rows).astype(BF16)
+        built = dot(own, jnp.concatenate(frame_rows(g_ref, h_ref, t), axis=0)).astype(BF16)
         for i in range(9):
             xb[i, t + 2] = built[i * 64 : (i + 1) * 64]
+    for i, (a, b, c) in enumerate(TAPS):
+        y = dot(xb[b * 3 + c, a : a + T].reshape(T * 64, C), k1[i * C : (i + 1) * C])
+        if i == 0:
+            pre[...] = y
+        else:
+            pre[...] += y
+
+
+def main_kernel(
+    at_ref, g_ref, h_ref, w_ref, k1, kd, table_ref, xb_ref, pre_ref, edge_ref,
+    mine_ref, other_ref, later_ref, xb, cu, pre, act, gp, tt, fix,
+):
+    ta, last_h, last_w = at_ref[0], at_ref[1] == HA - 1, at_ref[2] == WA - 1
+    core = lax.rem(at_ref[1], 2)
+    cot = 2 * F * W
+
+    edges = w_ref[...].reshape(T * 16, C)
+    m, n = iota((64, T * 16), 0), iota((64, T * 16), 1)
+    t, k, e = m // 8, (m // 2) % 4, m % 2
+    total = None
+    for i, (a, b, c) in enumerate(TAPS):
+        if c == 0:
+            continue
+        hit = (n == (t - 2 + a) * 16 + (k + b) * 2 + e + (c - 2)) & (e + c >= 2)
+        if b != 1:
+            hit = hit & jnp.logical_not(last_h & (k == (3 if b == 0 else 2)))
+        if c == 2:
+            hit = hit & jnp.logical_not(last_w & (e == 0))
+        y = dot(dot(onehot(hit), edges).astype(BF16), k1[i * C : (i + 1) * C])
+        total = y if total is None else total + y
+    fix[...] = total
 
     m, n = iota((144, 48), 0), iota((144, 48), 1)
     tap, place = m // 16, m % 16
@@ -113,18 +167,7 @@
         for i in range(9):
             cu[i, j] = built[i * 16 : (i + 1) * 16]
 
-    for i, (a, b, c) in enumerate(TAPS):
-        if i % 3 == 0:
-            copies1[i // 3].wait()
-        x = xb[b * 3 + c, a : a + T].reshape(T * 64, C)
-        y = dot(x, k1[i * C : (i + 1) * C])
-        if i == 0:
-            pre[...] = y
-        else:
-            pre[...] += y
-
-    for copy in copiesd:
-        copy.wait()
+    last = iota((8, C), 0) == 7
     for te in range(2):
         for ke in range(2):
             for ce in range(2):
@@ -139,7 +182,8 @@
                     for kk in range(2):
                         t, k = 2 * j + te, 2 * kk + ke
                         spot = t * 64 + k * W + ce * 8
-                        x = pre[spot : spot + 8]
+                        late = (t * 4 + k) * 2 + ce
+                        x = pre_ref[spot : spot + 8] + jnp.where(last, fix[late : late + 1], 0.0)
                         s = 1.0 / (1.0 + jnp.exp(-x))
                         at = (j * 2 + kk) * 8
                         g = total[at : at + 8]
@@ -158,27 +202,41 @@
         ],
         axis=0,
     )
+    late = edge_ref[...]
+    for bc in range(9):
+        xb[bc, 0:2] = jnp.zeros((2, 64, C), BF16)
+    for t in range(T):
+        built = dot(late, w_ref[t]).astype(BF16)
+        for bc in range(9):
+            xb[bc, t + 2] = xb_ref[bc, t + 2] + built[bc * 64 : (bc + 1) * 64]
     for bc in range(9):
         y = dot(left, xb[bc].reshape((T + 2) * 64, C)).astype(BF16)
         for a in range(3):
             tt[a * 9 + bc, 0:SHARE] = y[a * SHARE : (a + 1) * SHARE]
+    cots = {}
     for bc in range(9):
         for ja in range(2):
-            cots = dot_t(share, cu[bc, ja : ja + 4].reshape(64, C)).astype(BF16)
-            for a in (0, 1) if ja == 1 else (2,):
-                kind = (4 if a == 1 else 0) + (2 if bc // 3 == 1 else 0) + (1 if bc % 3 == 1 else 0)
-                tt[a * 9 + bc, SHARE:] = dot(cots, act[kind].astype(BF16)).astype(BF16)
-
-    m, n = iota((SLOT, C), 0), iota((SLOT, C), 1)
+            cots[bc, ja] = dot_t(share, cu[bc, ja : ja + 4].reshape(64, C)).astype(BF16)
+    for kind in range(8):
+        taps = [
+            (i, cots[b * 3 + c, 1 if a < 2 else 0])
+            for i, (a, b, c) in enumerate(TAPS)
+            if (a == 1) * 4 + (b == 1) * 2 + (c == 1) == kind
+        ]
+        y = dot(jnp.concatenate([x for _, x in taps], axis=0), act[kind].astype(BF16)).astype(BF16)
+        for place, (i, _) in enumerate(taps):
+            tt[i, SHARE:] = y[place * SHARE : (place + 1) * SHARE]
+
     for x in range(HA // 2):
         for w in range(WA):
             pair = []
             for cc in range(2):
                 first = ((x * 2 + cc) * WA + w) * PART
                 tap, off = first // C, first % C
-                y = dot_t(onehot((n == m + off) & (m < PART)), tt[tap])
+                r, low = off % 16 // 4, off // 16 * 16 + C // 2
+                y = dot_t(table_ref[r, low : low + SLOT], tt[tap])
                 if off + PART > C:
-                    y += dot_t(onehot((n == m + off - C) & (m < PART)), tt[tap + 1])
+                    y += dot_t(table_ref[r, low - C : low - C + SLOT], tt[tap + 1])
                 pair.append(y)
             spot = (x * WA + w) * SLOT
             mine_ref[spot : spot + SLOT] = jnp.where(core == 0, pair[0], pair[1]).astype(BF16)
@@ -188,15 +246,8 @@
 WIDE = 144
 
 
-def clip_kernel(at_ref, later_ref, k1_ref, main_ref, spill_ref, k1, yb, acc, sem):
+def clip_kernel(at_ref, later_ref, k1, main_ref, spill_ref, yb, acc):
     last_h, last_w = at_ref[1] == HA - 1, at_ref[2] == WA - 1
-    step = 3 * C
-    copies = [
-        pltpu.make_async_copy(k1_ref.at[pl.ds(i * step, step)], k1.at[pl.ds(i * step, step)], sem.at[i])
-        for i in range(9)
-    ]
-    for copy in copies:
-        copy.start()
     for i in range(9):
         b, c = i // 3, i % 3
         m, n = iota((WIDE, 64), 0), iota((WIDE, 64), 1)
@@ -213,8 +264,6 @@
         for t in range(F + 2):
             yb[i, t] = dot(pick, later_ref[t]).astype(BF16)
     for i, (a, b, c) in enumerate(TAPS):
-        if i % 3 == 0:
-            copies[i // 3].wait()
         y = dot_t(yb[b * 3 + c, 2 - a : 2 - a + F].reshape(F * WIDE, C), k1[i * C : (i + 1) * C])
         if i == 0:
             acc[...] = y
@@ -225,12 +274,17 @@
         spill_ref[f] = acc[f * WIDE + 96 : (f + 1) * WIDE]
 
 
+def join_kernel(mine_ref, other_ref, after_ref, out_ref):
+    out_ref[...] = (mine_ref[...].astype(F32) + other_ref[...].astype(F32)).astype(BF16)
+
+
 def sum_kernel(parts_ref, conv_ref, down_ref):
     total = parts_ref[0].astype(F32)
     for i in range(1, PEERS):
         total += parts_ref[i].astype(F32)
-    conv_ref[...] = total[:PART, :SHARE]
-    down_ref[...] = total[:PART, SHARE:]
+    total = jnp.concatenate([total, jnp.zeros((128 - SLOT, 2 * SHARE), F32)], axis=0).T
+    conv_ref[...] = total[:SHARE, :PART]
+    down_ref[...] = total[SHARE:, :PART]
 
 
 def whole():
@@ -254,6 +308,18 @@
     return jax.ShapeDtypeStruct(dims, dtype)
 
 
+def on_chip(dims, dtype=BF16):
+    return pltpu.VMEM(dims, dtype)
+
+
+def in_hbm(x):
+    return pltpu.with_memory_space_constraint(x, pltpu.HBM)
+
+
+def in_vmem(x):
+    return pltpu.with_memory_space_constraint(x, pltpu.VMEM)
+
+
 def shift(x, axis, by):
     count = lax.axis_size(axis)
     return lax.ppermute(x, axis, [(i, (i + by) % count) for i in range(count)])
@@ -262,59 +328,77 @@
 def local(clip, conv_weight, down_weight, out_cotangent):
     smem, anywhere = pl.BlockSpec(memory_space=pltpu.SMEM), pl.BlockSpec(memory_space=pl.ANY)
     at = jnp.stack([lax.axis_index(a) for a in ("ta", "ha", "wa")]).astype(jnp.int32)
-    head = clip[:, :2].reshape(2 * F * W, C)
-    tail = clip[:, 2:].reshape(2 * F * W, C)
-    packed = jnp.concatenate([head, out_cotangent.reshape(-1, C), tail], axis=0)
+    dma = pltpu.SemaphoreType.DMA
+    packed = call(
+        pack_kernel, shape((BLOCK, C)), [anywhere] * 2, [dma((9,))], 10**5, "pack"
+    )(in_hbm(clip), in_hbm(out_cotangent.reshape(-1, C)))
     g = lax.all_gather(packed, "ta", axis=0, tiled=False)
     h = shift(g[:, :HEAD], "ha", -1)
+    weight = on_chip((27 * C, C))
+    k1, kd, table = call(
+        load_kernel,
+        [weight, weight, on_chip((4, TABLE, C))],
+        [smem] + [anywhere] * 3,
+        [dma((18,))],
+        3 * 10**9,
+        "load",
+    )(at, g, in_hbm(conv_weight), in_hbm(down_weight))
+    k1, kd, table = in_vmem(k1), in_vmem(kd), in_vmem(table)
     w = call(edge_kernel, shape((T, 16, C)), [whole()] * 2, [], 10**7, "edge")(g, h)
     w = shift(w, "wa", -1)
+    xb, pre, edge = call(
+        early_kernel,
+        [shape((9, T + 2, 64, C)), shape((T * 64, C), F32), shape((576, 16))],
+        [smem] + [whole()] * 3,
+        [],
+        4 * 10**9,
+        "early",
+    )(at, g, h, k1)
     mine, other, later = call(
         main_kernel,
         [shape((PEERS * SLOT, 2 * SHARE)), shape((PEERS * SLOT, 2 * SHARE)), shape((F + 2, 64, C))],
-        [smem, whole(), whole(), whole(), anywhere, anywhere],
+        [smem] + [whole()] * 9,
         [
-            pltpu.VMEM((27 * C, C), BF16),
-            pltpu.VMEM((27 * C, C), BF16),
             pltpu.VMEM((9, T + 2, 64, C), BF16),
             pltpu.VMEM((9, TA + 1, 16, C), BF16),
             pltpu.VMEM((T * 64, C), F32),
             pltpu.VMEM((8, 64, C), F32),
             pltpu.VMEM((T + 4, 64, C), BF16),
             pltpu.VMEM((27, 2 * SHARE, C), BF16),
-            pltpu.SemaphoreType.DMA((9,)),
-            pltpu.SemaphoreType.DMA((9,)),
+            pltpu.VMEM((64, C), F32),
         ],
         5 * 10**9,
         "main",
-    )(at, g, h, w, conv_weight, down_weight)
+    )(at, g, h, w, k1, kd, table, xb, pre, edge)
     other = lax.ppermute(other, "ha", [(i, i ^ 1) for i in range(HA)])
     grad_clip, spill = call(
         clip_kernel,
         [shape((F, 96, C), F32), shape((F, 48, C), F32)],
-        [smem, whole(), anywhere],
-        [
-            pltpu.VMEM((27 * C, C), BF16),
-            pltpu.VMEM((9, F + 2, WIDE, C), BF16),
-            pltpu.VMEM((F * WIDE, C), F32),
-            pltpu.SemaphoreType.DMA((9,)),
-        ],
+        [smem, whole(), whole()],
+        [pltpu.VMEM((9, F + 2, WIDE, C), BF16), pltpu.VMEM((F * WIDE, C), F32)],
         10**9,
         "clip",
-    )(at, later, conv_weight)
+    )(at, later, k1)
+    pair = call(
+        join_kernel,
+        shape((PEERS * SLOT, 2 * SHARE)),
+        [whole(), whole(), anywhere],
+        [],
+        10**6,
+        "join",
+    )(mine, other, spill)
     spill = shift(spill, "wa", 1)
-    pair = (mine.astype(F32) + other.astype(F32)).astype(BF16)
     groups = [[i * WA + w for i in range(c, HA, 2) for w in range(WA)] for c in range(2)]
     parts = lax.all_to_all(pair, ("ha", "wa"), 0, 0, axis_index_groups=groups, tiled=True)
     grad_conv, grad_down = call(
-        sum_kernel, [shape((PART, SHARE), F32), shape((PART, SHARE), F32)], [whole()], [], 10**6, "sum"
+        sum_kernel, [shape((SHARE, PART), F32)] * 2, [whole()], [], 10**6, "sum"
     )(parts.reshape(PEERS, SLOT, 2 * SHARE))
     grad_clip = grad_clip.reshape(F, 6, W, C)
     spill = spill.reshape(F, 6, 8, C)
     grad_clip = jnp.concatenate([grad_clip[:, :, :8] + spill, grad_clip[:, :, 8:]], axis=2)
     past = shift(grad_clip[:, R:], "ha", 1)
     grad_clip = jnp.concatenate([grad_clip[:, :2] + past, grad_clip[:, 2:R]], axis=1).astype(BF16)
-    return (grad_clip, grad_conv, grad_down)
+    return (grad_clip, grad_conv.T, grad_down.T)
 
 
 def solution(mesh):

time: 81.4 us -> 70.9 us (0.87)
  local copies, waits for them, and re-layouts: 6.2 us -> 0.01 us
  starting transfers between devices: 18.7 us -> 16.8 us
  other arithmetic: 2.62 us -> 0.76 us
  Pallas kernels: 20.8 us -> 19.4 us
  waiting for transfers between devices: 15.5 us -> 16.4 us
    pallas_call x1 -> x5, Pallas kernels: 0.21 us -> 10.6 us  [the longest x1 4.02 us: local(): call(early_kernel, [shape((9, T + 2, 64, C)), shape((T * 64, C), F32), sh...]
    pallas_call x1, Pallas kernels: 14.5 us -> 6.2 us  [local(): call(main_kernel, [shape((PEERS * SLOT, 2 * SHARE)), shape((PEERS * SLOT,...]
    unnamed x6 -> x0, local copies, waits for them, and re-layouts: 5.4 us -> none
    pallas_call x1, Pallas kernels: 5.93 us -> 2.47 us  [local(): call(clip_kernel, [shape((F, 96, C), F32), shape((F, 48, C), F32)], [smem...]
    ppermute x4, waiting for transfers between devices: 13 us -> 16.4 us  [shift(): return lax.ppermute(x, axis, [(i, (i + by) % count) for i in range(count)])]
    ppermute x1, waiting for transfers between devices: 2.46 us -> 0.01 us  [local(): other = lax.ppermute(other, 'ha', [(i, i ^ 1) for i in range(HA)])]
    all_to_all x1, starting transfers between devices: 8.1 us -> 6.4 us  [local(): lax.all_to_all(pair, ('ha', 'wa'), 0, 0, axis_index_groups=groups, tiled=...]
    convert_element_type x1 -> x0, other arithmetic: 1.16 us -> none  [local(): pair = (mine.astype(F32) + other.astype(F32)).astype(BF16)]
  transfers between devices with their start and end apart: 6 -> 6, of which waited for: 5 -> 3; matrix products, arithmetic and copies ran while one was open for 1% -> 1% of each run, Pallas kernels for 7% -> 14%
where the time goes in v3:
time: 70.9 us; the launch traced here: 70.6 us
  Pallas kernels  19.4 us (27%)
  starting transfers between devices  16.8 us (24%)
  blocking collectives  16.5 us (23%)
  waiting for transfers between devices  16.4 us (23%)
  other arithmetic  0.76 us (1%)
  between operations  0.73 us (1%)
    all_gather x1, blocking collectives, local(): g = lax.all_gather(packed, 'ta', axis=0, tiled=False)  16.5 us
    ppermute x4, waiting for transfers between devices, shift(): return lax.ppermute(x, axis, [(i, (i + by) % count) for i in range(count)])  16.4 us
    ppermute x4, starting transfers between devices, shift(): return lax.ppermute(x, axis, [(i, (i + by) % count) for i in range(count)])  10.3 us
    all_to_all x1, starting transfers between devices, local(): lax.all_to_all(pair, ('ha', 'wa'), 0, 0, axis_index_groups=groups, tiled=...  6.4 us
    pallas_call x1, Pallas kernels, local(): call(main_kernel, [shape((PEERS * SLOT, 2 * SHARE)), shape((PEERS * SLOT,...  6.2 us
    pallas_call x1, Pallas kernels, local(): call(early_kernel, [shape((9, T + 2, 64, C)), shape((T * 64, C), F32), sh...  4.02 us
    pallas_call x1, Pallas kernels, local(): call(load_kernel, [weight, weight, on_chip((4, TABLE, C))], [smem] + [any...  3.69 us
    pallas_call x1, Pallas kernels, local(): call(clip_kernel, [shape((F, 96, C), F32), shape((F, 48, C), F32)], [smem...  2.47 us
  transfers between devices with their start and end apart: 6, of which 3 were waited for; matrix products, arithmetic and copies ran while one was open for 1% of the time, Pallas kernels for 14%

profile of v3, /device:TPU:1, one launch (start us, length us, event | category | flops | bytes accessed | tf_op | source)
XLA Modules:
  0.0 70.6 jit_solution(3786670319388711205)
XLA Ops:
  0.6 0.9 %pack.1 = bf16[144,256]{1,0:T(8,128)(2,1)S(1)} custom-call(bf16[2,4,16,256]{3,2,1,0:T(8,128)(2,1)} %clip_ref.1, bf16[16,256]{1,0:T(8,128)(2,1)} %bitcast.17), custom_call_target="tpu_custom_call" | custom-call | flops 100000 | bytes 8000000 | tf_op jit(solution)/shard_map/pack/pallas_call | solution.py:332
  1.5 16.5 %all-gather = bf16[576,256]{1,0:T(8,128)(2,1)S(1)} all-gather(bf16[144,256]{1,0:T(8,128)(2,1)S(1)} %pack.1), channel_id=2, replica_groups=mesh['ta'=4,'ha'=8,'wa'=8] {'ta'}, dimensions={0}, use_global_device_ids=true | all-gather | bytes 368640 | tf_op jit(solution)/shard_map/all_gather | solution.py:335
  18.0 3.3 %collective-permute-start = (bf16[4,80,256]{2,1,0:T(8,128)(2,1)S(1)}, bf16[4,80,256]{2,1,0:T(8,128)(2,1)S(1)}, u32[]{:S(2)}, u32[]{:S(2)}) collective-permute-start(bf16[4,80,256]{2,1,0:T(8,128)(2,1)S(1)} %slice.25), channel_id=1, source_target_pairs={{0,56},{8,0},{16,8},{24,16},{32,24},{40,32},{48,40},{56,48},{1,57}... | collective-permute-start | bytes 491528 | tf_op jit(solution)/shard_map/ppermute | solution.py:325
  21.4 0.1 pad_add_fusion.at_ref
  21.4 3.7 %load.1 = (bf16[6912,256]{1,0:T(8,128)(2,1)S(1)}, bf16[6912,256]{1,0:T(8,128)(2,1)S(1)}, bf16[4,496,256]{2,1,0:T(8,128)(2,1)S(1)}) custom-call(s32[3]{0:T(128)S(1)} %pad_add_fusion.at_ref, bf16[4,144,256]{2,1,0:T(8,128)(2,1)S(1)} %bitcast.12, bf16[6912,256]{1,0:T(8,128)(2,1)} %k1_ref.1, bf16[6912,256]{1,0:T(8,128)(2,1)} %kd_ref.1), custom_call_target="tpu_custom_call" | custom-call | flops 3000000000 | bytes 8000000 | tf_op jit(solution)/shard_map/load/pallas_call | solution.py:338
  25.1 0.3 collective-permute-done.h_ref
  25.5 0.2 edge.1
  25.6 3.4 %collective-permute-start.1 = (bf16[8,16,256]{2,1,0:T(8,128)(2,1)S(1)}, bf16[8,16,256]{2,1,0:T(8,128)(2,1)S(1)}, u32[]{:S(2)}, u32[]{:S(2)}) collective-permute-start(bf16[8,16,256]{2,1,0:T(8,128)(2,1)S(1)} %edge.1), channel_id=1, source_target_pairs={{0,7},{1,0},{2,1},{3,2},{4,3},{5,4},{6,5},{7,6},{8,15},{9,8},{10,9... | collective-permute-start | bytes 196616 | tf_op jit(solution)/shard_map/ppermute | solution.py:325
  29.1 4.0 %early.1 = (bf16[9,10,64,256]{3,2,1,0:T(8,128)(2,1)S(1)}, f32[512,256]{1,0:T(8,128)S(1)}, bf16[576,16]{1,0:T(8,128)(2,1)S(1)}) custom-call(s32[3]{0:T(128)S(1)} %pad_add_fusion.at_ref, bf16[4,144,256]{2,1,0:T(8,128)(2,1)S(1)} %bitcast.14, bf16[4,80,256]{2,1,0:T(8,128)(2,1)S(1)} %collective-permute-done.h_ref, bf16[6912,256]{1,0:T(8,128)(2,1)S(1)} %get-tuple-element.16.k1), custom_call_target="tpu_custom_call" | custom-call | flops 4000000000 | bytes 8000000 | tf_op jit(solution)/shard_map/early/pallas_call | solution.py:349
  33.1 0.0 collective-permute-done.1.w_ref
  33.1 6.2 %main.1 = (bf16[3584,128]{1,0:T(8,128)(2,1)S(1)}, bf16[3584,128]{1,0:T(8,128)(2,1)S(1)}, bf16[4,64,256]{2,1,0:T(8,128)(2,1)S(1)}) custom-call(s32[3]{0:T(128)S(1)} %pad_add_fusion.at_ref, bf16[4,144,256]{2,1,0:T(8,128)(2,1)S(1)} %bitcast.15, bf16[4,80,256]{2,1,0:T(8,128)(2,1)S(1)} %collective-permute-done.h_ref, ...), custom_call_target="tpu_custom_call" | custom-call | flops 5000000000 | bytes 8000000 | tf_op jit(solution)/shard_map/main/pallas_call | solution.py:357
  39.3 0.1 collective-permute-start.4
  39.4 2.5 %clip.1 = (f32[2,96,256]{2,1,0:T(8,128)S(1)}, f32[2,48,256]{2,1,0:T(8,128)S(1)}) custom-call(s32[3]{0:T(128)S(1)} %pad_add_fusion.at_ref, bf16[4,64,256]{2,1,0:T(8,128)(2,1)S(1)} %get-tuple-element.22.later_ref, bf16[6912,256]{1,0:T(8,128)(2,1)S(1)} %get-tuple-element.16.k1), custom_call_target="tpu_custom_call" | custom-call | flops 1000000000 | bytes 8000000 | tf_op jit(solution)/shard_map/clip/pallas_call | solution.py:374
  41.9 0.0 collective-permute-done.4.other_ref
  41.9 1.1 %join.1 = bf16[3584,128]{1,0:T(8,128)(2,1)} custom-call(bf16[3584,128]{1,0:T(8,128)(2,1)S(1)} %get-tuple-element.25.mine_ref, bf16[3584,128]{1,0:T(8,128)(2,1)S(1)} %collective-permute-done.4.other_ref, f32[2,48,256]{2,1,0:T(8,128)S(1)} %get-tuple-element.24.after_ref), custom_call_target="tpu_custom_call" | custom-call | flops 1000000 | bytes 8000000 | tf_op jit(solution)/shard_map/join/pallas_call | solution.py:382
  43.1 6.4 %all-to-all-start = ((bf16[32,112,128]{2,1,0:T(8,128)(2,1)}), bf16[32,112,128]{2,1,0:T(8,128)(2,1)S(1)}, u32[]{:S(2)}, u32[]{:S(2)}) async-start(bf16[32,112,128]{2,1,0:T(8,128)(2,1)} %bitcast.7), calls=%async_computation | async-start | bytes 1835008 | tf_op jit(solution)/shard_map/all_to_all | solution.py:392
  49.5 1.3 %collective-permute-start.2 = (f32[2,48,256]{2,1,0:T(8,128)S(1)}, f32[2,48,256]{2,1,0:T(8,128)S(1)}, u32[]{:S(2)}, u32[]{:S(2)}) collective-permute-start(f32[2,48,256]{2,1,0:T(8,128)S(1)} %get-tuple-element.24.after_ref), channel_id=1, source_target_pairs={{0,1},{1,2},{2,3},{3,4},{4,5},{5,6},{6,7},{7,0},{8,9},{9,10},{10,1... | collective-permute-start | bytes 294920 | tf_op jit(solution)/shard_map/ppermute | solution.py:325
  50.8 14.8 %collective-permute-done.2 = f32[2,48,256]{2,1,0:T(8,128)S(1)} collective-permute-done((f32[2,48,256]{2,1,0:T(8,128)S(1)}, f32[2,48,256]{2,1,0:T(8,128)S(1)}, u32[]{:S(2)}, u32[]{:S(2)}) %collective-permute-start.2) | collective-permute-done | bytes 98336 | tf_op jit(solution)/shard_map/ppermute | solution.py:325
  65.6 2.2 %collective-permute-start.3 = (f32[2,2,16,256]{3,2,1,0:T(8,128)S(1)}, f32[2,2,16,256]{3,2,1,0:T(8,128)S(1)}, u32[]{:S(2)}, u32[]{:S(2)}) collective-permute-start(f32[2,2,16,256]{3,2,1,0:T(8,128)S(1)} %fusion), channel_id=1, source_target_pairs={{0,8},{8,16},{16,24},{24,32},{32,40},{40,48},{48,56},{56,0},{1,9},... | collective-permute-start | bytes 196616 | tf_op jit(solution)/shard_map/ppermute | solution.py:325
  67.8 1.3 %collective-permute-done.3 = f32[2,2,16,256]{3,2,1,0:T(8,128)S(1)} collective-permute-done((f32[2,2,16,256]{3,2,1,0:T(8,128)S(1)}, f32[2,2,16,256]{3,2,1,0:T(8,128)S(1)}, u32[]{:S(2)}, u32[]{:S(2)}) %collective-permute-start.3) | collective-permute-done | bytes 65568 | tf_op jit(solution)/shard_map/ppermute | solution.py:325
  69.1 0.6 pad_maximum_fusion.1
  69.8 0.0 all-to-all-done.parts_ref
  69.8 0.8 %sum.1 = (f32[64,108]{1,0:T(8,128)}, f32[64,108]{1,0:T(8,128)}) custom-call(bf16[32,112,128]{2,1,0:T(8,128)(2,1)S(1)} %all-to-all-done.parts_ref), custom_call_target="tpu_custom_call" | custom-call | flops 1000000 | bytes 8000000 | tf_op jit(solution)/shard_map/sum/pallas_call | solution.py:393
  (5 shorter events, 0.1 us)
Async XLA Ops:
  18.0 7.4 %collective-permute-start = (bf16[4,80,256]{2,1,0:T(8,128)(2,1)S(1)}, bf16[4,80,256]{2,1,0:T(8,128)(2,1)S(1)}, u32[]{:S(2)}, u32[]{:S(2)}) collective-permute-start(bf16[4,80,256]{2,1,0:T(8,128)(2,1)S(1)} %slice.25), channel_id=1, source_target_pairs={{0,56},{8,0},{16,8},{24,16},{32,24},{40,32},{48,40},{56,48},{1,57}... | collective-permute-start | bytes 491528 | tf_op jit(solution)/shard_map/ppermute | solution.py:325
  25.6 7.5 %collective-permute-start.1 = (bf16[8,16,256]{2,1,0:T(8,128)(2,1)S(1)}, bf16[8,16,256]{2,1,0:T(8,128)(2,1)S(1)}, u32[]{:S(2)}, u32[]{:S(2)}) collective-permute-start(bf16[8,16,256]{2,1,0:T(8,128)(2,1)S(1)} %edge.1), channel_id=1, source_target_pairs={{0,7},{1,0},{2,1},{3,2},{4,3},{5,4},{6,5},{7,6},{8,15},{9,8},{10,9... | collective-permute-start | bytes 196616 | tf_op jit(solution)/shard_map/ppermute | solution.py:325
  39.3 2.6 %collective-permute-start.4 = (bf16[3584,128]{1,0:T(8,128)(2,1)S(1)}, bf16[3584,128]{1,0:T(8,128)(2,1)S(1)}, u32[]{:S(2)}, u32[]{:S(2)}) collective-permute-start(bf16[3584,128]{1,0:T(8,128)(2,1)S(1)} %get-tuple-element.26), channel_id=1, source_target_pairs={{0,8},{8,0},{16,24},{24,16},{32,40},{40,32},{48,56},{56,48},{1,9},... | collective-permute-start | bytes 2752520 | tf_op jit(solution)/shard_map/ppermute | solution.py:373
  43.1 26.7 %all-to-all-start = ((bf16[32,112,128]{2,1,0:T(8,128)(2,1)}), bf16[32,112,128]{2,1,0:T(8,128)(2,1)S(1)}, u32[]{:S(2)}, u32[]{:S(2)}) async-start(bf16[32,112,128]{2,1,0:T(8,128)(2,1)} %bitcast.7), calls=%async_computation | async-start | bytes 1835008 | tf_op jit(solution)/shard_map/all_to_all | solution.py:392
  49.5 16.1 %collective-permute-start.2 = (f32[2,48,256]{2,1,0:T(8,128)S(1)}, f32[2,48,256]{2,1,0:T(8,128)S(1)}, u32[]{:S(2)}, u32[]{:S(2)}) collective-permute-start(f32[2,48,256]{2,1,0:T(8,128)S(1)} %get-tuple-element.24.after_ref), channel_id=1, source_target_pairs={{0,1},{1,2},{2,3},{3,4},{4,5},{5,6},{6,7},{7,0},{8,9},{9,10},{10,1... | collective-permute-start | bytes 294920 | tf_op jit(solution)/shard_map/ppermute | solution.py:325
  65.6 3.6 %collective-permute-start.3 = (f32[2,2,16,256]{3,2,1,0:T(8,128)S(1)}, f32[2,2,16,256]{3,2,1,0:T(8,128)S(1)}, u32[]{:S(2)}, u32[]{:S(2)}) collective-permute-start(f32[2,2,16,256]{3,2,1,0:T(8,128)S(1)} %fusion), channel_id=1, source_target_pairs={{0,8},{8,16},{16,24},{24,32},{32,40},{40,48},{48,56},{56,0},{1,9},... | collective-permute-start | bytes 196616 | tf_op jit(solution)/shard_map/ppermute | solution.py:325

commit v4 on v3

v4 whole, which is shorter than its diff:
```python
import jax
import jax.numpy as jnp
from jax import lax
from jax.experimental import pallas as pl
from jax.experimental.pallas import tpu as pltpu
from jax.sharding import PartitionSpec as P

F, R, W, C = 2, 4, 16, 256
TA, HA, WA = 4, 8, 8
T = TA * F
HEAD = 2 * F * W + (R // 2) * (W // 2)
BLOCK = F * R * W + (R // 2) * (W // 2)
SHARE = C // TA
PART = 27 * C // (HA * WA)
SLOT = 112
PEERS = HA * WA // 2
TAPS = [(a, b, c) for a in range(3) for b in range(3) for c in range(3)]
BF16, F32 = jnp.bfloat16, jnp.float32
VMEM_BYTES = 28 * 1024 * 1024


def iota(shape, dim):
    return lax.broadcasted_iota(jnp.int32, shape, dim)


def onehot(hit):
    return jnp.where(hit, 1.0, 0.0).astype(F32).astype(BF16)


def div(x, n):
    return lax.shift_right_logical(x, n.bit_length() - 1)


def mod(x, n):
    return lax.bitwise_and(x, n - 1)


def third(x):
    high = jnp.where(x >= 3, 1, 0) + jnp.where(x >= 6, 1, 0)
    return high, x - 3 * high


def dot(x, y):
    return jnp.dot(x, y, preferred_element_type=F32)


def dot_t(x, y):
    return lax.dot_general(x, y, (((1,), (1,)), ((), ())), preferred_element_type=F32)


def column(order):
    return jnp.where(order < W // 2, 2 * order, 2 * (order - W // 2) + 1)


def frame_rows(g_ref, h_ref, t):
    s, f = t // F, t % F
    low = 2 * W * f
    return [
        g_ref[s, low : low + 2 * W],
        g_ref[s, HEAD + low : HEAD + low + 2 * W],
        h_ref[s, low : low + 2 * W],
    ]


def edge_kernel(g_ref, h_ref, out_ref):
    cot = 2 * F * W
    m, n = iota((16, 128), 0), iota((16, 128), 1)
    source = jnp.where(m < 12, div(m, 2) * W + mod(m, 2), jnp.where(m < 14, 96 + (m - 12) * 8, 112))
    pick = onehot((n == source) & (m < 15))
    for t in range(T):
        s = t // F
        rows = frame_rows(g_ref, h_ref, t) + [g_ref[s, cot : cot + 16], h_ref[s, cot : cot + 16]]
        out_ref[t] = dot(pick, jnp.concatenate(rows, axis=0)).astype(BF16)


def pack_kernel(clip_ref, cot_ref, out_ref, sems):
    half = 2 * W
    copies = []
    for f in range(F):
        for part in range(2):
            for k in range(2):
                spot = part * HEAD + f * half + k * W
                copies.append((clip_ref.at[f, 2 * part + k], out_ref.at[pl.ds(spot, W)]))
    copies.append((cot_ref, out_ref.at[pl.ds(2 * F * W, 16)]))
    copies = [pltpu.make_async_copy(x, y, sems.at[i]) for i, (x, y) in enumerate(copies)]
    for copy in copies:
        copy.start()
    for copy in copies:
        copy.wait()


def head_kernel(at_ref, own_ref, one_ref, two_ref, three_ref, after_ref, head_ref):
    for back, ref in enumerate((own_ref, one_ref, two_ref, three_ref)):
        head_ref[lax.rem(at_ref[0] + TA - back, TA)] = ref[:HEAD]


def fetch(source, target, sems):
    step = 3 * C
    parts = [pl.ds(i * step, step) for i in range(9)]
    copies = [
        pltpu.make_async_copy(source.at[part], target.at[part], sems.at[i])
        for i, part in enumerate(parts)
    ]
    for copy in copies:
        copy.start()
    return copies


def turn(copies, plain, turned):
    for i in range(27):
        if i % 3 == 0:
            copies[i // 3].wait()
        turned[i * C : (i + 1) * C] = plain[i * C : (i + 1) * C].T


def load_kernel(at_ref, after_ref, k1_ref, k1, k1t, sems):
    turn(fetch(k1_ref, k1, sems), k1, k1t)


def window_pick(at_ref, b):
    last_h, last_w = at_ref[1] == HA - 1, at_ref[2] == WA - 1
    m, n = iota((192, 112), 0), iota((192, 112), 1)
    c, place = div(m, 64), mod(m, 64)
    k, col = div(place, W), column(mod(place, W))
    row, v = k + b, col + c
    source = jnp.where(v < W, row * W + v, 96 + row * 2 + v - W)
    out = last_w & (((c == 0) & (col == 15)) | ((c == 2) & (col == 14)))
    if b != 1:
        out = out | (last_h & (k == (3 if b == 0 else 2)))
    return onehot((n == source) & jnp.logical_not(out))


def add_taps(total, taps, x, k1):
    for first, (a, b, c) in enumerate(taps):
        i = (a * 3 + b) * 3 + c
        y = dot(x(b, c)[a : a + T].reshape(T * 64, C), k1[i * C : (i + 1) * C])
        if first == 0 and total[1] is None:
            total[0][...] = y
        elif first == 0:
            total[0][...] = total[1][...] + y
        else:
            total[0][...] += y


def own_kernel(
    at_ref, own_ref, one_ref, two_ref, three_ref, after_ref, k1, kd_ref, g_ref, xb, pre, kdt, kd, sems
):
    copies = fetch(kd_ref, kd, sems)
    for back, ref in enumerate((own_ref, one_ref, two_ref, three_ref)):
        g_ref[lax.rem(at_ref[0] + TA - back, TA)] = ref[...]
    pick = window_pick(at_ref, 0)[:, :64]
    for c in range(3):
        xb[c, 0:2] = jnp.zeros((2, 64, C), BF16)
    for t in range(T):
        s, low = t // F, 2 * W * (t % F)
        rows = [g_ref[s, low : low + 2 * W], g_ref[s, HEAD + low : HEAD + low + 2 * W]]
        built = dot(pick, jnp.concatenate(rows, axis=0)).astype(BF16)
        for c in range(3):
            xb[c, t + 2] = built[c * 64 : (c + 1) * 64]
    add_taps((pre, None), [x for x in TAPS if x[1] == 0], lambda b, c: xb.at[c], k1)
    turn(copies, kd, kdt)


def early_kernel(at_ref, g_ref, h_ref, k1, pre_ref, xb, pre, edge_ref):
    picks = [window_pick(at_ref, b) for b in range(3)]
    for b in range(3):
        edge_ref[b] = picks[b][64:, 96:]
    own = jnp.concatenate([picks[1][:, :96], picks[2][:, :96]], axis=0)
    for i in range(6):
        xb[i, 0:2] = jnp.zeros((2, 64, C), BF16)
    for t in range(T):
        built = dot(own, jnp.concatenate(frame_rows(g_ref, h_ref, t), axis=0)).astype(BF16)
        for i in range(6):
            xb[i, t + 2] = built[i * 64 : (i + 1) * 64]
    taps = [x for x in TAPS if x[1] != 0]
    add_taps((pre, pre_ref), taps, lambda b, c: xb.at[b * 3 + c - 3], k1)


SPILL = 48


def clip_pick(at_ref, b, c, rows, width, first):
    m, n = iota((rows, 64), 0), iota((rows, 64), 1)
    h, v = div(m, width), first + mod(m, width)
    k, col = div(n, W), column(mod(n, W))
    hit = (h == k + b) & (v == col + c) & (v < W + 2)
    if b != 1:
        hit = hit & jnp.logical_not((at_ref[1] == HA - 1) & (k == (3 if b == 0 else 2)))
    if c != 1:
        hit = hit & jnp.logical_not((at_ref[2] == WA - 1) & (col == (15 if c == 0 else 14)))
    return onehot(hit)


def middle_kernel(
    at_ref, g_ref, h_ref, w_ref, k1, k1t, kdt, pre_ref,
    gp, act, cu, spill_ref, pre, act32, fix, yb,
):
    ta, last_h, last_w = at_ref[0], at_ref[1] == HA - 1, at_ref[2] == WA - 1
    cot = 2 * F * W

    edges = w_ref[...].reshape(T * 16, C)
    m, n = iota((64, T * 16), 0), iota((64, T * 16), 1)
    t, k, e = div(m, 8), mod(div(m, 2), 4), mod(m, 2)
    total = None
    for i, (a, b, c) in enumerate(TAPS):
        if c == 0:
            continue
        hit = (n == (t - 2 + a) * 16 + (k + b) * 2 + e + (c - 2)) & (e + c >= 2)
        if b != 1:
            hit = hit & jnp.logical_not(last_h & (k == (3 if b == 0 else 2)))
        if c == 2:
            hit = hit & jnp.logical_not(last_w & (e == 0))
        y = dot(dot(onehot(hit), edges).astype(BF16), k1[i * C : (i + 1) * C])
        total = y if total is None else total + y
    fix[...] = total

    m, n = iota((144, 48), 0), iota((144, 48), 1)
    (b, c), place = third(div(m, 16)), mod(m, 16)
    kk, mm = div(place, 8), mod(place, 8)
    r, q = kk + jnp.where(b < 2, 1, 0), mm + jnp.where(c < 2, 1, 0)
    source = jnp.where(q == 8, 44 + r, r * 8 + q)
    out_h = last_h & (b == 0) & (kk == 1)
    out_w = last_w & (c == 0) & (mm == 7)
    pick = onehot((n == source) & jnp.logical_not(out_h | out_w))
    for i in range(9):
        cu[i, TA] = jnp.zeros((16, C), BF16)
    for j in range(TA):
        rows = jnp.concatenate(
            [g_ref[j, cot : cot + 16], h_ref[j, cot : cot + 16], w_ref[2 * j]], axis=0
        )
        built = dot(pick, rows).astype(BF16)
        for i in range(9):
            cu[i, j] = built[i * 16 : (i + 1) * 16]

    last = iota((8, C), 0) == 7
    for te in range(2):
        for ke in range(2):
            for ce in range(2):
                total = None
                for i, (a, b, c) in enumerate(TAPS):
                    if (a == 1, b == 1, c == 1) != (te == 1, ke == 1, ce == 1):
                        continue
                    ja = 1 if a < 2 else 0
                    y = dot(cu[b * 3 + c, ja : ja + 4].reshape(64, C), kdt[i * C : (i + 1) * C])
                    total = y if total is None else total + y
                for j in range(4):
                    for kk in range(2):
                        t, k = 2 * j + te, 2 * kk + ke
                        spot = t * 64 + k * W + ce * 8
                        late = (t * 4 + k) * 2 + ce
                        x = pre_ref[spot : spot + 8] + jnp.where(last, fix[late : late + 1], 0.0)
                        s = 1.0 / (1.0 + jnp.exp(-x))
                        at = (j * 2 + kk) * 8
                        g = total[at : at + 8]
                        act32[te * 4 + ke * 2 + ce, at : at + 8] = x * s
                        pre[spot : spot + 8] = g * s * (1.0 + x * (1.0 - s))
    gp[0:2] = jnp.zeros((2, 64, C), BF16)
    gp[2 : T + 2] = pre[...].astype(BF16).reshape(T, 64, C)
    gp[T + 2 : T + 4] = jnp.zeros((2, 64, C), BF16)
    act[...] = act32[...].astype(BF16)

    later = gp[pl.ds(2 + F * ta, F + 2)]
    pick = jnp.concatenate(
        [clip_pick(at_ref, b, c, SPILL, 8, W) for b in range(3) for c in (1, 2)], axis=0
    )
    for t in range(F + 2):
        built = dot(pick, later[t]).astype(BF16)
        for i in range(6):
            yb[i, t] = built[i * SPILL : (i + 1) * SPILL]
    total = None
    for i, (a, b, c) in enumerate(TAPS):
        if c == 0:
            continue
        x = yb[b * 2 + c - 1, 2 - a : 2 - a + F].reshape(F * SPILL, C)
        y = dot(x, k1t[i * C : (i + 1) * C])
        total = y if total is None else total + y
    spill_ref[...] = total.reshape(F, SPILL, C)


def main_kernel(
    at_ref, w_ref, xa_ref, xb_ref, edge_ref, gp, act, cu, mine_ref, other_ref, xc, tt
):
    ta, core = at_ref[0], lax.rem(at_ref[1], 2)

    share = onehot(iota((SHARE, C), 1) == iota((SHARE, C), 0) + ta * SHARE)
    left = jnp.concatenate(
        [
            dot_t(share, gp[2 - a : 2 - a + T + 2].reshape((T + 2) * 64, C)).astype(BF16)
            for a in range(3)
        ],
        axis=0,
    )
    late = edge_ref[...].reshape(6 * 64, 16)
    windows = [xa_ref.at[i] if i < 3 else xb_ref.at[i - 3] for i in range(9)]
    for i in range(6):
        xc[i, 0:2] = jnp.zeros((2, 64, C), BF16)
    for t in range(T):
        built = dot(late, w_ref[t]).astype(BF16)
        for i in range(6):
            base = windows[i // 2 * 3 + i % 2 + 1]
            xc[i, t + 2] = base[t + 2] + built[i * 64 : (i + 1) * 64]
    upper, lower = {}, {}
    for bc in range(9):
        x = windows[bc] if bc % 3 == 0 else xc.at[bc // 3 * 2 + bc % 3 - 1]
        y = dot(left, x[...].reshape((T + 2) * 64, C))
        for a in range(3):
            upper[a * 9 + bc] = y[a * SHARE : (a + 1) * SHARE]
    cots = {}
    for bc in range(9):
        for ja in range(2):
            cots[bc, ja] = dot_t(share, cu[bc, ja : ja + 4].reshape(64, C)).astype(BF16)
    for kind in range(8):
        taps = [
            (i, cots[b * 3 + c, 1 if a < 2 else 0])
            for i, (a, b, c) in enumerate(TAPS)
            if (a == 1) * 4 + (b == 1) * 2 + (c == 1) == kind
        ]
        y = dot(jnp.concatenate([x for _, x in taps], axis=0), act[kind])
        for place, (i, _) in enumerate(taps):
            lower[i] = y[place * SHARE : (place + 1) * SHARE]
    for i in range(27):
        tt[i * C : (i + 1) * C] = jnp.concatenate([upper[i], lower[i]], axis=0).T
    tt[27 * C :] = jnp.zeros((8, 2 * SHARE), F32)

    for x in range(HA // 2):
        for w in range(WA):
            pair = []
            for cc in range(2):
                first = ((x * 2 + cc) * WA + w) * PART
                y = tt[first : first + SLOT]
                pair.append(y)
            spot = (x * WA + w) * SLOT
            mine_ref[spot : spot + SLOT] = jnp.where(core == 0, pair[0], pair[1]).astype(BF16)
            other_ref[spot : spot + SLOT] = jnp.where(core == 0, pair[1], pair[0]).astype(BF16)


WIDE = 96


def clip_kernel(at_ref, gp, k1t, own_ref, past_ref, yb, acc):
    later = gp[pl.ds(2 + F * at_ref[0], F + 2)]
    pick = jnp.concatenate([clip_pick(at_ref, i // 3, i % 3, WIDE, W, 0) for i in range(9)], axis=0)
    for t in range(F + 2):
        built = dot(pick, later[t]).astype(BF16)
        for i in range(9):
            yb[i, t] = built[i * WIDE : (i + 1) * WIDE]
    for i, (a, b, c) in enumerate(TAPS):
        y = dot(yb[b * 3 + c, 2 - a : 2 - a + F].reshape(F * WIDE, C), k1t[i * C : (i + 1) * C])
        if i == 0:
            acc[...] = y
        else:
            acc[...] += y
    for f in range(F):
        own_ref[f] = acc[f * WIDE : f * WIDE + R * W]
        past_ref[f] = acc[f * WIDE + R * W : (f + 1) * WIDE]


def seam_kernel(past_ref, spill_ref, out_ref):
    for f in range(F):
        for h in range(2):
            at, spot = h * W, (R + h) * 8
            out_ref[f, at : at + 8] = past_ref[f, at : at + 8] + spill_ref[f, spot : spot + 8]
            out_ref[f, at + 8 : at + W] = past_ref[f, at + 8 : at + W]


STAGES = 4


def join_kernel(mine_ref, other_ref, after_ref, out_ref, joined, sems):
    rows = PEERS * SLOT // STAGES
    copies = []
    for i in range(STAGES):
        part = pl.ds(i * rows, rows)
        joined[part] = mine_ref[part] + other_ref[part]
        copies.append(pltpu.make_async_copy(joined.at[part], out_ref.at[part], sems.at[i]))
        copies[-1].start()
    for copy in copies:
        copy.wait()


def finish_kernel(parts_ref, own_ref, spill_ref, past_ref, clip_ref, conv_ref, down_ref):
    for f in range(F):
        for h in range(R):
            at = h * W
            low = own_ref[f, at : at + 8] + spill_ref[f, h * 8 : h * 8 + 8]
            x = jnp.concatenate([low, own_ref[f, at + 8 : at + W]], axis=0)
            if h < 2:
                x += past_ref[f, at : at + W]
            clip_ref[f, at : at + W] = x.astype(BF16)
    total = parts_ref[0].astype(F32)
    for i in range(1, PEERS):
        total += parts_ref[i].astype(F32)
    total = jnp.concatenate([total, jnp.zeros((128 - SLOT, 2 * SHARE), F32)], axis=0).T
    conv_ref[...] = total[:SHARE, :PART]
    down_ref[...] = total[SHARE:, :PART]


def whole():
    return pl.BlockSpec(memory_space=pltpu.VMEM)


def call(kernel, outs, specs, scratch, flops, name, out=None):
    return pl.pallas_call(
        kernel,
        out_shape=outs,
        in_specs=specs,
        out_specs=jax.tree.map(lambda _: out or whole(), outs),
        scratch_shapes=scratch,
        compiler_params=pltpu.CompilerParams(vmem_limit_bytes=VMEM_BYTES),
        cost_estimate=pl.CostEstimate(flops=flops, bytes_accessed=8_000_000, transcendentals=0),
        name=name,
    )


def shape(dims, dtype=BF16):
    return jax.ShapeDtypeStruct(dims, dtype)


def on_chip(dims, dtype=BF16):
    return pltpu.VMEM(dims, dtype)


def in_hbm(x):
    return pltpu.with_memory_space_constraint(x, pltpu.HBM)


def in_vmem(x):
    return pltpu.with_memory_space_constraint(x, pltpu.VMEM)


def shift(x, axis, by):
    count = lax.axis_size(axis)
    return lax.ppermute(x, axis, [(i, (i + by) % count) for i in range(count)])


def local(clip, conv_weight, down_weight, out_cotangent):
    smem, anywhere = pl.BlockSpec(memory_space=pltpu.SMEM), pl.BlockSpec(memory_space=pl.ANY)
    at = jnp.stack([lax.axis_index(a) for a in ("ta", "ha", "wa")]).astype(jnp.int32)
    dma = pltpu.SemaphoreType.DMA
    packed = call(
        pack_kernel, shape((BLOCK, C)), [anywhere] * 2, [dma((9,))], 10**5, "pack"
    )(in_hbm(clip), in_hbm(out_cotangent.reshape(-1, C)))
    around = [shift(packed, "ta", by) for by in (1, 2, 3)]
    weight = on_chip((27 * C, C))
    k1, k1t = call(
        load_kernel,
        [weight] * 2,
        [smem] + [anywhere] * 2,
        [dma((9,))],
        2 * 10**9,
        "load",
    )(at, packed, in_hbm(conv_weight))
    k1, k1t = in_vmem(k1), in_vmem(k1t)
    head = call(
        head_kernel,
        shape((TA, HEAD, C)),
        [smem] + [whole()] * 4 + [anywhere],
        [],
        10**5,
        "head",
    )(at, packed, *around, k1t)
    h = shift(head, "ha", -1)
    g, xa, pre, kdt = call(
        own_kernel,
        [shape((TA, BLOCK, C)), on_chip((3, T + 2, 64, C)), on_chip((T * 64, C), F32), weight],
        [smem] + [whole()] * 4 + [anywhere, whole(), anywhere],
        [pltpu.VMEM((27 * C, C), BF16), dma((9,))],
        3 * 10**9,
        "own",
    )(at, packed, *around, head, k1, in_hbm(down_weight))
    xa, pre, kdt = in_vmem(xa), in_vmem(pre), in_vmem(kdt)
    w = call(edge_kernel, shape((T, 16, C)), [whole()] * 2, [], 10**7, "edge")(g, h)
    w = shift(w, "wa", -1)
    xb, pre, edge = call(
        early_kernel,
        [on_chip((6, T + 2, 64, C)), on_chip((T * 64, C), F32), on_chip((3, 128, 16))],
        [smem] + [whole()] * 4,
        [],
        3 * 10**9,
        "early",
    )(at, g, h, k1, pre)
    xb, pre, edge = in_vmem(xb), in_vmem(pre), in_vmem(edge)
    gp, act, cu, spill = call(
        middle_kernel,
        [
            on_chip((T + 4, 64, C)),
            on_chip((8, 64, C)),
            on_chip((9, TA + 1, 16, C)),
            shape((F, SPILL, C), F32),
        ],
        [smem] + [whole()] * 7,
        [
            pltpu.VMEM((T * 64, C), F32),
            pltpu.VMEM((8, 64, C), F32),
            pltpu.VMEM((64, C), F32),
            pltpu.VMEM((6, F + 2, SPILL, C), BF16),
        ],
        3 * 10**9,
        "middle",
    )(at, g, h, w, k1, k1t, kdt, pre)
    gp, act, cu = in_vmem(gp), in_vmem(act), in_vmem(cu)
    spill = shift(spill, "wa", 1)
    mine, other = call(
        main_kernel,
        [shape((PEERS * SLOT, 2 * SHARE)), shape((PEERS * SLOT, 2 * SHARE))],
        [smem] + [whole()] * 7,
        [pltpu.VMEM((6, T + 2, 64, C), BF16), pltpu.VMEM((27 * C + 8, 2 * SHARE), F32)],
        5 * 10**9,
        "main",
    )(at, w, xa, xb, edge, gp, act, cu)
    other = lax.ppermute(other, "ha", [(i, i ^ 1) for i in range(HA)])
    own, past = call(
        clip_kernel,
        [shape((F, R * W, C), F32), shape((F, 2 * W, C), F32)],
        [smem] + [whole()] * 2,
        [pltpu.VMEM((9, F + 2, WIDE, C), BF16), pltpu.VMEM((F * WIDE, C), F32)],
        10**9,
        "clip",
    )(at, gp, k1t)
    pair = call(
        join_kernel,
        shape((PEERS * SLOT, 2 * SHARE)),
        [whole(), whole(), anywhere],
        [pltpu.VMEM((PEERS * SLOT, 2 * SHARE), BF16), dma((STAGES,))],
        10**6,
        "join",
        anywhere,
    )(mine, other, own)
    pair, spill = lax.optimization_barrier((pair, spill))
    past = call(
        seam_kernel, shape((F, 2 * W, C), F32), [whole()] * 2, [], 10**5, "seam"
    )(past, spill)
    past = shift(past, "ha", 1)
    groups = [[i * WA + w for i in range(c, HA, 2) for w in range(WA)] for c in range(2)]
    parts = lax.all_to_all(pair, ("ha", "wa"), 0, 0, axis_index_groups=groups, tiled=True)
    grad_clip, grad_conv, grad_down = call(
        finish_kernel,
        [shape((F, R * W, C)), shape((SHARE, PART), F32), shape((SHARE, PART), F32)],
        [whole()] * 4,
        [],
        10**6,
        "finish",
    )(parts.reshape(PEERS, SLOT, 2 * SHARE), own, spill, past)
    grad_clip = grad_clip.reshape(F, R, W, C)
    return (grad_clip, grad_conv.T, grad_down.T)


def solution(mesh):
    return jax.shard_map(
        local,
        mesh=mesh,
        in_specs=(P("ta", "ha", "wa", None), P(), P(), P("ta", "ha", "wa", None)),
        out_specs=(P("ta", "ha", "wa", None), P(("ha", "wa"), "ta"), P(("ha", "wa"), "ta")),
        check_vma=False,
    )
```

time: 70.9 us -> 64.9 us (0.915)
  blocking collectives: 16.5 us -> 0 us
  starting transfers between devices: 16.8 us -> 23.4 us
  waiting for transfers between devices: 16.4 us -> 19 us
  Pallas kernels: 19.4 us -> 21.4 us
    all_gather x1 -> x0, blocking collectives: 16.5 us -> none  [local(): g = lax.all_gather(packed, 'ta', axis=0, tiled=False)]
    ppermute x4 -> x7, starting transfers between devices: 10.3 us -> 16.5 us  [shift(): return lax.ppermute(x, axis, [(i, (i + by) % count) for i in range(count)])]
    all_to_all x1, waiting for transfers between devices: 0.01 us -> 5.33 us  [local(): lax.all_to_all(pair, ('ha', 'wa'), 0, 0, axis_index_groups=groups, tiled=...]
    pallas_call x4 -> x8, Pallas kernels: 11 us -> 16 us  [the longest x1 3.35 us: local(): call(middle_kernel, [on_chip((T + 4, 64, C)), on_chip((8, 64, C)), on_chi...]
    pallas_call x1, Pallas kernels: 6.2 us -> 3.37 us  [local(): call(main_kernel, [shape((PEERS * SLOT, 2 * SHARE)), shape((PEERS * SLOT,...]
    ppermute x4 -> x7, waiting for transfers between devices: 16.4 us -> 13.6 us  [shift(): return lax.ppermute(x, axis, [(i, (i + by) % count) for i in range(count)])]
    ppermute x1, starting transfers between devices: 0.09 us -> 1.67 us  [local(): other = lax.ppermute(other, 'ha', [(i, i ^ 1) for i in range(HA)])]
    all_to_all x1, starting transfers between devices: 6.4 us -> 5.2 us  [local(): lax.all_to_all(pair, ('ha', 'wa'), 0, 0, axis_index_groups=groups, tiled=...]
  transfers between devices with their start and end apart: 6 -> 9, of which waited for: 3 -> 5; matrix products, arithmetic and copies ran while one was open for 1% -> 0% of each run, Pallas kernels for 14% -> 19%
where the time goes in v4:
time: 64.9 us; the launch traced here: 64.6 us
  starting transfers between devices  23.4 us (36%)
  Pallas kernels  21.4 us (33%)
  waiting for transfers between devices  19 us (29%)
  between operations  0.76 us (1%)
    ppermute x7, starting transfers between devices, shift(): return lax.ppermute(x, axis, [(i, (i + by) % count) for i in range(count)])  16.5 us
    ppermute x7, waiting for transfers between devices, shift(): return lax.ppermute(x, axis, [(i, (i + by) % count) for i in range(count)])  13.6 us
    all_to_all x1, waiting for transfers between devices, local(): lax.all_to_all(pair, ('ha', 'wa'), 0, 0, axis_index_groups=groups, tiled=...  5.33 us
    all_to_all x1, starting transfers between devices, local(): lax.all_to_all(pair, ('ha', 'wa'), 0, 0, axis_index_groups=groups, tiled=...  5.2 us
    pallas_call x1, Pallas kernels, local(): call(main_kernel, [shape((PEERS * SLOT, 2 * SHARE)), shape((PEERS * SLOT,...  3.37 us
    pallas_call x1, Pallas kernels, local(): call(middle_kernel, [on_chip((T + 4, 64, C)), on_chip((8, 64, C)), on_chi...  3.35 us
    pallas_call x1, Pallas kernels, local(): call(own_kernel, [shape((TA, BLOCK, C)), on_chip((3, T + 2, 64, C)), on_c...  3.14 us
    pallas_call x1, Pallas kernels, local(): call(load_kernel, [weight] * 2, [smem] + [anywhere] * 2, [dma((9,))], 2 *...  3.03 us
  transfers between devices with their start and end apart: 9, of which 5 were waited for; matrix products, arithmetic and copies ran while one was open for 0% of the time, Pallas kernels for 19%

profile of v4, /device:TPU:1, one launch (start us, length us, event | category | flops | bytes accessed | tf_op | source)
XLA Modules:
  0.0 64.6 jit_solution(1787381500450805201)
XLA Ops:
  0.6 0.9 %pack.1.after_ref.own_ref = bf16[144,256]{1,0:T(8,128)(2,1)S(1)} custom-call(bf16[2,4,16,256]{3,2,1,0:T(8,128)(2,1)} %clip_ref.1, bf16[16,256]{1,0:T(8,128)(2,1)} %bitcast.8), custom_call_target="tpu_custom_call" | custom-call | flops 100000 | bytes 8000000 | tf_op jit(solution)/shard_map/pack/pallas_call | solution.py:440
  1.5 3.9 %collective-permute-start = (bf16[144,256]{1,0:T(8,128)(2,1)S(1)}, bf16[144,256]{1,0:T(8,128)(2,1)S(1)}, u32[]{:S(2)}, u32[]{:S(2)}) collective-permute-start(bf16[144,256]{1,0:T(8,128)(2,1)S(1)} %pack.1.after_ref.own_ref), channel_id=1, source_target_pairs={{0,64},{64,128},{128,192},{192,0},{1,65},{65,129},{129,193},{193,1... | collective-permute-start | bytes 221192 | tf_op jit(solution)/shard_map/ppermute | solution.py:433
  5.4 5.1 %collective-permute-start.1 = (bf16[144,256]{1,0:T(8,128)(2,1)S(1)}, bf16[144,256]{1,0:T(8,128)(2,1)S(1)}, u32[]{:S(2)}, u32[]{:S(2)}) collective-permute-start(bf16[144,256]{1,0:T(8,128)(2,1)S(1)} %pack.1.after_ref.own_ref), channel_id=1, source_target_pairs={{0,128},{64,192},{128,0},{192,64},{1,129},{65,193},{129,1},{193,65... | collective-permute-start | bytes 221192 | tf_op jit(solution)/shard_map/ppermute | solution.py:433
  10.6 2.4 %collective-permute-start.2 = (bf16[144,256]{1,0:T(8,128)(2,1)S(1)}, bf16[144,256]{1,0:T(8,128)(2,1)S(1)}, u32[]{:S(2)}, u32[]{:S(2)}) collective-permute-start(bf16[144,256]{1,0:T(8,128)(2,1)S(1)} %pack.1.after_ref.own_ref), channel_id=1, source_target_pairs={{0,192},{64,0},{128,64},{192,128},{1,193},{65,1},{129,65},{193,129... | collective-permute-start | bytes 221192 | tf_op jit(solution)/shard_map/ppermute | solution.py:433
  12.9 0.1 pad_add_fusion.at_ref
  13.0 3.0 %load.1 = (bf16[6912,256]{1,0:T(8,128)(2,1)S(1)}, bf16[6912,256]{1,0:T(8,128)(2,1)S(1)}) custom-call(s32[3]{0:T(128)S(1)} %pad_add_fusion.at_ref, bf16[144,256]{1,0:T(8,128)(2,1)S(1)} %pack.1.after_ref.own_ref, bf16[6912,256]{1,0:T(8,128)(2,1)} %k1_ref.1), custom_call_target="tpu_custom_call" | custom-call | flops 2000000000 | bytes 8000000 | tf_op jit(solution)/shard_map/load/pallas_call | solution.py:445
  16.1 0.0 collective-permute-done.one_ref
  16.1 0.0 collective-permute-done.1.two_ref
  16.1 2.8 %collective-permute-done.2.three_ref = bf16[144,256]{1,0:T(8,128)(2,1)S(1)} collective-permute-done((bf16[144,256]{1,0:T(8,128)(2,1)S(1)}, bf16[144,256]{1,0:T(8,128)(2,1)S(1)}, u32[]{:S(2)}, u32[]{:S(2)}) %collective-permute-start.2) | collective-permute-done | bytes 73760 | tf_op jit(solution)/shard_map/ppermute | solution.py:433
  18.8 0.6 head.1.after_ref
  19.4 0.5 collective-permute-start.3
  19.9 3.1 %own.1 = (bf16[4,144,256]{2,1,0:T(8,128)(2,1)S(1)}, bf16[3,10,64,256]{3,2,1,0:T(8,128)(2,1)S(1)}, f32[512,256]{1,0:T(8,128)S(1)}, bf16[6912,256]{1,0:T(8,128)(2,1)S(1)}) custom-call(s32[3]{0:T(128)S(1)} %pad_add_fusion.at_ref, bf16[144,256]{1,0:T(8,128)(2,1)S(1)} %pack.1.after_ref.own_ref, bf16[144,256]{1,0:T(8,128)(2,1)S(1)} %collective-permute-done.one_ref, ...), custom_call_target="tpu_custom_call" | custom-call | flops 3000000000 | bytes 8000000 | tf_op jit(solution)/shard_map/own/pallas_call | solution.py:463
  23.1 1.1 %collective-permute-done.3.h_ref = bf16[4,80,256]{2,1,0:T(8,128)(2,1)S(1)} collective-permute-done((bf16[4,80,256]{2,1,0:T(8,128)(2,1)S(1)}, bf16[4,80,256]{2,1,0:T(8,128)(2,1)S(1)}, u32[]{:S(2)}, u32[]{:S(2)}) %collective-permute-start.3) | collective-permute-done | bytes 163872 | tf_op jit(solution)/shard_map/ppermute | solution.py:433
  24.2 0.2 edge.1
  24.3 1.7 %collective-permute-start.4 = (bf16[8,16,256]{2,1,0:T(8,128)(2,1)S(1)}, bf16[8,16,256]{2,1,0:T(8,128)(2,1)S(1)}, u32[]{:S(2)}, u32[]{:S(2)}) collective-permute-start(bf16[8,16,256]{2,1,0:T(8,128)(2,1)S(1)} %edge.1), channel_id=1, source_target_pairs={{0,7},{1,0},{2,1},{3,2},{4,3},{5,4},{6,5},{7,6},{8,15},{9,8},{10,9... | collective-permute-start | bytes 196616 | tf_op jit(solution)/shard_map/ppermute | solution.py:433
  26.0 2.4 %early.1 = (bf16[6,10,64,256]{3,2,1,0:T(8,128)(2,1)S(1)}, f32[512,256]{1,0:T(8,128)S(1)}, bf16[3,128,16]{2,1,0:T(8,128)(2,1)S(1)}) custom-call(s32[3]{0:T(128)S(1)} %pad_add_fusion.at_ref, bf16[4,144,256]{2,1,0:T(8,128)(2,1)S(1)} %get-tuple-element.27.g_ref, bf16[4,80,256]{2,1,0:T(8,128)(2,1)S(1)} %collective-permute-done.3.h_ref, ...), custom_call_target="tpu_custom_call" | custom-call | flops 3000000000 | bytes 8000000 | tf_op jit(solution)/shard_map/early/pallas_call | solution.py:474
  28.4 0.0 collective-permute-done.4.w_ref
  28.4 3.4 %middle.1 = (bf16[12,64,256]{2,1,0:T(8,128)(2,1)S(1)}, bf16[8,64,256]{2,1,0:T(8,128)(2,1)S(1)}, bf16[9,5,16,256]{3,2,1,0:T(8,128)(2,1)S(1)}, f32[2,48,256]{2,1,0:T(8,128)S(1)}) custom-call(s32[3]{0:T(128)S(1)} %pad_add_fusion.at_ref, bf16[4,144,256]{2,1,0:T(8,128)(2,1)S(1)} %get-tuple-element.27.g_ref, bf16[4,80,256]{2,1,0:T(8,128)(2,1)S(1)} %collective-permute-done.3.h_ref, ...), custom_call_target="tpu_custom_call" | custom-call | flops 3000000000 | bytes 8000000 | tf_op jit(solution)/shard_map/middle/pallas_call | solution.py:483
  31.7 3.4 %main.1 = (bf16[3584,128]{1,0:T(8,128)(2,1)S(1)}, bf16[3584,128]{1,0:T(8,128)(2,1)S(1)}) custom-call(s32[3]{0:T(128)S(1)} %pad_add_fusion.at_ref, bf16[8,16,256]{2,1,0:T(8,128)(2,1)S(1)} %collective-permute-done.4.w_ref, bf16[3,10,64,256]{3,2,1,0:T(8,128)(2,1)S(1)} %get-tuple-element.28.xa_ref, bf16[6,10,64,256]{3,2,1,0:T(8,128)(2,1)S(1)} %get-tuple-element.30.xb_ref, ...), custom_call_target="tpu_custom_call" | custom-call | flops 5000000000 | bytes 8000000 | tf_op jit(solution)/shard_map/main/pallas_call | solution.py:503
  35.1 1.7 %collective-permute-start.5 = (bf16[3584,128]{1,0:T(8,128)(2,1)S(1)}, bf16[3584,128]{1,0:T(8,128)(2,1)S(1)}, u32[]{:S(2)}, u32[]{:S(2)}) collective-permute-start(bf16[3584,128]{1,0:T(8,128)(2,1)S(1)} %get-tuple-element.38), channel_id=1, source_target_pairs={{0,8},{8,0},{16,24},{24,16},{32,40},{40,32},{48,56},{56,48},{1,9},... | collective-permute-start | bytes 2752520 | tf_op jit(solution)/shard_map/ppermute | solution.py:511
  36.8 0.7 %collective-permute-start.6 = (f32[2,48,256]{2,1,0:T(8,128)S(1)}, f32[2,48,256]{2,1,0:T(8,128)S(1)}, u32[]{:S(2)}, u32[]{:S(2)}) collective-permute-start(f32[2,48,256]{2,1,0:T(8,128)S(1)} %get-tuple-element.40), channel_id=1, source_target_pairs={{0,1},{1,2},{2,3},{3,4},{4,5},{5,6},{6,7},{7,0},{8,9},{9,10},{10,1... | collective-permute-start | bytes 294920 | tf_op jit(solution)/shard_map/ppermute | solution.py:433
  37.5 2.7 %clip.1 = (f32[2,64,256]{2,1,0:T(8,128)S(1)}, f32[2,32,256]{2,1,0:T(8,128)S(1)}) custom-call(s32[3]{0:T(128)S(1)} %pad_add_fusion.at_ref, bf16[12,64,256]{2,1,0:T(8,128)(2,1)S(1)} %get-tuple-element.34.gp, bf16[6912,256]{1,0:T(8,128)(2,1)S(1)} %get-tuple-element.25.after_ref.k1t), custom_call_target="tpu_custom_call" | custom-call | flops 1000000000 | bytes 8000000 | tf_op jit(solution)/shard_map/clip/pallas_call | solution.py:512
  40.2 0.0 collective-permute-done.5.other_ref
  40.2 1.0 %join.1 = bf16[3584,128]{1,0:T(8,128)(2,1)} custom-call(bf16[3584,128]{1,0:T(8,128)(2,1)S(1)} %get-tuple-element.37.mine_ref, bf16[3584,128]{1,0:T(8,128)(2,1)S(1)} %collective-permute-done.5.other_ref, f32[2,64,256]{2,1,0:T(8,128)S(1)} %get-tuple-element.39.after_ref.own_ref), custom_call_target="tpu_custom_call" | custom-call | flops 1000000 | bytes 8000000 | tf_op jit(solution)/shard_map/join/pallas_call | solution.py:520
  41.3 1.8 %collective-permute-done.6.spill_ref = f32[2,48,256]{2,1,0:T(8,128)S(1)} collective-permute-done((f32[2,48,256]{2,1,0:T(8,128)S(1)}, f32[2,48,256]{2,1,0:T(8,128)S(1)}, u32[]{:S(2)}, u32[]{:S(2)}) %collective-permute-start.6) | collective-permute-done | bytes 98336 | tf_op jit(solution)/shard_map/ppermute | solution.py:433
  43.1 5.2 %all-to-all-start = ((bf16[32,112,128]{2,1,0:T(8,128)(2,1)}), bf16[32,112,128]{2,1,0:T(8,128)(2,1)S(1)}, u32[]{:S(2)}, u32[]{:S(2)}) async-start(bf16[32,112,128]{2,1,0:T(8,128)(2,1)} %bitcast.4), calls=%async_computation | async-start | bytes 1835008 | tf_op jit(solution)/shard_map/all_to_all | solution.py:535
  48.3 2.2 %collective-permute-start.7 = (f32[2,32,256]{2,1,0:T(8,128)S(1)}, f32[2,32,256]{2,1,0:T(8,128)S(1)}, u32[]{:S(2)}, u32[]{:S(2)}) collective-permute-start(f32[2,32,256]{2,1,0:T(8,128)S(1)} %seam.1), channel_id=1, source_target_pairs={{0,8},{8,16},{16,24},{24,32},{32,40},{40,48},{48,56},{56,0},{1,9},... | collective-permute-start | bytes 196616 | tf_op jit(solution)/shard_map/ppermute | solution.py:433
  50.5 7.9 %collective-permute-done.7.past_ref = f32[2,32,256]{2,1,0:T(8,128)S(1)} collective-permute-done((f32[2,32,256]{2,1,0:T(8,128)S(1)}, f32[2,32,256]{2,1,0:T(8,128)S(1)}, u32[]{:S(2)}, u32[]{:S(2)}) %collective-permute-start.7) | collective-permute-done | bytes 65568 | tf_op jit(solution)/shard_map/ppermute | solution.py:433
  58.4 5.3 %all-to-all-done.parts_ref = bf16[32,112,128]{2,1,0:T(8,128)(2,1)S(1)} async-done(((bf16[32,112,128]{2,1,0:T(8,128)(2,1)}), bf16[32,112,128]{2,1,0:T(8,128)(2,1)S(1)}, u32[]{:S(2)}, u32[]{:S(2)}) %all-to-all-start) | async-done | bytes 917536 | tf_op jit(solution)/shard_map/all_to_all | solution.py:535
  63.8 0.8 %finish.1 = (bf16[2,64,256]{2,1,0:T(8,128)(2,1)}, f32[64,108]{1,0:T(8,128)}, f32[64,108]{1,0:T(8,128)}) custom-call(bf16[32,112,128]{2,1,0:T(8,128)(2,1)S(1)} %all-to-all-done.parts_ref, f32[2,64,256]{2,1,0:T(8,128)S(1)} %get-tuple-element.39.after_ref.own_ref, f32[2,48,256]{2,1,0:T(8,128)S(1)} %collective-permute-done.6.spill_ref, ...), custom_call_target="tpu_custom_call" | custom-call | flops 1000000 | bytes 8000000 | tf_op jit(solution)/shard_map/finish/pallas_call | solution.py:536
  (1 shorter events, 0.0 us)
Async XLA Ops:
  1.5 14.5 %collective-permute-start = (bf16[144,256]{1,0:T(8,128)(2,1)S(1)}, bf16[144,256]{1,0:T(8,128)(2,1)S(1)}, u32[]{:S(2)}, u32[]{:S(2)}) collective-permute-start(bf16[144,256]{1,0:T(8,128)(2,1)S(1)} %pack.1.after_ref.own_ref), channel_id=1, source_target_pairs={{0,64},{64,128},{128,192},{192,0},{1,65},{65,129},{129,193},{193,1... | collective-permute-start | bytes 221192 | tf_op jit(solution)/shard_map/ppermute | solution.py:433
  5.4 10.6 %collective-permute-start.1 = (bf16[144,256]{1,0:T(8,128)(2,1)S(1)}, bf16[144,256]{1,0:T(8,128)(2,1)S(1)}, u32[]{:S(2)}, u32[]{:S(2)}) collective-permute-start(bf16[144,256]{1,0:T(8,128)(2,1)S(1)} %pack.1.after_ref.own_ref), channel_id=1, source_target_pairs={{0,128},{64,192},{128,0},{192,64},{1,129},{65,193},{129,1},{193,65... | collective-permute-start | bytes 221192 | tf_op jit(solution)/shard_map/ppermute | solution.py:433
  10.6 8.3 %collective-permute-start.2 = (bf16[144,256]{1,0:T(8,128)(2,1)S(1)}, bf16[144,256]{1,0:T(8,128)(2,1)S(1)}, u32[]{:S(2)}, u32[]{:S(2)}) collective-permute-start(bf16[144,256]{1,0:T(8,128)(2,1)S(1)} %pack.1.after_ref.own_ref), channel_id=1, source_target_pairs={{0,192},{64,0},{128,64},{192,128},{1,193},{65,1},{129,65},{193,129... | collective-permute-start | bytes 221192 | tf_op jit(solution)/shard_map/ppermute | solution.py:433
  19.4 4.8 %collective-permute-start.3 = (bf16[4,80,256]{2,1,0:T(8,128)(2,1)S(1)}, bf16[4,80,256]{2,1,0:T(8,128)(2,1)S(1)}, u32[]{:S(2)}, u32[]{:S(2)}) collective-permute-start(bf16[4,80,256]{2,1,0:T(8,128)(2,1)S(1)} %head.1.after_ref), channel_id=1, source_target_pairs={{0,56},{8,0},{16,8},{24,16},{32,24},{40,32},{48,40},{56,48},{1,57}... | collective-permute-start | bytes 491528 | tf_op jit(solution)/shard_map/ppermute | solution.py:433
  24.3 4.0 %collective-permute-start.4 = (bf16[8,16,256]{2,1,0:T(8,128)(2,1)S(1)}, bf16[8,16,256]{2,1,0:T(8,128)(2,1)S(1)}, u32[]{:S(2)}, u32[]{:S(2)}) collective-permute-start(bf16[8,16,256]{2,1,0:T(8,128)(2,1)S(1)} %edge.1), channel_id=1, source_target_pairs={{0,7},{1,0},{2,1},{3,2},{4,3},{5,4},{6,5},{7,6},{8,15},{9,8},{10,9... | collective-permute-start | bytes 196616 | tf_op jit(solution)/shard_map/ppermute | solution.py:433
  35.1 5.1 %collective-permute-start.5 = (bf16[3584,128]{1,0:T(8,128)(2,1)S(1)}, bf16[3584,128]{1,0:T(8,128)(2,1)S(1)}, u32[]{:S(2)}, u32[]{:S(2)}) collective-permute-start(bf16[3584,128]{1,0:T(8,128)(2,1)S(1)} %get-tuple-element.38), channel_id=1, source_target_pairs={{0,8},{8,0},{16,24},{24,16},{32,40},{40,32},{48,56},{56,48},{1,9},... | collective-permute-start | bytes 2752520 | tf_op jit(solution)/shard_map/ppermute | solution.py:511
  36.8 6.3 %collective-permute-start.6 = (f32[2,48,256]{2,1,0:T(8,128)S(1)}, f32[2,48,256]{2,1,0:T(8,128)S(1)}, u32[]{:S(2)}, u32[]{:S(2)}) collective-permute-start(f32[2,48,256]{2,1,0:T(8,128)S(1)} %get-tuple-element.40), channel_id=1, source_target_pairs={{0,1},{1,2},{2,3},{3,4},{4,5},{5,6},{6,7},{7,0},{8,9},{9,10},{10,1... | collective-permute-start | bytes 294920 | tf_op jit(solution)/shard_map/ppermute | solution.py:433
  43.1 20.7 %all-to-all-start = ((bf16[32,112,128]{2,1,0:T(8,128)(2,1)}), bf16[32,112,128]{2,1,0:T(8,128)(2,1)S(1)}, u32[]{:S(2)}, u32[]{:S(2)}) async-start(bf16[32,112,128]{2,1,0:T(8,128)(2,1)} %bitcast.4), calls=%async_computation | async-start | bytes 1835008 | tf_op jit(solution)/shard_map/all_to_all | solution.py:535
  48.3 10.2 %collective-permute-start.7 = (f32[2,32,256]{2,1,0:T(8,128)S(1)}, f32[2,32,256]{2,1,0:T(8,128)S(1)}, u32[]{:S(2)}, u32[]{:S(2)}) collective-permute-start(f32[2,32,256]{2,1,0:T(8,128)S(1)} %seam.1), channel_id=1, source_target_pairs={{0,8},{8,16},{16,24},{24,32},{32,40},{40,48},{48,56},{56,0},{1,9},... | collective-permute-start | bytes 196616 | tf_op jit(solution)/shard_map/ppermute | solution.py:433

commit v5 on v4

--- a/solution.py
+++ b/solution.py
@@ -78,9 +78,8 @@
     copies = []
     for f in range(F):
         for part in range(2):
-            for k in range(2):
-                spot = part * HEAD + f * half + k * W
-                copies.append((clip_ref.at[f, 2 * part + k], out_ref.at[pl.ds(spot, W)]))
+            spot = part * HEAD + f * half
+            copies.append((clip_ref.at[2 * f + part], out_ref.at[pl.ds(spot, half)]))
     copies.append((cot_ref, out_ref.at[pl.ds(2 * F * W, 16)]))
     copies = [pltpu.make_async_copy(x, y, sems.at[i]) for i, (x, y) in enumerate(copies)]
     for copy in copies:
@@ -89,9 +88,9 @@
         copy.wait()
 
 
-def head_kernel(at_ref, own_ref, one_ref, two_ref, three_ref, after_ref, head_ref):
+def head_kernel(own_ref, one_ref, two_ref, three_ref, after_ref, head_ref):
     for back, ref in enumerate((own_ref, one_ref, two_ref, three_ref)):
-        head_ref[lax.rem(at_ref[0] + TA - back, TA)] = ref[:HEAD]
+        head_ref[lax.rem(lax.axis_index("ta") + TA - back, TA)] = ref[:HEAD]
 
 
 def fetch(source, target, sems):
@@ -113,12 +112,14 @@
         turned[i * C : (i + 1) * C] = plain[i * C : (i + 1) * C].T
 
 
-def load_kernel(at_ref, after_ref, k1_ref, k1, k1t, sems):
-    turn(fetch(k1_ref, k1, sems), k1, k1t)
-
-
-def window_pick(at_ref, b):
-    last_h, last_w = at_ref[1] == HA - 1, at_ref[2] == WA - 1
+def load_kernel(after_ref, k1_ref, kd_ref, k1, k1t, kdt, kd, sems1, semsd):
+    first, second = fetch(k1_ref, k1, sems1), fetch(kd_ref, kd, semsd)
+    turn(first, k1, k1t)
+    turn(second, kd, kdt)
+
+
+def window_pick(b):
+    last_h, last_w = lax.axis_index("ha") == HA - 1, lax.axis_index("wa") == WA - 1
     m, n = iota((192, 112), 0), iota((192, 112), 1)
     c, place = div(m, 64), mod(m, 64)
     k, col = div(place, W), column(mod(place, W))
@@ -143,12 +144,11 @@
 
 
 def own_kernel(
-    at_ref, own_ref, one_ref, two_ref, three_ref, after_ref, k1, kd_ref, g_ref, xb, pre, kdt, kd, sems
+    own_ref, one_ref, two_ref, three_ref, after_ref, k1, g_ref, xb, pre
 ):
-    copies = fetch(kd_ref, kd, sems)
     for back, ref in enumerate((own_ref, one_ref, two_ref, three_ref)):
-        g_ref[lax.rem(at_ref[0] + TA - back, TA)] = ref[...]
-    pick = window_pick(at_ref, 0)[:, :64]
+        g_ref[lax.rem(lax.axis_index("ta") + TA - back, TA)] = ref[...]
+    pick = window_pick(0)[:, :64]
     for c in range(3):
         xb[c, 0:2] = jnp.zeros((2, 64, C), BF16)
     for t in range(T):
@@ -158,11 +158,10 @@
         for c in range(3):
             xb[c, t + 2] = built[c * 64 : (c + 1) * 64]
     add_taps((pre, None), [x for x in TAPS if x[1] == 0], lambda b, c: xb.at[c], k1)
-    turn(copies, kd, kdt)
-
-
-def early_kernel(at_ref, g_ref, h_ref, k1, pre_ref, xb, pre, edge_ref):
-    picks = [window_pick(at_ref, b) for b in range(3)]
+
+
+def early_kernel(g_ref, h_ref, k1, pre_ref, xb, pre, edge_ref):
+    picks = [window_pick(b) for b in range(3)]
     for b in range(3):
         edge_ref[b] = picks[b][64:, 96:]
     own = jnp.concatenate([picks[1][:, :96], picks[2][:, :96]], axis=0)
@@ -176,26 +175,25 @@
     add_taps((pre, pre_ref), taps, lambda b, c: xb.at[b * 3 + c - 3], k1)
 
 
-SPILL = 48
-
-
-def clip_pick(at_ref, b, c, rows, width, first):
+SPILL = 16
+
+
+def clip_pick(b, c, rows, width, first):
     m, n = iota((rows, 64), 0), iota((rows, 64), 1)
     h, v = div(m, width), first + mod(m, width)
     k, col = div(n, W), column(mod(n, W))
     hit = (h == k + b) & (v == col + c) & (v < W + 2)
     if b != 1:
-        hit = hit & jnp.logical_not((at_ref[1] == HA - 1) & (k == (3 if b == 0 else 2)))
+        hit = hit & jnp.logical_not((lax.axis_index("ha") == HA - 1) & (k == (3 if b == 0 else 2)))
     if c != 1:
-        hit = hit & jnp.logical_not((at_ref[2] == WA - 1) & (col == (15 if c == 0 else 14)))
+        hit = hit & jnp.logical_not((lax.axis_index("wa") == WA - 1) & (col == (15 if c == 0 else 14)))
     return onehot(hit)
 
 
 def middle_kernel(
-    at_ref, g_ref, h_ref, w_ref, k1, k1t, kdt, pre_ref,
-    gp, act, cu, spill_ref, pre, act32, fix, yb,
+    g_ref, h_ref, w_ref, k1, kdt, pre_ref, gp, act, cu, pre, act32, fix
 ):
-    ta, last_h, last_w = at_ref[0], at_ref[1] == HA - 1, at_ref[2] == WA - 1
+    ta, last_h, last_w = lax.axis_index("ta"), lax.axis_index("ha") == HA - 1, lax.axis_index("wa") == WA - 1
     cot = 2 * F * W
 
     edges = w_ref[...].reshape(T * 16, C)
@@ -259,37 +257,17 @@
     gp[T + 2 : T + 4] = jnp.zeros((2, 64, C), BF16)
     act[...] = act32[...].astype(BF16)
 
-    later = gp[pl.ds(2 + F * ta, F + 2)]
-    pick = jnp.concatenate(
-        [clip_pick(at_ref, b, c, SPILL, 8, W) for b in range(3) for c in (1, 2)], axis=0
-    )
-    for t in range(F + 2):
-        built = dot(pick, later[t]).astype(BF16)
-        for i in range(6):
-            yb[i, t] = built[i * SPILL : (i + 1) * SPILL]
-    total = None
-    for i, (a, b, c) in enumerate(TAPS):
-        if c == 0:
-            continue
-        x = yb[b * 2 + c - 1, 2 - a : 2 - a + F].reshape(F * SPILL, C)
-        y = dot(x, k1t[i * C : (i + 1) * C])
-        total = y if total is None else total + y
-    spill_ref[...] = total.reshape(F, SPILL, C)
-
 
 def main_kernel(
-    at_ref, w_ref, xa_ref, xb_ref, edge_ref, gp, act, cu, mine_ref, other_ref, xc, tt
+    w_ref, xa_ref, xb_ref, edge_ref, gp, act, cu, mine_ref, other_ref, xc, tt
 ):
-    ta, core = at_ref[0], lax.rem(at_ref[1], 2)
+    ta, core = lax.axis_index("ta"), lax.rem(lax.axis_index("ha"), 2)
 
     share = onehot(iota((SHARE, C), 1) == iota((SHARE, C), 0) + ta * SHARE)
+    turned = dot_t(share, gp[...].reshape((T + 4) * 64, C))
     left = jnp.concatenate(
-        [
-            dot_t(share, gp[2 - a : 2 - a + T + 2].reshape((T + 2) * 64, C)).astype(BF16)
-            for a in range(3)
-        ],
-        axis=0,
-    )
+        [turned[:, (2 - a) * 64 : (2 - a + T + 2) * 64] for a in range(3)], axis=0
+    ).astype(BF16)
     late = edge_ref[...].reshape(6 * 64, 16)
     windows = [xa_ref.at[i] if i < 3 else xb_ref.at[i - 3] for i in range(9)]
     for i in range(6):
@@ -334,33 +312,34 @@
             other_ref[spot : spot + SLOT] = jnp.where(core == 0, pair[1], pair[0]).astype(BF16)
 
 
-WIDE = 96
-
-
-def clip_kernel(at_ref, gp, k1t, own_ref, past_ref, yb, acc):
-    later = gp[pl.ds(2 + F * at_ref[0], F + 2)]
-    pick = jnp.concatenate([clip_pick(at_ref, i // 3, i % 3, WIDE, W, 0) for i in range(9)], axis=0)
-    for t in range(F + 2):
-        built = dot(pick, later[t]).astype(BF16)
-        for i in range(9):
-            yb[i, t] = built[i * WIDE : (i + 1) * WIDE]
+MAIN = (R + 2) * W
+WIDE = MAIN + SPILL
+
+
+def clip_kernel(gp, k1t, own_ref, past_ref, spill_ref, yb, acc):
+    later = gp[pl.ds(2 + F * lax.axis_index("ta"), F + 2)]
+    for i in range(9):
+        b, c = i // 3, i % 3
+        pick = jnp.concatenate([clip_pick(b, c, MAIN, W, 0), clip_pick(b, c, SPILL, 2, W)], axis=0)
+        for t in range(F + 2):
+            yb[i, t] = dot(pick, later[t]).astype(BF16)
     for i, (a, b, c) in enumerate(TAPS):
-        y = dot(yb[b * 3 + c, 2 - a : 2 - a + F].reshape(F * WIDE, C), k1t[i * C : (i + 1) * C])
+        x = yb[b * 3 + c, 2 - a : 2 - a + F].reshape(F * WIDE, C)
+        y = dot(x, k1t[i * C : (i + 1) * C])
         if i == 0:
             acc[...] = y
         else:
             acc[...] += y
     for f in range(F):
         own_ref[f] = acc[f * WIDE : f * WIDE + R * W]
-        past_ref[f] = acc[f * WIDE + R * W : (f + 1) * WIDE]
-
-
-def seam_kernel(past_ref, spill_ref, out_ref):
-    for f in range(F):
-        for h in range(2):
-            at, spot = h * W, (R + h) * 8
-            out_ref[f, at : at + 8] = past_ref[f, at : at + 8] + spill_ref[f, spot : spot + 8]
-            out_ref[f, at + 8 : at + W] = past_ref[f, at + 8 : at + W]
+        past_ref[f] = acc[f * WIDE + R * W : f * WIDE + MAIN]
+        spill_ref[f] = acc[f * WIDE + MAIN : (f + 1) * WIDE]
+
+
+def spilled(spill_ref, f, h):
+    place = iota((8, C), 0)
+    first, second = spill_ref[f, 2 * h : 2 * h + 1], spill_ref[f, 2 * h + 1 : 2 * h + 2]
+    return jnp.where(place == 0, first, jnp.where(place == 1, second, 0.0))
 
 
 STAGES = 4
@@ -378,15 +357,18 @@
         copy.wait()
 
 
-def finish_kernel(parts_ref, own_ref, spill_ref, past_ref, clip_ref, conv_ref, down_ref):
+def finish_kernel(
+    parts_ref, own_ref, spill_ref, past_ref, corner_ref, clip_ref, conv_ref, down_ref
+):
     for f in range(F):
         for h in range(R):
             at = h * W
-            low = own_ref[f, at : at + 8] + spill_ref[f, h * 8 : h * 8 + 8]
-            x = jnp.concatenate([low, own_ref[f, at + 8 : at + W]], axis=0)
+            low = own_ref[f, at : at + 8] + spilled(spill_ref, f, h)
+            high = own_ref[f, at + 8 : at + W]
             if h < 2:
-                x += past_ref[f, at : at + W]
-            clip_ref[f, at : at + W] = x.astype(BF16)
+                low += past_ref[f, at : at + 8] + spilled(corner_ref, f, R + h)
+                high += past_ref[f, at + 8 : at + W]
+            clip_ref[f, at : at + W] = jnp.concatenate([low, high], axis=0).astype(BF16)
     total = parts_ref[0].astype(F32)
     for i in range(1, PEERS):
         total += parts_ref[i].astype(F32)
@@ -407,7 +389,7 @@
         out_specs=jax.tree.map(lambda _: out or whole(), outs),
         scratch_shapes=scratch,
         compiler_params=pltpu.CompilerParams(vmem_limit_bytes=VMEM_BYTES),
-        cost_estimate=pl.CostEstimate(flops=flops, bytes_accessed=8_000_000, transcendentals=0),
+        cost_estimate=pl.CostEstimate(flops=flops, bytes_accessed=10_000, transcendentals=0),
         name=name,
     )
 
@@ -434,89 +416,85 @@
 
 
 def local(clip, conv_weight, down_weight, out_cotangent):
-    smem, anywhere = pl.BlockSpec(memory_space=pltpu.SMEM), pl.BlockSpec(memory_space=pl.ANY)
-    at = jnp.stack([lax.axis_index(a) for a in ("ta", "ha", "wa")]).astype(jnp.int32)
+    anywhere = pl.BlockSpec(memory_space=pl.ANY)
     dma = pltpu.SemaphoreType.DMA
     packed = call(
-        pack_kernel, shape((BLOCK, C)), [anywhere] * 2, [dma((9,))], 10**5, "pack"
-    )(in_hbm(clip), in_hbm(out_cotangent.reshape(-1, C)))
+        pack_kernel, shape((BLOCK, C)), [anywhere] * 2, [dma((5,))], 10**5, "pack"
+    )(in_hbm(clip.reshape(2 * F, 2 * W, C)), in_hbm(out_cotangent.reshape(-1, C)))
     around = [shift(packed, "ta", by) for by in (1, 2, 3)]
     weight = on_chip((27 * C, C))
-    k1, k1t = call(
+    k1, k1t, kdt = call(
         load_kernel,
-        [weight] * 2,
-        [smem] + [anywhere] * 2,
-        [dma((9,))],
-        2 * 10**9,
+        [weight] * 3,
+        [anywhere] * 3,
+        [pltpu.VMEM((27 * C, C), BF16), dma((9,)), dma((9,))],
+        4 * 10**9,
         "load",
-    )(at, packed, in_hbm(conv_weight))
-    k1, k1t = in_vmem(k1), in_vmem(k1t)
+    )(packed, in_hbm(conv_weight), in_hbm(down_weight))
+    k1, k1t, kdt = in_vmem(k1), in_vmem(k1t), in_vmem(kdt)
     head = call(
         head_kernel,
         shape((TA, HEAD, C)),
-        [smem] + [whole()] * 4 + [anywhere],
+        [whole()] * 4 + [anywhere],
         [],
         10**5,
         "head",
-    )(at, packed, *around, k1t)
+    )(packed, *around, k1t)
     h = shift(head, "ha", -1)
-    g, xa, pre, kdt = call(
+    g, xa, pre = call(
         own_kernel,
-        [shape((TA, BLOCK, C)), on_chip((3, T + 2, 64, C)), on_chip((T * 64, C), F32), weight],
-        [smem] + [whole()] * 4 + [anywhere, whole(), anywhere],
-        [pltpu.VMEM((27 * C, C), BF16), dma((9,))],
+        [shape((TA, BLOCK, C)), on_chip((3, T + 2, 64, C)), on_chip((T * 64, C), F32)],
+        [whole()] * 4 + [anywhere, whole()],
+        [],
         3 * 10**9,
         "own",
-    )(at, packed, *around, head, k1, in_hbm(down_weight))
-    xa, pre, kdt = in_vmem(xa), in_vmem(pre), in_vmem(kdt)
+    )(packed, *around, head, k1)
+    xa, pre = in_vmem(xa), in_vmem(pre)
     w = call(edge_kernel, shape((T, 16, C)), [whole()] * 2, [], 10**7, "edge")(g, h)
     w = shift(w, "wa", -1)
     xb, pre, edge = call(
         early_kernel,
         [on_chip((6, T + 2, 64, C)), on_chip((T * 64, C), F32), on_chip((3, 128, 16))],
-        [smem] + [whole()] * 4,
+        [whole()] * 4,
         [],
         3 * 10**9,
         "early",
-    )(at, g, h, k1, pre)
+    )(g, h, k1, pre)
     xb, pre, edge = in_vmem(xb), in_vmem(pre), in_vmem(edge)
-    gp, act, cu, spill = call(
+    gp, act, cu = call(
         middle_kernel,
         [
             on_chip((T + 4, 64, C)),
             on_chip((8, 64, C)),
             on_chip((9, TA + 1, 16, C)),
-            shape((F, SPILL, C), F32),
         ],
-        [smem] + [whole()] * 7,
+        [whole()] * 6,
         [
             pltpu.VMEM((T * 64, C), F32),
             pltpu.VMEM((8, 64, C), F32),
             pltpu.VMEM((64, C), F32),
-            pltpu.VMEM((6, F + 2, SPILL, C), BF16),
         ],
         3 * 10**9,
         "middle",
-    )(at, g, h, w, k1, k1t, kdt, pre)
+    )(g, h, w, k1, kdt, pre)
     gp, act, cu = in_vmem(gp), in_vmem(act), in_vmem(cu)
-    spill = shift(spill, "wa", 1)
     mine, other = call(
         main_kernel,
         [shape((PEERS * SLOT, 2 * SHARE)), shape((PEERS * SLOT, 2 * SHARE))],
-        [smem] + [whole()] * 7,
+        [whole()] * 7,
         [pltpu.VMEM((6, T + 2, 64, C), BF16), pltpu.VMEM((27 * C + 8, 2 * SHARE), F32)],
         5 * 10**9,
         "main",
-    )(at, w, xa, xb, edge, gp, act, cu)
+    )(w, xa, xb, edge, gp, act, cu)
     other = lax.ppermute(other, "ha", [(i, i ^ 1) for i in range(HA)])
-    own, past = call(
+    own, past, spill = call(
         clip_kernel,
-        [shape((F, R * W, C), F32), shape((F, 2 * W, C), F32)],
-        [smem] + [whole()] * 2,
+        [shape((F, R * W, C), F32), shape((F, 2 * W, C), F32), shape((F, SPILL, C), F32)],
+        [whole()] * 2,
         [pltpu.VMEM((9, F + 2, WIDE, C), BF16), pltpu.VMEM((F * WIDE, C), F32)],
         10**9,
         "clip",
-    )(at, gp, k1t)
+    )(gp, k1t)
     pair = call(
         join_kernel,
         shape((PEERS * SLOT, 2 * SHARE)),
@@ -526,21 +504,20 @@
         "join",
         anywhere,
     )(mine, other, own)
-    pair, spill = lax.optimization_barrier((pair, spill))
-    past = call(
-        seam_kernel, shape((F, 2 * W, C), F32), [whole()] * 2, [], 10**5, "seam"
-    )(past, spill)
+    pairs = [(i * WA + j, (i + 1) % HA * WA + (j + 1) % WA) for i in range(HA) for j in range(WA)]
+    corner = lax.ppermute(spill, ("ha", "wa"), pairs)
+    spill = shift(spill, "wa", 1)
     past = shift(past, "ha", 1)
     groups = [[i * WA + w for i in range(c, HA, 2) for w in range(WA)] for c in range(2)]
     parts = lax.all_to_all(pair, ("ha", "wa"), 0, 0, axis_index_groups=groups, tiled=True)
     grad_clip, grad_conv, grad_down = call(
         finish_kernel,
         [shape((F, R * W, C)), shape((SHARE, PART), F32), shape((SHARE, PART), F32)],
-        [whole()] * 4,
+        [whole()] * 5,
         [],
         10**6,
         "finish",
-    )(parts.reshape(PEERS, SLOT, 2 * SHARE), own, spill, past)
+    )(parts.reshape(PEERS, SLOT, 2 * SHARE), own, spill, past, corner)
     grad_clip = grad_clip.reshape(F, R, W, C)
     return (grad_clip, grad_conv.T, grad_down.T)
 

time: 64.9 us -> 61.1 us (0.941)
  Pallas kernels: 21.4 us -> 15.9 us
  starting transfers between devices: 23.4 us -> 27.3 us
  waiting for transfers between devices: 19 us -> 16.9 us
    all_to_all x1, waiting for transfers between devices: 5.33 us -> 0.39 us  [local(): lax.all_to_all(pair, ('ha', 'wa'), 0, 0, axis_index_groups=groups, tiled=...]
    all_to_all x1, starting transfers between devices: 5.2 us -> 7.37 us  [local(): lax.all_to_all(pair, ('ha', 'wa'), 0, 0, axis_index_groups=groups, tiled=...]
    pallas_call x1, Pallas kernels: 3.14 us -> 1 us  [local(): call(own_kernel, [shape((TA, BLOCK, C)), on_chip((3, T + 2, 64, C)), on_c...]
    pallas_call x1, Pallas kernels: 3.35 us -> 1.4 us  [local(): call(middle_kernel, [on_chip((T + 4, 64, C)), on_chip((8, 64, C)), on_chi...]
    ppermute x7, starting transfers between devices: 16.5 us -> 17.8 us  [shift(): return lax.ppermute(x, axis, [(i, (i + by) % count) for i in range(count)])]
    ppermute x0 -> x1, starting transfers between devices: none -> 1.27 us  [local(): corner = lax.ppermute(spill, ('ha', 'wa'), pairs)]
    ppermute x7, waiting for transfers between devices: 13.6 us -> 14.8 us  [shift(): return lax.ppermute(x, axis, [(i, (i + by) % count) for i in range(count)])]
    ppermute x0 -> x1, waiting for transfers between devices: none -> 1.17 us  [local(): corner = lax.ppermute(spill, ('ha', 'wa'), pairs)]
  transfers between devices with their start and end apart: 9 -> 10, of which waited for: 5 -> 6; matrix products, arithmetic and copies ran while one was open for 0% -> 0% of each run, Pallas kernels for 19% -> 15%
where the time goes in v5:
time: 61.1 us; the launch traced here: 60.8 us
  starting transfers between devices  27.3 us (45%)
  waiting for transfers between devices  16.9 us (28%)
  Pallas kernels  15.9 us (26%)
  between operations  0.74 us (1%)
    ppermute x7, starting transfers between devices, shift(): return lax.ppermute(x, axis, [(i, (i + by) % count) for i in range(count)])  17.8 us
    ppermute x7, waiting for transfers between devices, shift(): return lax.ppermute(x, axis, [(i, (i + by) % count) for i in range(count)])  14.8 us
    all_to_all x1, starting transfers between devices, local(): lax.all_to_all(pair, ('ha', 'wa'), 0, 0, axis_index_groups=groups, tiled=...  7.37 us
    pallas_call x1, Pallas kernels, local(): call(load_kernel, [weight] * 3, [anywhere] * 3, [pltpu.VMEM((27 * C, C),...  4.6 us
    pallas_call x1, Pallas kernels, local(): call(main_kernel, [shape((PEERS * SLOT, 2 * SHARE)), shape((PEERS * SLOT,...  2.66 us
    pallas_call x1, Pallas kernels, local(): call(early_kernel, [on_chip((6, T + 2, 64, C)), on_chip((T * 64, C), F32)...  1.81 us
    pallas_call x1, Pallas kernels, local(): call(clip_kernel, [shape((F, R * W, C), F32), shape((F, 2 * W, C), F32),...  1.57 us
    pallas_call x1, Pallas kernels, local(): call(middle_kernel, [on_chip((T + 4, 64, C)), on_chip((8, 64, C)), on_chi...  1.4 us
  transfers between devices with their start and end apart: 10, of which 6 were waited for; matrix products, arithmetic and copies ran while one was open for 0% of the time, Pallas kernels for 15%

profile of v5, /device:TPU:1, one launch (start us, length us, event | category | flops | bytes accessed | tf_op | source)
XLA Modules:
  0.0 60.8 jit_solution(13534879628826982111)
XLA Ops:
  0.6 0.8 %pack.1.after_ref.own_ref = bf16[144,256]{1,0:T(8,128)(2,1)S(1)} custom-call(bf16[4,32,256]{2,1,0:T(8,128)(2,1)} %bitcast.6, bf16[16,256]{1,0:T(8,128)(2,1)} %bitcast.7), custom_call_target="tpu_custom_call" | custom-call | flops 100000 | bytes 10000 | tf_op jit(solution)/shard_map/pack/pallas_call | solution.py:421
  1.5 3.9 %collective-permute-start = (bf16[144,256]{1,0:T(8,128)(2,1)S(1)}, bf16[144,256]{1,0:T(8,128)(2,1)S(1)}, u32[]{:S(2)}, u32[]{:S(2)}) collective-permute-start(bf16[144,256]{1,0:T(8,128)(2,1)S(1)} %pack.1.after_ref.own_ref), channel_id=1, source_target_pairs={{0,64},{64,128},{128,192},{192,0},{1,65},{65,129},{129,193},{193,1... | collective-permute-start | bytes 221192 | tf_op jit(solution)/shard_map/ppermute | solution.py:415
  5.3 5.1 %collective-permute-start.1 = (bf16[144,256]{1,0:T(8,128)(2,1)S(1)}, bf16[144,256]{1,0:T(8,128)(2,1)S(1)}, u32[]{:S(2)}, u32[]{:S(2)}) collective-permute-start(bf16[144,256]{1,0:T(8,128)(2,1)S(1)} %pack.1.after_ref.own_ref), channel_id=1, source_target_pairs={{0,128},{64,192},{128,0},{192,64},{1,129},{65,193},{129,1},{193,65... | collective-permute-start | bytes 221192 | tf_op jit(solution)/shard_map/ppermute | solution.py:415
  10.5 2.4 %collective-permute-start.2 = (bf16[144,256]{1,0:T(8,128)(2,1)S(1)}, bf16[144,256]{1,0:T(8,128)(2,1)S(1)}, u32[]{:S(2)}, u32[]{:S(2)}) collective-permute-start(bf16[144,256]{1,0:T(8,128)(2,1)S(1)} %pack.1.after_ref.own_ref), channel_id=1, source_target_pairs={{0,192},{64,0},{128,64},{192,128},{1,193},{65,1},{129,65},{193,129... | collective-permute-start | bytes 221192 | tf_op jit(solution)/shard_map/ppermute | solution.py:415
  12.8 4.6 %load.1 = (bf16[6912,256]{1,0:T(8,128)(2,1)S(1)}, bf16[6912,256]{1,0:T(8,128)(2,1)S(1)}, bf16[6912,256]{1,0:T(8,128)(2,1)S(1)}) custom-call(bf16[144,256]{1,0:T(8,128)(2,1)S(1)} %pack.1.after_ref.own_ref, bf16[6912,256]{1,0:T(8,128)(2,1)} %k1_ref.1, bf16[6912,256]{1,0:T(8,128)(2,1)} %kd_ref.1), custom_call_target="tpu_custom_call" | custom-call | flops 4000000000 | bytes 10000 | tf_op jit(solution)/shard_map/load/pallas_call | solution.py:426
  17.5 0.0 collective-permute-done.one_ref
  17.5 0.0 collective-permute-done.1.two_ref
  17.5 1.3 %collective-permute-done.2.three_ref = bf16[144,256]{1,0:T(8,128)(2,1)S(1)} collective-permute-done((bf16[144,256]{1,0:T(8,128)(2,1)S(1)}, bf16[144,256]{1,0:T(8,128)(2,1)S(1)}, u32[]{:S(2)}, u32[]{:S(2)}) %collective-permute-start.2) | collective-permute-done | bytes 73760 | tf_op jit(solution)/shard_map/ppermute | solution.py:415
  18.8 0.5 collective-permute-start.3
  19.3 1.0 %own.1 = (bf16[4,144,256]{2,1,0:T(8,128)(2,1)S(1)}, bf16[3,10,64,256]{3,2,1,0:T(8,128)(2,1)S(1)}, f32[512,256]{1,0:T(8,128)S(1)}) custom-call(bf16[144,256]{1,0:T(8,128)(2,1)S(1)} %pack.1.after_ref.own_ref, bf16[144,256]{1,0:T(8,128)(2,1)S(1)} %collective-permute-done.one_ref, bf16[144,256]{1,0:T(8,128)(2,1)S(1)} %collective-permute-done.1.two_ref, ...), custom_call_target="tpu_custom_call" | custom-call | flops 3000000000 | bytes 10000 | tf_op jit(solution)/shard_map/own/pallas_call | solution.py:444
  20.3 3.2 %collective-permute-done.3.h_ref = bf16[4,80,256]{2,1,0:T(8,128)(2,1)S(1)} collective-permute-done((bf16[4,80,256]{2,1,0:T(8,128)(2,1)S(1)}, bf16[4,80,256]{2,1,0:T(8,128)(2,1)S(1)}, u32[]{:S(2)}, u32[]{:S(2)}) %collective-permute-start.3) | collective-permute-done | bytes 163872 | tf_op jit(solution)/shard_map/ppermute | solution.py:415
  23.5 0.2 edge.1
  23.7 2.9 %collective-permute-start.4 = (bf16[8,16,256]{2,1,0:T(8,128)(2,1)S(1)}, bf16[8,16,256]{2,1,0:T(8,128)(2,1)S(1)}, u32[]{:S(2)}, u32[]{:S(2)}) collective-permute-start(bf16[8,16,256]{2,1,0:T(8,128)(2,1)S(1)} %edge.1), channel_id=1, source_target_pairs={{0,7},{1,0},{2,1},{3,2},{4,3},{5,4},{6,5},{7,6},{8,15},{9,8},{10,9... | collective-permute-start | bytes 196616 | tf_op jit(solution)/shard_map/ppermute | solution.py:415
  26.6 1.8 %early.1 = (bf16[6,10,64,256]{3,2,1,0:T(8,128)(2,1)S(1)}, f32[512,256]{1,0:T(8,128)S(1)}, bf16[3,128,16]{2,1,0:T(8,128)(2,1)S(1)}) custom-call(bf16[4,144,256]{2,1,0:T(8,128)(2,1)S(1)} %get-tuple-element.25.g_ref, bf16[4,80,256]{2,1,0:T(8,128)(2,1)S(1)} %collective-permute-done.3.h_ref, bf16[6912,256]{1,0:T(8,128)(2,1)S(1)} %get-tuple-element.24.k1, ...), custom_call_target="tpu_custom_call" | custom-call | flops 3000000000 | bytes 10000 | tf_op jit(solution)/shard_map/early/pallas_call | solution.py:455
  28.4 0.0 collective-permute-done.4.w_ref
  28.4 1.4 %middle.1 = (bf16[12,64,256]{2,1,0:T(8,128)(2,1)S(1)}, bf16[8,64,256]{2,1,0:T(8,128)(2,1)S(1)}, bf16[9,5,16,256]{3,2,1,0:T(8,128)(2,1)S(1)}) custom-call(bf16[4,144,256]{2,1,0:T(8,128)(2,1)S(1)} %get-tuple-element.25.g_ref, bf16[4,80,256]{2,1,0:T(8,128)(2,1)S(1)} %collective-permute-done.3.h_ref, bf16[8,16,256]{2,1,0:T(8,128)(2,1)S(1)} %collective-permute-done.4.w_ref, ...), custom_call_target="tpu_custom_call" | custom-call | flops 3000000000 | bytes 10000 | tf_op jit(solution)/shard_map/middle/pallas_call | solution.py:464
  29.8 2.7 %main.1 = (bf16[3584,128]{1,0:T(8,128)(2,1)S(1)}, bf16[3584,128]{1,0:T(8,128)(2,1)S(1)}) custom-call(bf16[8,16,256]{2,1,0:T(8,128)(2,1)S(1)} %collective-permute-done.4.w_ref, bf16[3,10,64,256]{3,2,1,0:T(8,128)(2,1)S(1)} %get-tuple-element.26.xa_ref, bf16[6,10,64,256]{3,2,1,0:T(8,128)(2,1)S(1)} %get-tuple-element.28.xb_ref, ...), custom_call_target="tpu_custom_call" | custom-call | flops 5000000000 | bytes 10000 | tf_op jit(solution)/shard_map/main/pallas_call | solution.py:481
  32.5 0.9 %collective-permute-start.5 = (bf16[3584,128]{1,0:T(8,128)(2,1)S(1)}, bf16[3584,128]{1,0:T(8,128)(2,1)S(1)}, u32[]{:S(2)}, u32[]{:S(2)}) collective-permute-start(bf16[3584,128]{1,0:T(8,128)(2,1)S(1)} %get-tuple-element.36), channel_id=1, source_target_pairs={{0,8},{8,0},{16,24},{24,16},{32,40},{40,32},{48,56},{56,48},{1,9},... | collective-permute-start | bytes 2752520 | tf_op jit(solution)/shard_map/ppermute | solution.py:489
  33.4 1.6 %clip.1 = (f32[2,64,256]{2,1,0:T(8,128)S(1)}, f32[2,32,256]{2,1,0:T(8,128)S(1)}, f32[2,16,256]{2,1,0:T(8,128)S(1)}) custom-call(bf16[12,64,256]{2,1,0:T(8,128)(2,1)S(1)} %get-tuple-element.32.gp, bf16[6912,256]{1,0:T(8,128)(2,1)S(1)} %get-tuple-element.23.after_ref.k1t), custom_call_target="tpu_custom_call" | custom-call | flops 1000000000 | bytes 10000 | tf_op jit(solution)/shard_map/clip/pallas_call | solution.py:490
  34.9 0.5 collective-permute-done.5.other_ref
  35.5 1.0 %join.1 = bf16[3584,128]{1,0:T(8,128)(2,1)} custom-call(bf16[3584,128]{1,0:T(8,128)(2,1)S(1)} %get-tuple-element.35.mine_ref, bf16[3584,128]{1,0:T(8,128)(2,1)S(1)} %collective-permute-done.5.other_ref, f32[2,64,256]{2,1,0:T(8,128)S(1)} %get-tuple-element.37.after_ref.own_ref), custom_call_target="tpu_custom_call" | custom-call | flops 1000000 | bytes 10000 | tf_op jit(solution)/shard_map/join/pallas_call | solution.py:498
  36.5 7.4 %all-to-all-start = ((bf16[32,112,128]{2,1,0:T(8,128)(2,1)}), bf16[32,112,128]{2,1,0:T(8,128)(2,1)S(1)}, u32[]{:S(2)}, u32[]{:S(2)}) async-start(bf16[32,112,128]{2,1,0:T(8,128)(2,1)} %bitcast.2), calls=%async_computation | async-start | bytes 1835008 | tf_op jit(solution)/shard_map/all_to_all | solution.py:512
  43.8 1.8 %collective-permute-start.7 = (f32[2,32,256]{2,1,0:T(8,128)S(1)}, f32[2,32,256]{2,1,0:T(8,128)S(1)}, u32[]{:S(2)}, u32[]{:S(2)}) collective-permute-start(f32[2,32,256]{2,1,0:T(8,128)S(1)} %get-tuple-element.39), channel_id=1, source_target_pairs={{0,8},{8,16},{16,24},{24,32},{32,40},{40,48},{48,56},{56,0},{1,9},... | collective-permute-start | bytes 196616 | tf_op jit(solution)/shard_map/ppermute | solution.py:415
  45.7 1.2 %collective-permute-start.6 = (f32[2,16,256]{2,1,0:T(8,128)S(1)}, f32[2,16,256]{2,1,0:T(8,128)S(1)}, u32[]{:S(2)}, u32[]{:S(2)}) collective-permute-start(f32[2,16,256]{2,1,0:T(8,128)S(1)} %get-tuple-element.38), channel_id=1, source_target_pairs={{0,1},{1,2},{2,3},{3,4},{4,5},{5,6},{6,7},{7,0},{8,9},{9,10},{10,1... | collective-permute-start | bytes 98312 | tf_op jit(solution)/shard_map/ppermute | solution.py:415
  46.9 1.3 %collective-permute-start.8 = (f32[2,16,256]{2,1,0:T(8,128)S(1)}, f32[2,16,256]{2,1,0:T(8,128)S(1)}, u32[]{:S(2)}, u32[]{:S(2)}) collective-permute-start(f32[2,16,256]{2,1,0:T(8,128)S(1)} %get-tuple-element.38), channel_id=1, source_target_pairs={{0,9},{1,10},{2,11},{3,12},{4,13},{5,14},{6,15},{7,8},{8,17},{9,18... | collective-permute-start | bytes 98312 | tf_op jit(solution)/shard_map/ppermute | solution.py:508
  48.1 10.3 %collective-permute-done.6.spill_ref = f32[2,16,256]{2,1,0:T(8,128)S(1)} collective-permute-done((f32[2,16,256]{2,1,0:T(8,128)S(1)}, f32[2,16,256]{2,1,0:T(8,128)S(1)}, u32[]{:S(2)}, u32[]{:S(2)}) %collective-permute-start.6) | collective-permute-done | bytes 32800 | tf_op jit(solution)/shard_map/ppermute | solution.py:415
  58.4 1.2 %collective-permute-done.8.corner_ref = f32[2,16,256]{2,1,0:T(8,128)S(1)} collective-permute-done((f32[2,16,256]{2,1,0:T(8,128)S(1)}, f32[2,16,256]{2,1,0:T(8,128)S(1)}, u32[]{:S(2)}, u32[]{:S(2)}) %collective-permute-start.8) | collective-permute-done | bytes 32800 | tf_op jit(solution)/shard_map/ppermute | solution.py:508
  59.6 0.0 collective-permute-done.7.past_ref
  59.6 0.4 all-to-all-done.parts_ref
  60.0 0.8 %finish.1 = (bf16[2,64,256]{2,1,0:T(8,128)(2,1)}, f32[64,108]{1,0:T(8,128)}, f32[64,108]{1,0:T(8,128)}) custom-call(bf16[32,112,128]{2,1,0:T(8,128)(2,1)S(1)} %all-to-all-done.parts_ref, f32[2,64,256]{2,1,0:T(8,128)S(1)} %get-tuple-element.37.after_ref.own_ref, f32[2,16,256]{2,1,0:T(8,128)S(1)} %collective-permute-done.6.spill_ref, ...), custom_call_target="tpu_custom_call" | custom-call | flops 1000000 | bytes 10000 | tf_op jit(solution)/shard_map/finish/pallas_call | solution.py:513
  (1 shorter events, 0.0 us)
Async XLA Ops:
  1.5 16.0 %collective-permute-start = (bf16[144,256]{1,0:T(8,128)(2,1)S(1)}, bf16[144,256]{1,0:T(8,128)(2,1)S(1)}, u32[]{:S(2)}, u32[]{:S(2)}) collective-permute-start(bf16[144,256]{1,0:T(8,128)(2,1)S(1)} %pack.1.after_ref.own_ref), channel_id=1, source_target_pairs={{0,64},{64,128},{128,192},{192,0},{1,65},{65,129},{129,193},{193,1... | collective-permute-start | bytes 221192 | tf_op jit(solution)/shard_map/ppermute | solution.py:415
  5.3 12.1 %collective-permute-start.1 = (bf16[144,256]{1,0:T(8,128)(2,1)S(1)}, bf16[144,256]{1,0:T(8,128)(2,1)S(1)}, u32[]{:S(2)}, u32[]{:S(2)}) collective-permute-start(bf16[144,256]{1,0:T(8,128)(2,1)S(1)} %pack.1.after_ref.own_ref), channel_id=1, source_target_pairs={{0,128},{64,192},{128,0},{192,64},{1,129},{65,193},{129,1},{193,65... | collective-permute-start | bytes 221192 | tf_op jit(solution)/shard_map/ppermute | solution.py:415
  10.5 8.3 %collective-permute-start.2 = (bf16[144,256]{1,0:T(8,128)(2,1)S(1)}, bf16[144,256]{1,0:T(8,128)(2,1)S(1)}, u32[]{:S(2)}, u32[]{:S(2)}) collective-permute-start(bf16[144,256]{1,0:T(8,128)(2,1)S(1)} %pack.1.after_ref.own_ref), channel_id=1, source_target_pairs={{0,192},{64,0},{128,64},{192,128},{1,193},{65,1},{129,65},{193,129... | collective-permute-start | bytes 221192 | tf_op jit(solution)/shard_map/ppermute | solution.py:415
  18.8 4.8 %collective-permute-start.3 = (bf16[4,80,256]{2,1,0:T(8,128)(2,1)S(1)}, bf16[4,80,256]{2,1,0:T(8,128)(2,1)S(1)}, u32[]{:S(2)}, u32[]{:S(2)}) collective-permute-start(bf16[4,80,256]{2,1,0:T(8,128)(2,1)S(1)} %head.1.after_ref), channel_id=1, source_target_pairs={{0,56},{8,0},{16,8},{24,16},{32,24},{40,32},{48,40},{56,48},{1,57}... | collective-permute-start | bytes 491528 | tf_op jit(solution)/shard_map/ppermute | solution.py:415
  23.7 4.7 %collective-permute-start.4 = (bf16[8,16,256]{2,1,0:T(8,128)(2,1)S(1)}, bf16[8,16,256]{2,1,0:T(8,128)(2,1)S(1)}, u32[]{:S(2)}, u32[]{:S(2)}) collective-permute-start(bf16[8,16,256]{2,1,0:T(8,128)(2,1)S(1)} %edge.1), channel_id=1, source_target_pairs={{0,7},{1,0},{2,1},{3,2},{4,3},{5,4},{6,5},{7,6},{8,15},{9,8},{10,9... | collective-permute-start | bytes 196616 | tf_op jit(solution)/shard_map/ppermute | solution.py:415
  32.5 3.0 %collective-permute-start.5 = (bf16[3584,128]{1,0:T(8,128)(2,1)S(1)}, bf16[3584,128]{1,0:T(8,128)(2,1)S(1)}, u32[]{:S(2)}, u32[]{:S(2)}) collective-permute-start(bf16[3584,128]{1,0:T(8,128)(2,1)S(1)} %get-tuple-element.36), channel_id=1, source_target_pairs={{0,8},{8,0},{16,24},{24,16},{32,40},{40,32},{48,56},{56,48},{1,9},... | collective-permute-start | bytes 2752520 | tf_op jit(solution)/shard_map/ppermute | solution.py:489
  36.5 23.5 %all-to-all-start = ((bf16[32,112,128]{2,1,0:T(8,128)(2,1)}), bf16[32,112,128]{2,1,0:T(8,128)(2,1)S(1)}, u32[]{:S(2)}, u32[]{:S(2)}) async-start(bf16[32,112,128]{2,1,0:T(8,128)(2,1)} %bitcast.2), calls=%async_computation | async-start | bytes 1835008 | tf_op jit(solution)/shard_map/all_to_all | solution.py:512
  43.8 15.8 %collective-permute-start.7 = (f32[2,32,256]{2,1,0:T(8,128)S(1)}, f32[2,32,256]{2,1,0:T(8,128)S(1)}, u32[]{:S(2)}, u32[]{:S(2)}) collective-permute-start(f32[2,32,256]{2,1,0:T(8,128)S(1)} %get-tuple-element.39), channel_id=1, source_target_pairs={{0,8},{8,16},{16,24},{24,32},{32,40},{40,48},{48,56},{56,0},{1,9},... | collective-permute-start | bytes 196616 | tf_op jit(solution)/shard_map/ppermute | solution.py:415
  45.7 12.8 %collective-permute-start.6 = (f32[2,16,256]{2,1,0:T(8,128)S(1)}, f32[2,16,256]{2,1,0:T(8,128)S(1)}, u32[]{:S(2)}, u32[]{:S(2)}) collective-permute-start(f32[2,16,256]{2,1,0:T(8,128)S(1)} %get-tuple-element.38), channel_id=1, source_target_pairs={{0,1},{1,2},{2,3},{3,4},{4,5},{5,6},{6,7},{7,0},{8,9},{9,10},{10,1... | collective-permute-start | bytes 98312 | tf_op jit(solution)/shard_map/ppermute | solution.py:415
  46.9 12.7 %collective-permute-start.8 = (f32[2,16,256]{2,1,0:T(8,128)S(1)}, f32[2,16,256]{2,1,0:T(8,128)S(1)}, u32[]{:S(2)}, u32[]{:S(2)}) collective-permute-start(f32[2,16,256]{2,1,0:T(8,128)S(1)} %get-tuple-element.38), channel_id=1, source_target_pairs={{0,9},{1,10},{2,11},{3,12},{4,13},{5,14},{6,15},{7,8},{8,17},{9,18... | collective-permute-start | bytes 98312 | tf_op jit(solution)/shard_map/ppermute | solution.py:508

commit v6 on v5

--- a/solution.py
+++ b/solution.py
@@ -297,19 +297,23 @@
         for place, (i, _) in enumerate(taps):
             lower[i] = y[place * SHARE : (place + 1) * SHARE]
     for i in range(27):
-        tt[i * C : (i + 1) * C] = jnp.concatenate([upper[i], lower[i]], axis=0).T
+        both = jnp.concatenate([upper[i], lower[i]], axis=0).astype(BF16)
+        tt[i * C : (i + 1) * C] = both.T.astype(F32)
     tt[27 * C :] = jnp.zeros((8, 2 * SHARE), F32)
 
-    for x in range(HA // 2):
-        for w in range(WA):
-            pair = []
-            for cc in range(2):
-                first = ((x * 2 + cc) * WA + w) * PART
-                y = tt[first : first + SLOT]
-                pair.append(y)
-            spot = (x * WA + w) * SLOT
-            mine_ref[spot : spot + SLOT] = jnp.where(core == 0, pair[0], pair[1]).astype(BF16)
-            other_ref[spot : spot + SLOT] = jnp.where(core == 0, pair[1], pair[0]).astype(BF16)
+    def cut(out_ref, parity):
+        for x in range(HA // 2):
+            for w in range(WA):
+                first = ((x * 2 + parity) * WA + w) * PART
+                spot = (x * WA + w) * SLOT
+                out_ref[spot : spot + SLOT] = tt[first : first + SLOT].astype(BF16)
+
+    for parity in range(2):
+
+        @pl.when(core == parity)
+        def _(parity=parity):
+            cut(mine_ref, parity)
+            cut(other_ref, 1 - parity)
 
 
 MAIN = (R + 2) * W
@@ -332,13 +336,13 @@
             acc[...] += y
     for f in range(F):
         own_ref[f] = acc[f * WIDE : f * WIDE + R * W]
-        past_ref[f] = acc[f * WIDE + R * W : f * WIDE + MAIN]
-        spill_ref[f] = acc[f * WIDE + MAIN : (f + 1) * WIDE]
-
-
-def spilled(spill_ref, f, h):
+        past_ref[f] = acc[f * WIDE + R * W : f * WIDE + MAIN].astype(BF16)
+        spill_ref[f] = acc[f * WIDE + MAIN : (f + 1) * WIDE].astype(BF16)
+
+
+def spilled(spill, h):
     place = iota((8, C), 0)
-    first, second = spill_ref[f, 2 * h : 2 * h + 1], spill_ref[f, 2 * h + 1 : 2 * h + 2]
+    first, second = spill[2 * h : 2 * h + 1], spill[2 * h + 1 : 2 * h + 2]
     return jnp.where(place == 0, first, jnp.where(place == 1, second, 0.0))
 
 
@@ -361,13 +365,15 @@
     parts_ref, own_ref, spill_ref, past_ref, corner_ref, clip_ref, conv_ref, down_ref
 ):
     for f in range(F):
+        spill, corner = spill_ref[f].astype(F32), corner_ref[f].astype(F32)
+        past = past_ref[f].astype(F32)
         for h in range(R):
             at = h * W
-            low = own_ref[f, at : at + 8] + spilled(spill_ref, f, h)
+            low = own_ref[f, at : at + 8] + spilled(spill, h)
             high = own_ref[f, at + 8 : at + W]
             if h < 2:
-                low += past_ref[f, at : at + 8] + spilled(corner_ref, f, R + h)
-                high += past_ref[f, at + 8 : at + W]
+                low += past[at : at + 8] + spilled(corner, R + h)
+                high += past[at + 8 : at + W]
             clip_ref[f, at : at + W] = jnp.concatenate([low, high], axis=0).astype(BF16)
     total = parts_ref[0].astype(F32)
     for i in range(1, PEERS):
@@ -489,7 +495,7 @@
     other = lax.ppermute(other, "ha", [(i, i ^ 1) for i in range(HA)])
     own, past, spill = call(
         clip_kernel,
-        [shape((F, R * W, C), F32), shape((F, 2 * W, C), F32), shape((F, SPILL, C), F32)],
+        [shape((F, R * W, C), F32), shape((F, 2 * W, C)), shape((F, SPILL, C))],
         [whole()] * 2,
         [pltpu.VMEM((9, F + 2, WIDE, C), BF16), pltpu.VMEM((F * WIDE, C), F32)],
         10**9,

time: 61.1 us -> 60.4 us (0.989)
  no operation moved by 1% of the time
where the time goes in v6:
time: 60.4 us; the launch traced here: 60.1 us
  starting transfers between devices  27.3 us (45%)
  waiting for transfers between devices  16.6 us (27%)
  Pallas kernels  15.4 us (25%)
  between operations  0.74 us (1%)
    ppermute x7, starting transfers between devices, shift(): return lax.ppermute(x, axis, [(i, (i + by) % count) for i in range(count)])  17.8 us
    ppermute x7, waiting for transfers between devices, shift(): return lax.ppermute(x, axis, [(i, (i + by) % count) for i in range(count)])  14.6 us
    all_to_all x1, starting transfers between devices, local(): lax.all_to_all(pair, ('ha', 'wa'), 0, 0, axis_index_groups=groups, tiled=...  7.39 us
    pallas_call x1, Pallas kernels, local(): call(load_kernel, [weight] * 3, [anywhere] * 3, [pltpu.VMEM((27 * C, C),...  4.6 us
    pallas_call x1, Pallas kernels, local(): call(main_kernel, [shape((PEERS * SLOT, 2 * SHARE)), shape((PEERS * SLOT,...  2.25 us
    pallas_call x1, Pallas kernels, local(): call(early_kernel, [on_chip((6, T + 2, 64, C)), on_chip((T * 64, C), F32)...  1.81 us
    pallas_call x1, Pallas kernels, local(): call(clip_kernel, [shape((F, R * W, C), F32), shape((F, 2 * W, C)), shape...  1.57 us
    pallas_call x1, Pallas kernels, local(): call(middle_kernel, [on_chip((T + 4, 64, C)), on_chip((8, 64, C)), on_chi...  1.39 us
  transfers between devices with their start and end apart: 10, of which 6 were waited for; matrix products, arithmetic and copies ran while one was open for 0% of the time, Pallas kernels for 15%

profile of v6, /device:TPU:1, one launch (start us, length us, event | category | flops | bytes accessed | tf_op | source)
XLA Modules:
  0.0 60.1 jit_solution(17175983710238058878)
XLA Ops:
  0.6 0.8 %pack.1.after_ref.own_ref = bf16[144,256]{1,0:T(8,128)(2,1)S(1)} custom-call(bf16[4,32,256]{2,1,0:T(8,128)(2,1)} %bitcast.6, bf16[16,256]{1,0:T(8,128)(2,1)} %bitcast.7), custom_call_target="tpu_custom_call" | custom-call | flops 100000 | bytes 10000 | tf_op jit(solution)/shard_map/pack/pallas_call | solution.py:427
  1.5 3.9 %collective-permute-start = (bf16[144,256]{1,0:T(8,128)(2,1)S(1)}, bf16[144,256]{1,0:T(8,128)(2,1)S(1)}, u32[]{:S(2)}, u32[]{:S(2)}) collective-permute-start(bf16[144,256]{1,0:T(8,128)(2,1)S(1)} %pack.1.after_ref.own_ref), channel_id=1, source_target_pairs={{0,64},{64,128},{128,192},{192,0},{1,65},{65,129},{129,193},{193,1... | collective-permute-start | bytes 221192 | tf_op jit(solution)/shard_map/ppermute | solution.py:421
  5.3 5.1 %collective-permute-start.1 = (bf16[144,256]{1,0:T(8,128)(2,1)S(1)}, bf16[144,256]{1,0:T(8,128)(2,1)S(1)}, u32[]{:S(2)}, u32[]{:S(2)}) collective-permute-start(bf16[144,256]{1,0:T(8,128)(2,1)S(1)} %pack.1.after_ref.own_ref), channel_id=1, source_target_pairs={{0,128},{64,192},{128,0},{192,64},{1,129},{65,193},{129,1},{193,65... | collective-permute-start | bytes 221192 | tf_op jit(solution)/shard_map/ppermute | solution.py:421
  10.5 2.4 %collective-permute-start.2 = (bf16[144,256]{1,0:T(8,128)(2,1)S(1)}, bf16[144,256]{1,0:T(8,128)(2,1)S(1)}, u32[]{:S(2)}, u32[]{:S(2)}) collective-permute-start(bf16[144,256]{1,0:T(8,128)(2,1)S(1)} %pack.1.after_ref.own_ref), channel_id=1, source_target_pairs={{0,192},{64,0},{128,64},{192,128},{1,193},{65,1},{129,65},{193,129... | collective-permute-start | bytes 221192 | tf_op jit(solution)/shard_map/ppermute | solution.py:421
  12.8 4.6 %load.1 = (bf16[6912,256]{1,0:T(8,128)(2,1)S(1)}, bf16[6912,256]{1,0:T(8,128)(2,1)S(1)}, bf16[6912,256]{1,0:T(8,128)(2,1)S(1)}) custom-call(bf16[144,256]{1,0:T(8,128)(2,1)S(1)} %pack.1.after_ref.own_ref, bf16[6912,256]{1,0:T(8,128)(2,1)} %k1_ref.1, bf16[6912,256]{1,0:T(8,128)(2,1)} %kd_ref.1), custom_call_target="tpu_custom_call" | custom-call | flops 4000000000 | bytes 10000 | tf_op jit(solution)/shard_map/load/pallas_call | solution.py:432
  17.5 0.0 collective-permute-done.one_ref
  17.5 0.0 collective-permute-done.1.two_ref
  17.5 1.3 %collective-permute-done.2.three_ref = bf16[144,256]{1,0:T(8,128)(2,1)S(1)} collective-permute-done((bf16[144,256]{1,0:T(8,128)(2,1)S(1)}, bf16[144,256]{1,0:T(8,128)(2,1)S(1)}, u32[]{:S(2)}, u32[]{:S(2)}) %collective-permute-start.2) | collective-permute-done | bytes 73760 | tf_op jit(solution)/shard_map/ppermute | solution.py:421
  18.8 0.5 collective-permute-start.3
  19.3 1.0 %own.1 = (bf16[4,144,256]{2,1,0:T(8,128)(2,1)S(1)}, bf16[3,10,64,256]{3,2,1,0:T(8,128)(2,1)S(1)}, f32[512,256]{1,0:T(8,128)S(1)}) custom-call(bf16[144,256]{1,0:T(8,128)(2,1)S(1)} %pack.1.after_ref.own_ref, bf16[144,256]{1,0:T(8,128)(2,1)S(1)} %collective-permute-done.one_ref, bf16[144,256]{1,0:T(8,128)(2,1)S(1)} %collective-permute-done.1.two_ref, ...), custom_call_target="tpu_custom_call" | custom-call | flops 3000000000 | bytes 10000 | tf_op jit(solution)/shard_map/own/pallas_call | solution.py:450
  20.3 3.2 %collective-permute-done.3.h_ref = bf16[4,80,256]{2,1,0:T(8,128)(2,1)S(1)} collective-permute-done((bf16[4,80,256]{2,1,0:T(8,128)(2,1)S(1)}, bf16[4,80,256]{2,1,0:T(8,128)(2,1)S(1)}, u32[]{:S(2)}, u32[]{:S(2)}) %collective-permute-start.3) | collective-permute-done | bytes 163872 | tf_op jit(solution)/shard_map/ppermute | solution.py:421
  23.5 0.2 edge.1
  23.7 2.9 %collective-permute-start.4 = (bf16[8,16,256]{2,1,0:T(8,128)(2,1)S(1)}, bf16[8,16,256]{2,1,0:T(8,128)(2,1)S(1)}, u32[]{:S(2)}, u32[]{:S(2)}) collective-permute-start(bf16[8,16,256]{2,1,0:T(8,128)(2,1)S(1)} %edge.1), channel_id=1, source_target_pairs={{0,7},{1,0},{2,1},{3,2},{4,3},{5,4},{6,5},{7,6},{8,15},{9,8},{10,9... | collective-permute-start | bytes 196616 | tf_op jit(solution)/shard_map/ppermute | solution.py:421
  26.6 1.8 %early.1 = (bf16[6,10,64,256]{3,2,1,0:T(8,128)(2,1)S(1)}, f32[512,256]{1,0:T(8,128)S(1)}, bf16[3,128,16]{2,1,0:T(8,128)(2,1)S(1)}) custom-call(bf16[4,144,256]{2,1,0:T(8,128)(2,1)S(1)} %get-tuple-element.25.g_ref, bf16[4,80,256]{2,1,0:T(8,128)(2,1)S(1)} %collective-permute-done.3.h_ref, bf16[6912,256]{1,0:T(8,128)(2,1)S(1)} %get-tuple-element.24.k1, ...), custom_call_target="tpu_custom_call" | custom-call | flops 3000000000 | bytes 10000 | tf_op jit(solution)/shard_map/early/pallas_call | solution.py:461
  28.4 0.0 collective-permute-done.4.w_ref
  28.4 1.4 %middle.1 = (bf16[12,64,256]{2,1,0:T(8,128)(2,1)S(1)}, bf16[8,64,256]{2,1,0:T(8,128)(2,1)S(1)}, bf16[9,5,16,256]{3,2,1,0:T(8,128)(2,1)S(1)}) custom-call(bf16[4,144,256]{2,1,0:T(8,128)(2,1)S(1)} %get-tuple-element.25.g_ref, bf16[4,80,256]{2,1,0:T(8,128)(2,1)S(1)} %collective-permute-done.3.h_ref, bf16[8,16,256]{2,1,0:T(8,128)(2,1)S(1)} %collective-permute-done.4.w_ref, ...), custom_call_target="tpu_custom_call" | custom-call | flops 3000000000 | bytes 10000 | tf_op jit(solution)/shard_map/middle/pallas_call | solution.py:470
  29.8 2.2 %main.1 = (bf16[3584,128]{1,0:T(8,128)(2,1)S(1)}, bf16[3584,128]{1,0:T(8,128)(2,1)S(1)}) custom-call(bf16[8,16,256]{2,1,0:T(8,128)(2,1)S(1)} %collective-permute-done.4.w_ref, bf16[3,10,64,256]{3,2,1,0:T(8,128)(2,1)S(1)} %get-tuple-element.26.xa_ref, bf16[6,10,64,256]{3,2,1,0:T(8,128)(2,1)S(1)} %get-tuple-element.28.xb_ref, ...), custom_call_target="tpu_custom_call" | custom-call | flops 5000000000 | bytes 10000 | tf_op jit(solution)/shard_map/main/pallas_call | solution.py:487
  32.1 0.8 %collective-permute-start.5 = (bf16[3584,128]{1,0:T(8,128)(2,1)S(1)}, bf16[3584,128]{1,0:T(8,128)(2,1)S(1)}, u32[]{:S(2)}, u32[]{:S(2)}) collective-permute-start(bf16[3584,128]{1,0:T(8,128)(2,1)S(1)} %get-tuple-element.36), channel_id=1, source_target_pairs={{0,8},{8,0},{16,24},{24,16},{32,40},{40,32},{48,56},{56,48},{1,9},... | collective-permute-start | bytes 2752520 | tf_op jit(solution)/shard_map/ppermute | solution.py:495
  32.9 1.6 %clip.1 = (f32[2,64,256]{2,1,0:T(8,128)S(1)}, bf16[2,32,256]{2,1,0:T(8,128)(2,1)S(1)}, bf16[2,16,256]{2,1,0:T(8,128)(2,1)S(1)}) custom-call(bf16[12,64,256]{2,1,0:T(8,128)(2,1)S(1)} %get-tuple-element.32.gp, bf16[6912,256]{1,0:T(8,128)(2,1)S(1)} %get-tuple-element.23.after_ref.k1t), custom_call_target="tpu_custom_call" | custom-call | flops 1000000000 | bytes 10000 | tf_op jit(solution)/shard_map/clip/pallas_call | solution.py:496
  34.5 0.5 collective-permute-done.5.other_ref
  35.0 1.0 %join.1 = bf16[3584,128]{1,0:T(8,128)(2,1)} custom-call(bf16[3584,128]{1,0:T(8,128)(2,1)S(1)} %get-tuple-element.35.mine_ref, bf16[3584,128]{1,0:T(8,128)(2,1)S(1)} %collective-permute-done.5.other_ref, f32[2,64,256]{2,1,0:T(8,128)S(1)} %get-tuple-element.37.after_ref.own_ref), custom_call_target="tpu_custom_call" | custom-call | flops 1000000 | bytes 10000 | tf_op jit(solution)/shard_map/join/pallas_call | solution.py:504
  36.0 7.4 %all-to-all-start = ((bf16[32,112,128]{2,1,0:T(8,128)(2,1)}), bf16[32,112,128]{2,1,0:T(8,128)(2,1)S(1)}, u32[]{:S(2)}, u32[]{:S(2)}) async-start(bf16[32,112,128]{2,1,0:T(8,128)(2,1)} %bitcast.2), calls=%async_computation | async-start | bytes 1835008 | tf_op jit(solution)/shard_map/all_to_all | solution.py:518
  43.4 1.8 %collective-permute-start.7 = (bf16[2,32,256]{2,1,0:T(8,128)(2,1)S(1)}, bf16[2,32,256]{2,1,0:T(8,128)(2,1)S(1)}, u32[]{:S(2)}, u32[]{:S(2)}) collective-permute-start(bf16[2,32,256]{2,1,0:T(8,128)(2,1)S(1)} %get-tuple-element.39), channel_id=1, source_target_pairs={{0,8},{8,16},{16,24},{24,32},{32,40},{40,48},{48,56},{56,0},{1,9},... | collective-permute-start | bytes 98312 | tf_op jit(solution)/shard_map/ppermute | solution.py:421
  45.3 1.2 %collective-permute-start.6 = (bf16[2,16,256]{2,1,0:T(8,128)(2,1)S(1)}, bf16[2,16,256]{2,1,0:T(8,128)(2,1)S(1)}, u32[]{:S(2)}, u32[]{:S(2)}) collective-permute-start(bf16[2,16,256]{2,1,0:T(8,128)(2,1)S(1)} %get-tuple-element.38), channel_id=1, source_target_pairs={{0,1},{1,2},{2,3},{3,4},{4,5},{5,6},{6,7},{7,0},{8,9},{9,10},{10,1... | collective-permute-start | bytes 49160 | tf_op jit(solution)/shard_map/ppermute | solution.py:421
  46.5 1.3 %collective-permute-start.8 = (bf16[2,16,256]{2,1,0:T(8,128)(2,1)S(1)}, bf16[2,16,256]{2,1,0:T(8,128)(2,1)S(1)}, u32[]{:S(2)}, u32[]{:S(2)}) collective-permute-start(bf16[2,16,256]{2,1,0:T(8,128)(2,1)S(1)} %get-tuple-element.38), channel_id=1, source_target_pairs={{0,9},{1,10},{2,11},{3,12},{4,13},{5,14},{6,15},{7,8},{8,17},{9,18... | collective-permute-start | bytes 49160 | tf_op jit(solution)/shard_map/ppermute | solution.py:514
  47.7 10.1 %collective-permute-done.6.spill_ref = bf16[2,16,256]{2,1,0:T(8,128)(2,1)S(1)} collective-permute-done((bf16[2,16,256]{2,1,0:T(8,128)(2,1)S(1)}, bf16[2,16,256]{2,1,0:T(8,128)(2,1)S(1)}, u32[]{:S(2)}, u32[]{:S(2)}) %collective-permute-start.6) | collective-permute-done | bytes 16416 | tf_op jit(solution)/shard_map/ppermute | solution.py:421
  57.8 0.8 %collective-permute-done.8.corner_ref = bf16[2,16,256]{2,1,0:T(8,128)(2,1)S(1)} collective-permute-done((bf16[2,16,256]{2,1,0:T(8,128)(2,1)S(1)}, bf16[2,16,256]{2,1,0:T(8,128)(2,1)S(1)}, u32[]{:S(2)}, u32[]{:S(2)}) %collective-permute-start.8) | collective-permute-done | bytes 16416 | tf_op jit(solution)/shard_map/ppermute | solution.py:514
  58.6 0.0 collective-permute-done.7.past_ref
  58.6 0.6 %all-to-all-done.parts_ref = bf16[32,112,128]{2,1,0:T(8,128)(2,1)S(1)} async-done(((bf16[32,112,128]{2,1,0:T(8,128)(2,1)}), bf16[32,112,128]{2,1,0:T(8,128)(2,1)S(1)}, u32[]{:S(2)}, u32[]{:S(2)}) %all-to-all-start) | async-done | bytes 917536 | tf_op jit(solution)/shard_map/all_to_all | solution.py:518
  59.3 0.8 %finish.1 = (bf16[2,64,256]{2,1,0:T(8,128)(2,1)}, f32[64,108]{1,0:T(8,128)}, f32[64,108]{1,0:T(8,128)}) custom-call(bf16[32,112,128]{2,1,0:T(8,128)(2,1)S(1)} %all-to-all-done.parts_ref, f32[2,64,256]{2,1,0:T(8,128)S(1)} %get-tuple-element.37.after_ref.own_ref, bf16[2,16,256]{2,1,0:T(8,128)(2,1)S(1)} %collective-permute-done.6.spill_ref, ...), custom_call_target="tpu_custom_call" | custom-call | flops 1000000 | bytes 10000 | tf_op jit(solution)/shard_map/finish/pallas_call | solution.py:519
  (1 shorter events, 0.0 us)
Async XLA Ops:
  1.5 16.0 %collective-permute-start = (bf16[144,256]{1,0:T(8,128)(2,1)S(1)}, bf16[144,256]{1,0:T(8,128)(2,1)S(1)}, u32[]{:S(2)}, u32[]{:S(2)}) collective-permute-start(bf16[144,256]{1,0:T(8,128)(2,1)S(1)} %pack.1.after_ref.own_ref), channel_id=1, source_target_pairs={{0,64},{64,128},{128,192},{192,0},{1,65},{65,129},{129,193},{193,1... | collective-permute-start | bytes 221192 | tf_op jit(solution)/shard_map/ppermute | solution.py:421
  5.3 12.1 %collective-permute-start.1 = (bf16[144,256]{1,0:T(8,128)(2,1)S(1)}, bf16[144,256]{1,0:T(8,128)(2,1)S(1)}, u32[]{:S(2)}, u32[]{:S(2)}) collective-permute-start(bf16[144,256]{1,0:T(8,128)(2,1)S(1)} %pack.1.after_ref.own_ref), channel_id=1, source_target_pairs={{0,128},{64,192},{128,0},{192,64},{1,129},{65,193},{129,1},{193,65... | collective-permute-start | bytes 221192 | tf_op jit(solution)/shard_map/ppermute | solution.py:421
  10.5 8.3 %collective-permute-start.2 = (bf16[144,256]{1,0:T(8,128)(2,1)S(1)}, bf16[144,256]{1,0:T(8,128)(2,1)S(1)}, u32[]{:S(2)}, u32[]{:S(2)}) collective-permute-start(bf16[144,256]{1,0:T(8,128)(2,1)S(1)} %pack.1.after_ref.own_ref), channel_id=1, source_target_pairs={{0,192},{64,0},{128,64},{192,128},{1,193},{65,1},{129,65},{193,129... | collective-permute-start | bytes 221192 | tf_op jit(solution)/shard_map/ppermute | solution.py:421
  18.8 4.8 %collective-permute-start.3 = (bf16[4,80,256]{2,1,0:T(8,128)(2,1)S(1)}, bf16[4,80,256]{2,1,0:T(8,128)(2,1)S(1)}, u32[]{:S(2)}, u32[]{:S(2)}) collective-permute-start(bf16[4,80,256]{2,1,0:T(8,128)(2,1)S(1)} %head.1.after_ref), channel_id=1, source_target_pairs={{0,56},{8,0},{16,8},{24,16},{32,24},{40,32},{48,40},{56,48},{1,57}... | collective-permute-start | bytes 491528 | tf_op jit(solution)/shard_map/ppermute | solution.py:421
  23.7 4.7 %collective-permute-start.4 = (bf16[8,16,256]{2,1,0:T(8,128)(2,1)S(1)}, bf16[8,16,256]{2,1,0:T(8,128)(2,1)S(1)}, u32[]{:S(2)}, u32[]{:S(2)}) collective-permute-start(bf16[8,16,256]{2,1,0:T(8,128)(2,1)S(1)} %edge.1), channel_id=1, source_target_pairs={{0,7},{1,0},{2,1},{3,2},{4,3},{5,4},{6,5},{7,6},{8,15},{9,8},{10,9... | collective-permute-start | bytes 196616 | tf_op jit(solution)/shard_map/ppermute | solution.py:421
  32.1 2.9 %collective-permute-start.5 = (bf16[3584,128]{1,0:T(8,128)(2,1)S(1)}, bf16[3584,128]{1,0:T(8,128)(2,1)S(1)}, u32[]{:S(2)}, u32[]{:S(2)}) collective-permute-start(bf16[3584,128]{1,0:T(8,128)(2,1)S(1)} %get-tuple-element.36), channel_id=1, source_target_pairs={{0,8},{8,0},{16,24},{24,16},{32,40},{40,32},{48,56},{56,48},{1,9},... | collective-permute-start | bytes 2752520 | tf_op jit(solution)/shard_map/ppermute | solution.py:495
  36.0 23.3 %all-to-all-start = ((bf16[32,112,128]{2,1,0:T(8,128)(2,1)}), bf16[32,112,128]{2,1,0:T(8,128)(2,1)S(1)}, u32[]{:S(2)}, u32[]{:S(2)}) async-start(bf16[32,112,128]{2,1,0:T(8,128)(2,1)} %bitcast.2), calls=%async_computation | async-start | bytes 1835008 | tf_op jit(solution)/shard_map/all_to_all | solution.py:518
  43.4 15.2 %collective-permute-start.7 = (bf16[2,32,256]{2,1,0:T(8,128)(2,1)S(1)}, bf16[2,32,256]{2,1,0:T(8,128)(2,1)S(1)}, u32[]{:S(2)}, u32[]{:S(2)}) collective-permute-start(bf16[2,32,256]{2,1,0:T(8,128)(2,1)S(1)} %get-tuple-element.39), channel_id=1, source_target_pairs={{0,8},{8,16},{16,24},{24,32},{32,40},{40,48},{48,56},{56,0},{1,9},... | collective-permute-start | bytes 98312 | tf_op jit(solution)/shard_map/ppermute | solution.py:421
  45.3 12.5 %collective-permute-start.6 = (bf16[2,16,256]{2,1,0:T(8,128)(2,1)S(1)}, bf16[2,16,256]{2,1,0:T(8,128)(2,1)S(1)}, u32[]{:S(2)}, u32[]{:S(2)}) collective-permute-start(bf16[2,16,256]{2,1,0:T(8,128)(2,1)S(1)} %get-tuple-element.38), channel_id=1, source_target_pairs={{0,1},{1,2},{2,3},{3,4},{4,5},{5,6},{6,7},{7,0},{8,9},{9,10},{10,1... | collective-permute-start | bytes 49160 | tf_op jit(solution)/shard_map/ppermute | solution.py:421
  46.5 12.2 %collective-permute-start.8 = (bf16[2,16,256]{2,1,0:T(8,128)(2,1)S(1)}, bf16[2,16,256]{2,1,0:T(8,128)(2,1)S(1)}, u32[]{:S(2)}, u32[]{:S(2)}) collective-permute-start(bf16[2,16,256]{2,1,0:T(8,128)(2,1)S(1)} %get-tuple-element.38), channel_id=1, source_target_pairs={{0,9},{1,10},{2,11},{3,12},{4,13},{5,14},{6,15},{7,8},{8,17},{9,18... | collective-permute-start | bytes 49160 | tf_op jit(solution)/shard_map/ppermute | solution.py:514

commit v7 on v6

--- a/solution.py
+++ b/solution.py
@@ -1,3 +1,5 @@
+import functools
+
 import jax
 import jax.numpy as jnp
 from jax import lax
@@ -14,6 +16,7 @@
 PART = 27 * C // (HA * WA)
 SLOT = 112
 PEERS = HA * WA // 2
+HALF = PEERS * SLOT // 2
 TAPS = [(a, b, c) for a in range(3) for b in range(3) for c in range(3)]
 BF16, F32 = jnp.bfloat16, jnp.float32
 VMEM_BYTES = 28 * 1024 * 1024
@@ -259,7 +262,7 @@
 
 
 def main_kernel(
-    w_ref, xa_ref, xb_ref, edge_ref, gp, act, cu, mine_ref, other_ref, xc, tt
+    w_ref, xa_ref, xb_ref, edge_ref, gp, act, cu, mine_ref, mine2_ref, other_ref, other2_ref, xc, tt
 ):
     ta, core = lax.axis_index("ta"), lax.rem(lax.axis_index("ha"), 2)
 
@@ -301,19 +304,21 @@
         tt[i * C : (i + 1) * C] = both.T.astype(F32)
     tt[27 * C :] = jnp.zeros((8, 2 * SHARE), F32)
 
-    def cut(out_ref, parity):
+    def cut(out_refs, parity):
         for x in range(HA // 2):
             for w in range(WA):
                 first = ((x * 2 + parity) * WA + w) * PART
                 spot = (x * WA + w) * SLOT
-                out_ref[spot : spot + SLOT] = tt[first : first + SLOT].astype(BF16)
+                ref = out_refs[spot // HALF]
+                spot %= HALF
+                ref[spot : spot + SLOT] = tt[first : first + SLOT].astype(BF16)
 
     for parity in range(2):
 
         @pl.when(core == parity)
         def _(parity=parity):
-            cut(mine_ref, parity)
-            cut(other_ref, 1 - parity)
+            cut((mine_ref, mine2_ref), parity)
+            cut((other_ref, other2_ref), 1 - parity)
 
 
 MAIN = (R + 2) * W
@@ -346,16 +351,17 @@
     return jnp.where(place == 0, first, jnp.where(place == 1, second, 0.0))
 
 
-STAGES = 4
-
-
-def join_kernel(mine_ref, other_ref, after_ref, out_ref, joined, sems):
-    rows = PEERS * SLOT // STAGES
+STAGES = 2
+
+
+def join_kernel(part, mine_ref, other_ref, after_ref, out_ref, joined, sems):
+    rows = HALF // STAGES
     copies = []
     for i in range(STAGES):
-        part = pl.ds(i * rows, rows)
-        joined[part] = mine_ref[part] + other_ref[part]
-        copies.append(pltpu.make_async_copy(joined.at[part], out_ref.at[part], sems.at[i]))
+        spot = pl.ds(i * rows, rows)
+        joined[spot] = mine_ref[spot] + other_ref[spot]
+        there = pl.ds(part * HALF + i * rows, rows)
+        copies.append(pltpu.make_async_copy(joined.at[spot], out_ref.at[there], sems.at[i]))
         copies[-1].start()
     for copy in copies:
         copy.wait()
@@ -387,13 +393,14 @@
     return pl.BlockSpec(memory_space=pltpu.VMEM)
 
 
-def call(kernel, outs, specs, scratch, flops, name, out=None):
+def call(kernel, outs, specs, scratch, flops, name, out=None, aliases={}):
     return pl.pallas_call(
         kernel,
         out_shape=outs,
         in_specs=specs,
         out_specs=jax.tree.map(lambda _: out or whole(), outs),
         scratch_shapes=scratch,
+        input_output_aliases=aliases,
         compiler_params=pltpu.CompilerParams(vmem_limit_bytes=VMEM_BYTES),
         cost_estimate=pl.CostEstimate(flops=flops, bytes_accessed=10_000, transcendentals=0),
         name=name,
@@ -484,15 +491,16 @@
         "middle",
     )(g, h, w, k1, kdt, pre)
     gp, act, cu = in_vmem(gp), in_vmem(act), in_vmem(cu)
-    mine, other = call(
+    mine, mine2, other, other2 = call(
         main_kernel,
-        [shape((PEERS * SLOT, 2 * SHARE)), shape((PEERS * SLOT, 2 * SHARE))],
+        [shape((HALF, 2 * SHARE))] * 4,
         [whole()] * 7,
         [pltpu.VMEM((6, T + 2, 64, C), BF16), pltpu.VMEM((27 * C + 8, 2 * SHARE), F32)],
         5 * 10**9,
         "main",
     )(w, xa, xb, edge, gp, act, cu)
-    other = lax.ppermute(other, "ha", [(i, i ^ 1) for i in range(HA)])
+    cores = [(i, i ^ 1) for i in range(HA)]
+    other, other2 = lax.ppermute(other, "ha", cores), lax.ppermute(other2, "ha", cores)
     own, past, spill = call(
         clip_kernel,
         [shape((F, R * W, C), F32), shape((F, 2 * W, C)), shape((F, SPILL, C))],
@@ -501,15 +509,18 @@
         10**9,
         "clip",
     )(gp, k1t)
-    pair = call(
-        join_kernel,
-        shape((PEERS * SLOT, 2 * SHARE)),
-        [whole(), whole(), anywhere],
-        [pltpu.VMEM((PEERS * SLOT, 2 * SHARE), BF16), dma((STAGES,))],
-        10**6,
-        "join",
-        anywhere,
-    )(mine, other, own)
+    pair = own
+    for part, (x, y) in enumerate(((mine, other), (mine2, other2))):
+        pair = call(
+            functools.partial(join_kernel, part),
+            shape((PEERS * SLOT, 2 * SHARE)),
+            [whole(), whole(), anywhere],
+            [pltpu.VMEM((HALF, 2 * SHARE), BF16), dma((STAGES,))],
+            10**6,
+            "join" + str(part),
+            anywhere,
+            aliases={2: 0} if part else {},
+        )(x, y, pair)
     pairs = [(i * WA + j, (i + 1) % HA * WA + (j + 1) % WA) for i in range(HA) for j in range(WA)]
     corner = lax.ppermute(spill, ("ha", "wa"), pairs)
     spill = shift(spill, "wa", 1)

time: 60.4 us -> 60.4 us (level)
  waiting for transfers between devices: 16.6 us -> 15.8 us
  Pallas kernels: 15.4 us -> 16.1 us
    pallas_call x2 -> x3, Pallas kernels: 3.25 us -> 3.91 us  [the longest x1 2.24 us: local(): call(main_kernel, [shape((HALF, 2 * SHARE))] * 4, [whole()] * 7, [pltpu.V...]
  transfers between devices with their start and end apart: 10 -> 11, of which waited for: 6 -> 5; matrix products, arithmetic and copies ran while one was open for 0% -> 0% of each run, Pallas kernels for 15% -> 16%
where the time goes in v7:
time: 60.4 us; the launch traced here: 60.1 us
  starting transfers between devices  27.4 us (45%)
  Pallas kernels  16.1 us (27%)
  waiting for transfers between devices  15.8 us (26%)
  between operations  0.76 us (1%)
    ppermute x7, starting transfers between devices, shift(): return lax.ppermute(x, axis, [(i, (i + by) % count) for i in range(count)])  17.9 us
    ppermute x7, waiting for transfers between devices, shift(): return lax.ppermute(x, axis, [(i, (i + by) % count) for i in range(count)])  14.3 us
    all_to_all x1, starting transfers between devices, local(): lax.all_to_all(pair, ('ha', 'wa'), 0, 0, axis_index_groups=groups, tiled=...  7.26 us
    pallas_call x1, Pallas kernels, local(): call(load_kernel, [weight] * 3, [anywhere] * 3, [pltpu.VMEM((27 * C, C),...  4.6 us
    pallas_call x1, Pallas kernels, local(): call(main_kernel, [shape((HALF, 2 * SHARE))] * 4, [whole()] * 7, [pltpu.V...  2.24 us
    pallas_call x1, Pallas kernels, local(): call(early_kernel, [on_chip((6, T + 2, 64, C)), on_chip((T * 64, C), F32)...  1.81 us
    pallas_call x2, Pallas kernels, local(): call(functools.partial(join_kernel, part), shape((PEERS * SLOT, 2 * SHARE...  1.66 us
    pallas_call x1, Pallas kernels, local(): call(clip_kernel, [shape((F, R * W, C), F32), shape((F, 2 * W, C)), shape...  1.57 us
  transfers between devices with their start and end apart: 11, of which 5 were waited for; matrix products, arithmetic and copies ran while one was open for 0% of the time, Pallas kernels for 16%

profile of v7, /device:TPU:1, one launch (start us, length us, event | category | flops | bytes accessed | tf_op | source)
XLA Modules:
  0.0 60.1 jit_solution(4321643190935755805)
XLA Ops:
  0.6 0.8 %pack.1.after_ref.own_ref = bf16[144,256]{1,0:T(8,128)(2,1)S(1)} custom-call(bf16[4,32,256]{2,1,0:T(8,128)(2,1)} %bitcast.6, bf16[16,256]{1,0:T(8,128)(2,1)} %bitcast.7), custom_call_target="tpu_custom_call" | custom-call | flops 100000 | bytes 10000 | tf_op jit(solution)/shard_map/pack/pallas_call | solution.py:434
  1.5 3.9 %collective-permute-start = (bf16[144,256]{1,0:T(8,128)(2,1)S(1)}, bf16[144,256]{1,0:T(8,128)(2,1)S(1)}, u32[]{:S(2)}, u32[]{:S(2)}) collective-permute-start(bf16[144,256]{1,0:T(8,128)(2,1)S(1)} %pack.1.after_ref.own_ref), channel_id=1, source_target_pairs={{0,64},{64,128},{128,192},{192,0},{1,65},{65,129},{129,193},{193,1... | collective-permute-start | bytes 221192 | tf_op jit(solution)/shard_map/ppermute | solution.py:428
  5.3 5.1 %collective-permute-start.1 = (bf16[144,256]{1,0:T(8,128)(2,1)S(1)}, bf16[144,256]{1,0:T(8,128)(2,1)S(1)}, u32[]{:S(2)}, u32[]{:S(2)}) collective-permute-start(bf16[144,256]{1,0:T(8,128)(2,1)S(1)} %pack.1.after_ref.own_ref), channel_id=1, source_target_pairs={{0,128},{64,192},{128,0},{192,64},{1,129},{65,193},{129,1},{193,65... | collective-permute-start | bytes 221192 | tf_op jit(solution)/shard_map/ppermute | solution.py:428
  10.5 2.4 %collective-permute-start.2 = (bf16[144,256]{1,0:T(8,128)(2,1)S(1)}, bf16[144,256]{1,0:T(8,128)(2,1)S(1)}, u32[]{:S(2)}, u32[]{:S(2)}) collective-permute-start(bf16[144,256]{1,0:T(8,128)(2,1)S(1)} %pack.1.after_ref.own_ref), channel_id=1, source_target_pairs={{0,192},{64,0},{128,64},{192,128},{1,193},{65,1},{129,65},{193,129... | collective-permute-start | bytes 221192 | tf_op jit(solution)/shard_map/ppermute | solution.py:428
  12.8 4.6 %load.1 = (bf16[6912,256]{1,0:T(8,128)(2,1)S(1)}, bf16[6912,256]{1,0:T(8,128)(2,1)S(1)}, bf16[6912,256]{1,0:T(8,128)(2,1)S(1)}) custom-call(bf16[144,256]{1,0:T(8,128)(2,1)S(1)} %pack.1.after_ref.own_ref, bf16[6912,256]{1,0:T(8,128)(2,1)} %k1_ref.1, bf16[6912,256]{1,0:T(8,128)(2,1)} %kd_ref.1), custom_call_target="tpu_custom_call" | custom-call | flops 4000000000 | bytes 10000 | tf_op jit(solution)/shard_map/load/pallas_call | solution.py:439
  17.5 0.0 collective-permute-done.one_ref
  17.5 0.0 collective-permute-done.1.two_ref
  17.5 1.3 %collective-permute-done.2.three_ref = bf16[144,256]{1,0:T(8,128)(2,1)S(1)} collective-permute-done((bf16[144,256]{1,0:T(8,128)(2,1)S(1)}, bf16[144,256]{1,0:T(8,128)(2,1)S(1)}, u32[]{:S(2)}, u32[]{:S(2)}) %collective-permute-start.2) | collective-permute-done | bytes 73760 | tf_op jit(solution)/shard_map/ppermute | solution.py:428
  18.8 0.5 collective-permute-start.3
  19.3 1.0 %own.1 = (bf16[4,144,256]{2,1,0:T(8,128)(2,1)S(1)}, bf16[3,10,64,256]{3,2,1,0:T(8,128)(2,1)S(1)}, f32[512,256]{1,0:T(8,128)S(1)}) custom-call(bf16[144,256]{1,0:T(8,128)(2,1)S(1)} %pack.1.after_ref.own_ref, bf16[144,256]{1,0:T(8,128)(2,1)S(1)} %collective-permute-done.one_ref, bf16[144,256]{1,0:T(8,128)(2,1)S(1)} %collective-permute-done.1.two_ref, ...), custom_call_target="tpu_custom_call" | custom-call | flops 3000000000 | bytes 10000 | tf_op jit(solution)/shard_map/own/pallas_call | solution.py:457
  20.3 3.2 %collective-permute-done.3.h_ref = bf16[4,80,256]{2,1,0:T(8,128)(2,1)S(1)} collective-permute-done((bf16[4,80,256]{2,1,0:T(8,128)(2,1)S(1)}, bf16[4,80,256]{2,1,0:T(8,128)(2,1)S(1)}, u32[]{:S(2)}, u32[]{:S(2)}) %collective-permute-start.3) | collective-permute-done | bytes 163872 | tf_op jit(solution)/shard_map/ppermute | solution.py:428
  23.5 0.2 edge.1
  23.7 2.9 %collective-permute-start.4 = (bf16[8,16,256]{2,1,0:T(8,128)(2,1)S(1)}, bf16[8,16,256]{2,1,0:T(8,128)(2,1)S(1)}, u32[]{:S(2)}, u32[]{:S(2)}) collective-permute-start(bf16[8,16,256]{2,1,0:T(8,128)(2,1)S(1)} %edge.1), channel_id=1, source_target_pairs={{0,7},{1,0},{2,1},{3,2},{4,3},{5,4},{6,5},{7,6},{8,15},{9,8},{10,9... | collective-permute-start | bytes 196616 | tf_op jit(solution)/shard_map/ppermute | solution.py:428
  26.6 1.8 %early.1 = (bf16[6,10,64,256]{3,2,1,0:T(8,128)(2,1)S(1)}, f32[512,256]{1,0:T(8,128)S(1)}, bf16[3,128,16]{2,1,0:T(8,128)(2,1)S(1)}) custom-call(bf16[4,144,256]{2,1,0:T(8,128)(2,1)S(1)} %get-tuple-element.27.g_ref, bf16[4,80,256]{2,1,0:T(8,128)(2,1)S(1)} %collective-permute-done.3.h_ref, bf16[6912,256]{1,0:T(8,128)(2,1)S(1)} %get-tuple-element.26.k1, ...), custom_call_target="tpu_custom_call" | custom-call | flops 3000000000 | bytes 10000 | tf_op jit(solution)/shard_map/early/pallas_call | solution.py:468
  28.4 0.0 collective-permute-done.4.w_ref
  28.4 1.4 %middle.1 = (bf16[12,64,256]{2,1,0:T(8,128)(2,1)S(1)}, bf16[8,64,256]{2,1,0:T(8,128)(2,1)S(1)}, bf16[9,5,16,256]{3,2,1,0:T(8,128)(2,1)S(1)}) custom-call(bf16[4,144,256]{2,1,0:T(8,128)(2,1)S(1)} %get-tuple-element.27.g_ref, bf16[4,80,256]{2,1,0:T(8,128)(2,1)S(1)} %collective-permute-done.3.h_ref, bf16[8,16,256]{2,1,0:T(8,128)(2,1)S(1)} %collective-permute-done.4.w_ref, ...), custom_call_target="tpu_custom_call" | custom-call | flops 3000000000 | bytes 10000 | tf_op jit(solution)/shard_map/middle/pallas_call | solution.py:477
  29.8 2.2 %main.1 = (bf16[1792,128]{1,0:T(8,128)(2,1)S(1)}, bf16[1792,128]{1,0:T(8,128)(2,1)S(1)}, bf16[1792,128]{1,0:T(8,128)(2,1)S(1)}, bf16[1792,128]{1,0:T(8,128)(2,1)S(1)}) custom-call(bf16[8,16,256]{2,1,0:T(8,128)(2,1)S(1)} %collective-permute-done.4.w_ref, bf16[3,10,64,256]{3,2,1,0:T(8,128)(2,1)S(1)} %get-tuple-element.28.xa_ref, ...), custom_call_target="tpu_custom_call" | custom-call | flops 5000000000 | bytes 10000 | tf_op jit(solution)/shard_map/main/pallas_call | solution.py:494
  32.1 0.7 %collective-permute-start.6 = (bf16[1792,128]{1,0:T(8,128)(2,1)S(1)}, bf16[1792,128]{1,0:T(8,128)(2,1)S(1)}, u32[]{:S(2)}, u32[]{:S(2)}) collective-permute-start(bf16[1792,128]{1,0:T(8,128)(2,1)S(1)} %get-tuple-element.40), channel_id=1, source_target_pairs={{0,8},{8,0},{16,24},{24,16},{32,40},{40,32},{48,56},{56,48},{1,9},... | collective-permute-start | bytes 1376264 | tf_op jit(solution)/shard_map/ppermute | solution.py:503
  32.7 0.3 collective-permute-start.5
  33.0 1.6 %clip.1 = (f32[2,64,256]{2,1,0:T(8,128)S(1)}, bf16[2,32,256]{2,1,0:T(8,128)(2,1)S(1)}, bf16[2,16,256]{2,1,0:T(8,128)(2,1)S(1)}) custom-call(bf16[12,64,256]{2,1,0:T(8,128)(2,1)S(1)} %get-tuple-element.34.gp, bf16[6912,256]{1,0:T(8,128)(2,1)S(1)} %get-tuple-element.25.after_ref.k1t), custom_call_target="tpu_custom_call" | custom-call | flops 1000000000 | bytes 10000 | tf_op jit(solution)/shard_map/clip/pallas_call | solution.py:504
  34.6 0.0 collective-permute-done.6.other_ref
  34.6 0.8 %join0.1.after_ref = bf16[3584,128]{1,0:T(8,128)(2,1)} custom-call(bf16[1792,128]{1,0:T(8,128)(2,1)S(1)} %get-tuple-element.39.mine_ref, bf16[1792,128]{1,0:T(8,128)(2,1)S(1)} %collective-permute-done.6.other_ref, f32[2,64,256]{2,1,0:T(8,128)S(1)} %get-tuple-element.41.after_ref.own_ref), custom_call_target="tpu_custom_call" | custom-call | flops 1000000 | bytes 10000 | tf_op jit(solution)/shard_map/join0/pallas_call | solution.py:514
  35.4 0.0 collective-permute-done.5.other_ref
  35.5 0.8 %join1.1 = bf16[3584,128]{1,0:T(8,128)(2,1)} custom-call(bf16[1792,128]{1,0:T(8,128)(2,1)S(1)} %get-tuple-element.37.mine_ref, bf16[1792,128]{1,0:T(8,128)(2,1)S(1)} %collective-permute-done.5.other_ref, bf16[3584,128]{1,0:T(8,128)(2,1)} %join0.1.after_ref), custom_call_target="tpu_custom_call", output_to_operand_aliasing={{}: (2, {})} | custom-call | flops 1000000 | bytes 10000 | tf_op jit(solution)/shard_map/join1/pallas_call | solution.py:514
  36.3 7.3 %all-to-all-start = ((bf16[32,112,128]{2,1,0:T(8,128)(2,1)}), bf16[32,112,128]{2,1,0:T(8,128)(2,1)S(1)}, u32[]{:S(2)}, u32[]{:S(2)}) async-start(bf16[32,112,128]{2,1,0:T(8,128)(2,1)} %bitcast.2), calls=%async_computation | async-start | bytes 1835008 | tf_op jit(solution)/shard_map/all_to_all | solution.py:529
  43.6 2.0 %collective-permute-start.8 = (bf16[2,32,256]{2,1,0:T(8,128)(2,1)S(1)}, bf16[2,32,256]{2,1,0:T(8,128)(2,1)S(1)}, u32[]{:S(2)}, u32[]{:S(2)}) collective-permute-start(bf16[2,32,256]{2,1,0:T(8,128)(2,1)S(1)} %get-tuple-element.43), channel_id=1, source_target_pairs={{0,8},{8,16},{16,24},{24,32},{32,40},{40,48},{48,56},{56,0},{1,9},... | collective-permute-start | bytes 98312 | tf_op jit(solution)/shard_map/ppermute | solution.py:428
  45.5 1.2 %collective-permute-start.7 = (bf16[2,16,256]{2,1,0:T(8,128)(2,1)S(1)}, bf16[2,16,256]{2,1,0:T(8,128)(2,1)S(1)}, u32[]{:S(2)}, u32[]{:S(2)}) collective-permute-start(bf16[2,16,256]{2,1,0:T(8,128)(2,1)S(1)} %get-tuple-element.42), channel_id=1, source_target_pairs={{0,1},{1,2},{2,3},{3,4},{4,5},{5,6},{6,7},{7,0},{8,9},{9,10},{10,1... | collective-permute-start | bytes 49160 | tf_op jit(solution)/shard_map/ppermute | solution.py:428
  46.7 1.3 %collective-permute-start.9 = (bf16[2,16,256]{2,1,0:T(8,128)(2,1)S(1)}, bf16[2,16,256]{2,1,0:T(8,128)(2,1)S(1)}, u32[]{:S(2)}, u32[]{:S(2)}) collective-permute-start(bf16[2,16,256]{2,1,0:T(8,128)(2,1)S(1)} %get-tuple-element.42), channel_id=1, source_target_pairs={{0,9},{1,10},{2,11},{3,12},{4,13},{5,14},{6,15},{7,8},{8,17},{9,18... | collective-permute-start | bytes 49160 | tf_op jit(solution)/shard_map/ppermute | solution.py:525
  48.0 9.8 %collective-permute-done.7.spill_ref = bf16[2,16,256]{2,1,0:T(8,128)(2,1)S(1)} collective-permute-done((bf16[2,16,256]{2,1,0:T(8,128)(2,1)S(1)}, bf16[2,16,256]{2,1,0:T(8,128)(2,1)S(1)}, u32[]{:S(2)}, u32[]{:S(2)}) %collective-permute-start.7) | collective-permute-done | bytes 16416 | tf_op jit(solution)/shard_map/ppermute | solution.py:428
  57.8 1.0 %collective-permute-done.9.corner_ref = bf16[2,16,256]{2,1,0:T(8,128)(2,1)S(1)} collective-permute-done((bf16[2,16,256]{2,1,0:T(8,128)(2,1)S(1)}, bf16[2,16,256]{2,1,0:T(8,128)(2,1)S(1)}, u32[]{:S(2)}, u32[]{:S(2)}) %collective-permute-start.9) | collective-permute-done | bytes 16416 | tf_op jit(solution)/shard_map/ppermute | solution.py:525
  58.8 0.0 collective-permute-done.8.past_ref
  58.8 0.5 all-to-all-done.parts_ref
  59.3 0.8 %finish.1 = (bf16[2,64,256]{2,1,0:T(8,128)(2,1)}, f32[64,108]{1,0:T(8,128)}, f32[64,108]{1,0:T(8,128)}) custom-call(bf16[32,112,128]{2,1,0:T(8,128)(2,1)S(1)} %all-to-all-done.parts_ref, f32[2,64,256]{2,1,0:T(8,128)S(1)} %get-tuple-element.41.after_ref.own_ref, bf16[2,16,256]{2,1,0:T(8,128)(2,1)S(1)} %collective-permute-done.7.spill_ref, ...), custom_call_target="tpu_custom_call" | custom-call | flops 1000000 | bytes 10000 | tf_op jit(solution)/shard_map/finish/pallas_call | solution.py:530
  (1 shorter events, 0.0 us)
Async XLA Ops:
  1.5 16.0 %collective-permute-start = (bf16[144,256]{1,0:T(8,128)(2,1)S(1)}, bf16[144,256]{1,0:T(8,128)(2,1)S(1)}, u32[]{:S(2)}, u32[]{:S(2)}) collective-permute-start(bf16[144,256]{1,0:T(8,128)(2,1)S(1)} %pack.1.after_ref.own_ref), channel_id=1, source_target_pairs={{0,64},{64,128},{128,192},{192,0},{1,65},{65,129},{129,193},{193,1... | collective-permute-start | bytes 221192 | tf_op jit(solution)/shard_map/ppermute | solution.py:428
  5.3 12.1 %collective-permute-start.1 = (bf16[144,256]{1,0:T(8,128)(2,1)S(1)}, bf16[144,256]{1,0:T(8,128)(2,1)S(1)}, u32[]{:S(2)}, u32[]{:S(2)}) collective-permute-start(bf16[144,256]{1,0:T(8,128)(2,1)S(1)} %pack.1.after_ref.own_ref), channel_id=1, source_target_pairs={{0,128},{64,192},{128,0},{192,64},{1,129},{65,193},{129,1},{193,65... | collective-permute-start | bytes 221192 | tf_op jit(solution)/shard_map/ppermute | solution.py:428
  10.5 8.3 %collective-permute-start.2 = (bf16[144,256]{1,0:T(8,128)(2,1)S(1)}, bf16[144,256]{1,0:T(8,128)(2,1)S(1)}, u32[]{:S(2)}, u32[]{:S(2)}) collective-permute-start(bf16[144,256]{1,0:T(8,128)(2,1)S(1)} %pack.1.after_ref.own_ref), channel_id=1, source_target_pairs={{0,192},{64,0},{128,64},{192,128},{1,193},{65,1},{129,65},{193,129... | collective-permute-start | bytes 221192 | tf_op jit(solution)/shard_map/ppermute | solution.py:428
  18.8 4.8 %collective-permute-start.3 = (bf16[4,80,256]{2,1,0:T(8,128)(2,1)S(1)}, bf16[4,80,256]{2,1,0:T(8,128)(2,1)S(1)}, u32[]{:S(2)}, u32[]{:S(2)}) collective-permute-start(bf16[4,80,256]{2,1,0:T(8,128)(2,1)S(1)} %head.1.after_ref), channel_id=1, source_target_pairs={{0,56},{8,0},{16,8},{24,16},{32,24},{40,32},{48,40},{56,48},{1,57}... | collective-permute-start | bytes 491528 | tf_op jit(solution)/shard_map/ppermute | solution.py:428
  23.7 4.7 %collective-permute-start.4 = (bf16[8,16,256]{2,1,0:T(8,128)(2,1)S(1)}, bf16[8,16,256]{2,1,0:T(8,128)(2,1)S(1)}, u32[]{:S(2)}, u32[]{:S(2)}) collective-permute-start(bf16[8,16,256]{2,1,0:T(8,128)(2,1)S(1)} %edge.1), channel_id=1, source_target_pairs={{0,7},{1,0},{2,1},{3,2},{4,3},{5,4},{6,5},{7,6},{8,15},{9,8},{10,9... | collective-permute-start | bytes 196616 | tf_op jit(solution)/shard_map/ppermute | solution.py:428
  32.1 2.5 %collective-permute-start.6 = (bf16[1792,128]{1,0:T(8,128)(2,1)S(1)}, bf16[1792,128]{1,0:T(8,128)(2,1)S(1)}, u32[]{:S(2)}, u32[]{:S(2)}) collective-permute-start(bf16[1792,128]{1,0:T(8,128)(2,1)S(1)} %get-tuple-element.40), channel_id=1, source_target_pairs={{0,8},{8,0},{16,24},{24,16},{32,40},{40,32},{48,56},{56,48},{1,9},... | collective-permute-start | bytes 1376264 | tf_op jit(solution)/shard_map/ppermute | solution.py:503
  32.7 2.7 %collective-permute-start.5 = (bf16[1792,128]{1,0:T(8,128)(2,1)S(1)}, bf16[1792,128]{1,0:T(8,128)(2,1)S(1)}, u32[]{:S(2)}, u32[]{:S(2)}) collective-permute-start(bf16[1792,128]{1,0:T(8,128)(2,1)S(1)} %get-tuple-element.38), channel_id=1, source_target_pairs={{0,8},{8,0},{16,24},{24,16},{32,40},{40,32},{48,56},{56,48},{1,9},... | collective-permute-start | bytes 1376264 | tf_op jit(solution)/shard_map/ppermute | solution.py:503
  36.3 23.0 %all-to-all-start = ((bf16[32,112,128]{2,1,0:T(8,128)(2,1)}), bf16[32,112,128]{2,1,0:T(8,128)(2,1)S(1)}, u32[]{:S(2)}, u32[]{:S(2)}) async-start(bf16[32,112,128]{2,1,0:T(8,128)(2,1)} %bitcast.2), calls=%async_computation | async-start | bytes 1835008 | tf_op jit(solution)/shard_map/all_to_all | solution.py:529
  43.6 15.2 %collective-permute-start.8 = (bf16[2,32,256]{2,1,0:T(8,128)(2,1)S(1)}, bf16[2,32,256]{2,1,0:T(8,128)(2,1)S(1)}, u32[]{:S(2)}, u32[]{:S(2)}) collective-permute-start(bf16[2,32,256]{2,1,0:T(8,128)(2,1)S(1)} %get-tuple-element.43), channel_id=1, source_target_pairs={{0,8},{8,16},{16,24},{24,32},{32,40},{40,48},{48,56},{56,0},{1,9},... | collective-permute-start | bytes 98312 | tf_op jit(solution)/shard_map/ppermute | solution.py:428
  45.5 12.3 %collective-permute-start.7 = (bf16[2,16,256]{2,1,0:T(8,128)(2,1)S(1)}, bf16[2,16,256]{2,1,0:T(8,128)(2,1)S(1)}, u32[]{:S(2)}, u32[]{:S(2)}) collective-permute-start(bf16[2,16,256]{2,1,0:T(8,128)(2,1)S(1)} %get-tuple-element.42), channel_id=1, source_target_pairs={{0,1},{1,2},{2,3},{3,4},{4,5},{5,6},{6,7},{7,0},{8,9},{9,10},{10,1... | collective-permute-start | bytes 49160 | tf_op jit(solution)/shard_map/ppermute | solution.py:428
  46.7 12.1 %collective-permute-start.9 = (bf16[2,16,256]{2,1,0:T(8,128)(2,1)S(1)}, bf16[2,16,256]{2,1,0:T(8,128)(2,1)S(1)}, u32[]{:S(2)}, u32[]{:S(2)}) collective-permute-start(bf16[2,16,256]{2,1,0:T(8,128)(2,1)S(1)} %get-tuple-element.42), channel_id=1, source_target_pairs={{0,9},{1,10},{2,11},{3,12},{4,13},{5,14},{6,15},{7,8},{8,17},{9,18... | collective-permute-start | bytes 49160 | tf_op jit(solution)/shard_map/ppermute | solution.py:525

commit v8 on v6

--- a/solution.py
+++ b/solution.py
@@ -90,7 +90,7 @@
 
 def head_kernel(own_ref, one_ref, two_ref, three_ref, after_ref, head_ref):
     for back, ref in enumerate((own_ref, one_ref, two_ref, three_ref)):
-        head_ref[lax.rem(lax.axis_index("ta") + TA - back, TA)] = ref[:HEAD]
+        head_ref[lax.bitwise_xor(lax.axis_index("ta"), back)] = ref[:HEAD]
 
 
 def fetch(source, target, sems):
@@ -147,7 +147,7 @@
     own_ref, one_ref, two_ref, three_ref, after_ref, k1, g_ref, xb, pre
 ):
     for back, ref in enumerate((own_ref, one_ref, two_ref, three_ref)):
-        g_ref[lax.rem(lax.axis_index("ta") + TA - back, TA)] = ref[...]
+        g_ref[lax.bitwise_xor(lax.axis_index("ta"), back)] = ref[...]
     pick = window_pick(0)[:, :64]
     for c in range(3):
         xb[c, 0:2] = jnp.zeros((2, 64, C), BF16)
@@ -160,7 +160,7 @@
     add_taps((pre, None), [x for x in TAPS if x[1] == 0], lambda b, c: xb.at[c], k1)
 
 
-def early_kernel(g_ref, h_ref, k1, pre_ref, xb, pre, edge_ref):
+def early_kernel(g_ref, h_ref, k1, kdt, pre_ref, xb, pre, edge_ref, part, cu):
     picks = [window_pick(b) for b in range(3)]
     for b in range(3):
         edge_ref[b] = picks[b][64:, 96:]
@@ -174,6 +174,31 @@
     taps = [x for x in TAPS if x[1] != 0]
     add_taps((pre, pre_ref), taps, lambda b, c: xb.at[b * 3 + c - 3], k1)
 
+    cot = 2 * F * W
+    m, n = iota((48, 32), 0), iota((48, 32), 1)
+    b, place = div(m, 16), mod(m, 16)
+    kk, mm = div(place, 8), mod(place, 8)
+    r = kk + jnp.where(b < 2, 1, 0)
+    out = (lax.axis_index("ha") == HA - 1) & (b == 0) & (kk == 1)
+    pick = onehot((n == r * 8 + mm) & jnp.logical_not(out))
+    for b in range(3):
+        cu[b, TA] = jnp.zeros((16, C), BF16)
+    for j in range(TA):
+        rows = jnp.concatenate([g_ref[j, cot : cot + 16], h_ref[j, cot : cot + 16]], axis=0)
+        built = dot(pick, rows).astype(BF16)
+        for b in range(3):
+            cu[b, j] = built[b * 16 : (b + 1) * 16]
+    for te in range(2):
+        for ke in range(2):
+            total = None
+            for i, (a, b, c) in enumerate(TAPS):
+                if (a == 1, b == 1, c) != (te == 1, ke == 1, 2):
+                    continue
+                ja = 1 if a < 2 else 0
+                y = dot(cu[b, ja : ja + 4].reshape(64, C), kdt[i * C : (i + 1) * C])
+                total = y if total is None else total + y
+            part[te * 2 + ke] = total
+
 
 SPILL = 16
 
@@ -191,7 +216,7 @@
 
 
 def middle_kernel(
-    g_ref, h_ref, w_ref, k1, kdt, pre_ref, gp, act, cu, pre, act32, fix
+    g_ref, h_ref, w_ref, k1, kdt, pre_ref, part_ref, gp, act, cu, pre, act32, fix
 ):
     ta, last_h, last_w = lax.axis_index("ta"), lax.axis_index("ha") == HA - 1, lax.axis_index("wa") == WA - 1
     cot = 2 * F * W
@@ -234,9 +259,9 @@
     for te in range(2):
         for ke in range(2):
             for ce in range(2):
-                total = None
+                total = part_ref[te * 2 + ke] if ce == 0 else None
                 for i, (a, b, c) in enumerate(TAPS):
-                    if (a == 1, b == 1, c == 1) != (te == 1, ke == 1, ce == 1):
+                    if c == 2 or (a == 1, b == 1, c == 1) != (te == 1, ke == 1, ce == 1):
                         continue
                     ja = 1 if a < 2 else 0
                     y = dot(cu[b * 3 + c, ja : ja + 4].reshape(64, C), kdt[i * C : (i + 1) * C])
@@ -285,8 +310,9 @@
             upper[a * 9 + bc] = y[a * SHARE : (a + 1) * SHARE]
     cots = {}
     for bc in range(9):
+        full = dot_t(share, cu[bc].reshape((TA + 1) * 16, C))
         for ja in range(2):
-            cots[bc, ja] = dot_t(share, cu[bc, ja : ja + 4].reshape(64, C)).astype(BF16)
+            cots[bc, ja] = full[:, ja * 16 : ja * 16 + 64].astype(BF16)
     for kind in range(8):
         taps = [
             (i, cots[b * 3 + c, 1 if a < 2 else 0])
@@ -362,7 +388,8 @@
 
 
 def finish_kernel(
-    parts_ref, own_ref, spill_ref, past_ref, corner_ref, clip_ref, conv_ref, down_ref
+    parts_ref, own_ref, spill_ref, past_ref, corner_ref, clip_out, conv_out, down_out,
+    clip_ref, conv_ref, down_ref, sems,
 ):
     for f in range(F):
         spill, corner = spill_ref[f].astype(F32), corner_ref[f].astype(F32)
@@ -375,12 +402,18 @@
                 low += past[at : at + 8] + spilled(corner, R + h)
                 high += past[at + 8 : at + W]
             clip_ref[f, at : at + W] = jnp.concatenate([low, high], axis=0).astype(BF16)
+    leaving = [pltpu.make_async_copy(clip_ref, clip_out, sems.at[0])]
+    leaving[0].start()
     total = parts_ref[0].astype(F32)
     for i in range(1, PEERS):
         total += parts_ref[i].astype(F32)
     total = jnp.concatenate([total, jnp.zeros((128 - SLOT, 2 * SHARE), F32)], axis=0).T
-    conv_ref[...] = total[:SHARE, :PART]
-    down_ref[...] = total[SHARE:, :PART]
+    for i, (ref, out) in enumerate(((conv_ref, conv_out), (down_ref, down_out))):
+        ref[...] = total[i * SHARE : (i + 1) * SHARE, :PART]
+        leaving.append(pltpu.make_async_copy(ref, out, sems.at[i + 1]))
+        leaving[-1].start()
+    for copy in leaving:
+        copy.wait()
 
 
 def whole():
@@ -427,7 +460,7 @@
     packed = call(
         pack_kernel, shape((BLOCK, C)), [anywhere] * 2, [dma((5,))], 10**5, "pack"
     )(in_hbm(clip.reshape(2 * F, 2 * W, C)), in_hbm(out_cotangent.reshape(-1, C)))
-    around = [shift(packed, "ta", by) for by in (1, 2, 3)]
+    around = [lax.ppermute(packed, "ta", [(i, i ^ by) for i in range(TA)]) for by in (1, 2, 3)]
     weight = on_chip((27 * C, C))
     k1, k1t, kdt = call(
         load_kernel,
@@ -458,15 +491,15 @@
     xa, pre = in_vmem(xa), in_vmem(pre)
     w = call(edge_kernel, shape((T, 16, C)), [whole()] * 2, [], 10**7, "edge")(g, h)
     w = shift(w, "wa", -1)
-    xb, pre, edge = call(
+    xb, pre, edge, part = call(
         early_kernel,
-        [on_chip((6, T + 2, 64, C)), on_chip((T * 64, C), F32), on_chip((3, 128, 16))],
-        [whole()] * 4,
-        [],
+        [on_chip((6, T + 2, 64, C)), on_chip((T * 64, C), F32), on_chip((3, 128, 16)), on_chip((4, 64, C), F32)],
+        [whole()] * 5,
+        [pltpu.VMEM((3, TA + 1, 16, C), BF16)],
         3 * 10**9,
         "early",
-    )(g, h, k1, pre)
-    xb, pre, edge = in_vmem(xb), in_vmem(pre), in_vmem(edge)
+    )(g, h, k1, kdt, pre)
+    xb, pre, edge, part = in_vmem(xb), in_vmem(pre), in_vmem(edge), in_vmem(part)
     gp, act, cu = call(
         middle_kernel,
         [
@@ -474,7 +507,7 @@
             on_chip((8, 64, C)),
             on_chip((9, TA + 1, 16, C)),
         ],
-        [whole()] * 6,
+        [whole()] * 7,
         [
             pltpu.VMEM((T * 64, C), F32),
             pltpu.VMEM((8, 64, C), F32),
@@ -482,7 +515,7 @@
         ],
         3 * 10**9,
         "middle",
-    )(g, h, w, k1, kdt, pre)
+    )(g, h, w, k1, kdt, pre, part)
     gp, act, cu = in_vmem(gp), in_vmem(act), in_vmem(cu)
     mine, other = call(
         main_kernel,
@@ -520,9 +553,15 @@
         finish_kernel,
         [shape((F, R * W, C)), shape((SHARE, PART), F32), shape((SHARE, PART), F32)],
         [whole()] * 5,
-        [],
+        [
+            pltpu.VMEM((F, R * W, C), BF16),
+            pltpu.VMEM((SHARE, PART), F32),
+            pltpu.VMEM((SHARE, PART), F32),
+            dma((3,)),
+        ],
         10**6,
         "finish",
+        anywhere,
     )(parts.reshape(PEERS, SLOT, 2 * SHARE), own, spill, past, corner)
     grad_clip = grad_clip.reshape(F, R, W, C)
     return (grad_clip, grad_conv.T, grad_down.T)

time: 60.4 us -> 60.4 us (level)
    ppermute x0 -> x3, starting transfers between devices: none -> 9.02 us  [local(): lax.ppermute(packed, 'ta', [(i, i ^ by) for i in range(TA)])]
    ppermute x7 -> x4, starting transfers between devices: 17.8 us -> 9.09 us  [shift(): return lax.ppermute(x, axis, [(i, (i + by) % count) for i in range(count)])]
    ppermute x7 -> x4, waiting for transfers between devices: 14.6 us -> 13 us  [shift(): return lax.ppermute(x, axis, [(i, (i + by) % count) for i in range(count)])]
    ppermute x0 -> x3, waiting for transfers between devices: none -> 1.41 us  [local(): lax.ppermute(packed, 'ta', [(i, i ^ by) for i in range(TA)])]
where the time goes in v8:
time: 60.4 us; the launch traced here: 60.1 us
  starting transfers between devices  26.8 us (44%)
  waiting for transfers between devices  16.8 us (28%)
  Pallas kernels  15.5 us (26%)
  between operations  0.9 us (1%)
    ppermute x4, waiting for transfers between devices, shift(): return lax.ppermute(x, axis, [(i, (i + by) % count) for i in range(count)])  13 us
    ppermute x4, starting transfers between devices, shift(): return lax.ppermute(x, axis, [(i, (i + by) % count) for i in range(count)])  9.09 us
    ppermute x3, starting transfers between devices, local(): lax.ppermute(packed, 'ta', [(i, i ^ by) for i in range(TA)])  9.02 us
    all_to_all x1, starting transfers between devices, local(): lax.all_to_all(pair, ('ha', 'wa'), 0, 0, axis_index_groups=groups, tiled=...  7.19 us
    pallas_call x1, Pallas kernels, local(): call(load_kernel, [weight] * 3, [anywhere] * 3, [pltpu.VMEM((27 * C, C),...  4.6 us
    pallas_call x1, Pallas kernels, local(): call(main_kernel, [shape((PEERS * SLOT, 2 * SHARE)), shape((PEERS * SLOT,...  2.28 us
    pallas_call x1, Pallas kernels, local(): call(early_kernel, [on_chip((6, T + 2, 64, C)), on_chip((T * 64, C), F32)...  2.06 us
    pallas_call x1, Pallas kernels, local(): call(clip_kernel, [shape((F, R * W, C), F32), shape((F, 2 * W, C)), shape...  1.49 us
  transfers between devices with their start and end apart: 10, of which 6 were waited for; matrix products, arithmetic and copies ran while one was open for 0% of the time, Pallas kernels for 15%

profile of v8, /device:TPU:1, one launch (start us, length us, event | category | flops | bytes accessed | tf_op | source)
XLA Modules:
  0.0 60.1 jit_solution(17277891129196217308)
XLA Ops:
  0.6 0.8 %pack.1.after_ref.own_ref = bf16[144,256]{1,0:T(8,128)(2,1)S(1)} custom-call(bf16[4,32,256]{2,1,0:T(8,128)(2,1)} %bitcast.6, bf16[16,256]{1,0:T(8,128)(2,1)} %bitcast.7), custom_call_target="tpu_custom_call" | custom-call | flops 100000 | bytes 10000 | tf_op jit(solution)/shard_map/pack/pallas_call | solution.py:460
  1.5 3.9 %collective-permute-start = (bf16[144,256]{1,0:T(8,128)(2,1)S(1)}, bf16[144,256]{1,0:T(8,128)(2,1)S(1)}, u32[]{:S(2)}, u32[]{:S(2)}) collective-permute-start(bf16[144,256]{1,0:T(8,128)(2,1)S(1)} %pack.1.after_ref.own_ref), channel_id=1, source_target_pairs={{0,64},{64,0},{128,192},{192,128},{1,65},{65,1},{129,193},{193,129... | collective-permute-start | bytes 221192 | tf_op jit(solution)/shard_map/ppermute | solution.py:463
  5.4 5.1 %collective-permute-start.1 = (bf16[144,256]{1,0:T(8,128)(2,1)S(1)}, bf16[144,256]{1,0:T(8,128)(2,1)S(1)}, u32[]{:S(2)}, u32[]{:S(2)}) collective-permute-start(bf16[144,256]{1,0:T(8,128)(2,1)S(1)} %pack.1.after_ref.own_ref), channel_id=1, source_target_pairs={{0,128},{64,192},{128,0},{192,64},{1,129},{65,193},{129,1},{193,65... | collective-permute-start | bytes 221192 | tf_op jit(solution)/shard_map/ppermute | solution.py:463
  10.5 0.0 collective-permute-start.2
  10.5 4.6 %load.1 = (bf16[6912,256]{1,0:T(8,128)(2,1)S(1)}, bf16[6912,256]{1,0:T(8,128)(2,1)S(1)}, bf16[6912,256]{1,0:T(8,128)(2,1)S(1)}) custom-call(bf16[144,256]{1,0:T(8,128)(2,1)S(1)} %pack.1.after_ref.own_ref, bf16[6912,256]{1,0:T(8,128)(2,1)} %k1_ref.1, bf16[6912,256]{1,0:T(8,128)(2,1)} %kd_ref.1), custom_call_target="tpu_custom_call" | custom-call | flops 4000000000 | bytes 10000 | tf_op jit(solution)/shard_map/load/pallas_call | solution.py:465
  15.1 0.0 collective-permute-done.one_ref
  15.1 0.0 collective-permute-done.1.two_ref
  15.1 1.4 %collective-permute-done.2.three_ref = bf16[144,256]{1,0:T(8,128)(2,1)S(1)} collective-permute-done((bf16[144,256]{1,0:T(8,128)(2,1)S(1)}, bf16[144,256]{1,0:T(8,128)(2,1)S(1)}, u32[]{:S(2)}, u32[]{:S(2)}) %collective-permute-start.2) | collective-permute-done | bytes 73760 | tf_op jit(solution)/shard_map/ppermute | solution.py:463
  16.5 1.7 %collective-permute-start.3 = (bf16[4,80,256]{2,1,0:T(8,128)(2,1)S(1)}, bf16[4,80,256]{2,1,0:T(8,128)(2,1)S(1)}, u32[]{:S(2)}, u32[]{:S(2)}) collective-permute-start(bf16[4,80,256]{2,1,0:T(8,128)(2,1)S(1)} %head.1.after_ref), channel_id=1, source_target_pairs={{0,56},{8,0},{16,8},{24,16},{32,24},{40,32},{48,40},{56,48},{1,57}... | collective-permute-start | bytes 491528 | tf_op jit(solution)/shard_map/ppermute | solution.py:454
  18.2 1.0 %own.1 = (bf16[4,144,256]{2,1,0:T(8,128)(2,1)S(1)}, bf16[3,10,64,256]{3,2,1,0:T(8,128)(2,1)S(1)}, f32[512,256]{1,0:T(8,128)S(1)}) custom-call(bf16[144,256]{1,0:T(8,128)(2,1)S(1)} %pack.1.after_ref.own_ref, bf16[144,256]{1,0:T(8,128)(2,1)S(1)} %collective-permute-done.one_ref, bf16[144,256]{1,0:T(8,128)(2,1)S(1)} %collective-permute-done.1.two_ref, ...), custom_call_target="tpu_custom_call" | custom-call | flops 3000000000 | bytes 10000 | tf_op jit(solution)/shard_map/own/pallas_call | solution.py:483
  19.2 3.1 %collective-permute-done.3.h_ref = bf16[4,80,256]{2,1,0:T(8,128)(2,1)S(1)} collective-permute-done((bf16[4,80,256]{2,1,0:T(8,128)(2,1)S(1)}, bf16[4,80,256]{2,1,0:T(8,128)(2,1)S(1)}, u32[]{:S(2)}, u32[]{:S(2)}) %collective-permute-start.3) | collective-permute-done | bytes 163872 | tf_op jit(solution)/shard_map/ppermute | solution.py:454
  22.3 0.2 edge.1
  22.5 4.3 %collective-permute-start.4 = (bf16[8,16,256]{2,1,0:T(8,128)(2,1)S(1)}, bf16[8,16,256]{2,1,0:T(8,128)(2,1)S(1)}, u32[]{:S(2)}, u32[]{:S(2)}) collective-permute-start(bf16[8,16,256]{2,1,0:T(8,128)(2,1)S(1)} %edge.1), channel_id=1, source_target_pairs={{0,7},{1,0},{2,1},{3,2},{4,3},{5,4},{6,5},{7,6},{8,15},{9,8},{10,9... | collective-permute-start | bytes 196616 | tf_op jit(solution)/shard_map/ppermute | solution.py:454
  26.8 2.1 %early.1 = (bf16[6,10,64,256]{3,2,1,0:T(8,128)(2,1)S(1)}, f32[512,256]{1,0:T(8,128)S(1)}, bf16[3,128,16]{2,1,0:T(8,128)(2,1)S(1)}, f32[4,64,256]{2,1,0:T(8,128)S(1)}) custom-call(bf16[4,144,256]{2,1,0:T(8,128)(2,1)S(1)} %get-tuple-element.26.g_ref, bf16[4,80,256]{2,1,0:T(8,128)(2,1)S(1)} %collective-permute-done.3.h_ref, ...), custom_call_target="tpu_custom_call" | custom-call | flops 3000000000 | bytes 10000 | tf_op jit(solution)/shard_map/early/pallas_call | solution.py:494
  28.8 0.0 collective-permute-done.4.w_ref
  28.8 1.2 %middle.1 = (bf16[12,64,256]{2,1,0:T(8,128)(2,1)S(1)}, bf16[8,64,256]{2,1,0:T(8,128)(2,1)S(1)}, bf16[9,5,16,256]{3,2,1,0:T(8,128)(2,1)S(1)}) custom-call(bf16[4,144,256]{2,1,0:T(8,128)(2,1)S(1)} %get-tuple-element.26.g_ref, bf16[4,80,256]{2,1,0:T(8,128)(2,1)S(1)} %collective-permute-done.3.h_ref, bf16[8,16,256]{2,1,0:T(8,128)(2,1)S(1)} %collective-permute-done.4.w_ref, ...), custom_call_target="tpu_custom_call" | custom-call | flops 3000000000 | bytes 10000 | tf_op jit(solution)/shard_map/middle/pallas_call | solution.py:503
  30.1 2.3 %main.1 = (bf16[3584,128]{1,0:T(8,128)(2,1)S(1)}, bf16[3584,128]{1,0:T(8,128)(2,1)S(1)}) custom-call(bf16[8,16,256]{2,1,0:T(8,128)(2,1)S(1)} %collective-permute-done.4.w_ref, bf16[3,10,64,256]{3,2,1,0:T(8,128)(2,1)S(1)} %get-tuple-element.27.xa_ref, bf16[6,10,64,256]{3,2,1,0:T(8,128)(2,1)S(1)} %get-tuple-element.30.xb_ref, ...), custom_call_target="tpu_custom_call" | custom-call | flops 5000000000 | bytes 10000 | tf_op jit(solution)/shard_map/main/pallas_call | solution.py:520
  32.4 0.3 collective-permute-start.5
  32.6 1.5 %clip.1 = (f32[2,64,256]{2,1,0:T(8,128)S(1)}, bf16[2,32,256]{2,1,0:T(8,128)(2,1)S(1)}, bf16[2,16,256]{2,1,0:T(8,128)(2,1)S(1)}) custom-call(bf16[12,64,256]{2,1,0:T(8,128)(2,1)S(1)} %get-tuple-element.34.gp, bf16[6912,256]{1,0:T(8,128)(2,1)S(1)} %get-tuple-element.24.after_ref.k1t), custom_call_target="tpu_custom_call" | custom-call | flops 1000000000 | bytes 10000 | tf_op jit(solution)/shard_map/clip/pallas_call | solution.py:529
  34.1 1.0 %collective-permute-done.5.other_ref = bf16[3584,128]{1,0:T(8,128)(2,1)S(1)} collective-permute-done((bf16[3584,128]{1,0:T(8,128)(2,1)S(1)}, bf16[3584,128]{1,0:T(8,128)(2,1)S(1)}, u32[]{:S(2)}, u32[]{:S(2)}) %collective-permute-start.5) | collective-permute-done | bytes 917536 | tf_op jit(solution)/shard_map/ppermute | solution.py:528
  35.1 1.0 %join.1 = bf16[3584,128]{1,0:T(8,128)(2,1)} custom-call(bf16[3584,128]{1,0:T(8,128)(2,1)S(1)} %get-tuple-element.37.mine_ref, bf16[3584,128]{1,0:T(8,128)(2,1)S(1)} %collective-permute-done.5.other_ref, f32[2,64,256]{2,1,0:T(8,128)S(1)} %get-tuple-element.39.after_ref.own_ref), custom_call_target="tpu_custom_call" | custom-call | flops 1000000 | bytes 10000 | tf_op jit(solution)/shard_map/join/pallas_call | solution.py:537
  36.1 7.2 %all-to-all-start = ((bf16[32,112,128]{2,1,0:T(8,128)(2,1)}), bf16[32,112,128]{2,1,0:T(8,128)(2,1)S(1)}, u32[]{:S(2)}, u32[]{:S(2)}) async-start(bf16[32,112,128]{2,1,0:T(8,128)(2,1)} %bitcast.2), calls=%async_computation | async-start | bytes 1835008 | tf_op jit(solution)/shard_map/all_to_all | solution.py:551
  43.3 1.9 %collective-permute-start.7 = (bf16[2,32,256]{2,1,0:T(8,128)(2,1)S(1)}, bf16[2,32,256]{2,1,0:T(8,128)(2,1)S(1)}, u32[]{:S(2)}, u32[]{:S(2)}) collective-permute-start(bf16[2,32,256]{2,1,0:T(8,128)(2,1)S(1)} %get-tuple-element.41), channel_id=1, source_target_pairs={{0,8},{8,16},{16,24},{24,32},{32,40},{40,48},{48,56},{56,0},{1,9},... | collective-permute-start | bytes 98312 | tf_op jit(solution)/shard_map/ppermute | solution.py:454
  45.3 1.2 %collective-permute-start.6 = (bf16[2,16,256]{2,1,0:T(8,128)(2,1)S(1)}, bf16[2,16,256]{2,1,0:T(8,128)(2,1)S(1)}, u32[]{:S(2)}, u32[]{:S(2)}) collective-permute-start(bf16[2,16,256]{2,1,0:T(8,128)(2,1)S(1)} %get-tuple-element.40), channel_id=1, source_target_pairs={{0,1},{1,2},{2,3},{3,4},{4,5},{5,6},{6,7},{7,0},{8,9},{9,10},{10,1... | collective-permute-start | bytes 49160 | tf_op jit(solution)/shard_map/ppermute | solution.py:454
  46.4 1.3 %collective-permute-start.8 = (bf16[2,16,256]{2,1,0:T(8,128)(2,1)S(1)}, bf16[2,16,256]{2,1,0:T(8,128)(2,1)S(1)}, u32[]{:S(2)}, u32[]{:S(2)}) collective-permute-start(bf16[2,16,256]{2,1,0:T(8,128)(2,1)S(1)} %get-tuple-element.40), channel_id=1, source_target_pairs={{0,9},{1,10},{2,11},{3,12},{4,13},{5,14},{6,15},{7,8},{8,17},{9,18... | collective-permute-start | bytes 49160 | tf_op jit(solution)/shard_map/ppermute | solution.py:547
  47.7 9.9 %collective-permute-done.6.spill_ref = bf16[2,16,256]{2,1,0:T(8,128)(2,1)S(1)} collective-permute-done((bf16[2,16,256]{2,1,0:T(8,128)(2,1)S(1)}, bf16[2,16,256]{2,1,0:T(8,128)(2,1)S(1)}, u32[]{:S(2)}, u32[]{:S(2)}) %collective-permute-start.6) | collective-permute-done | bytes 16416 | tf_op jit(solution)/shard_map/ppermute | solution.py:454
  57.6 0.9 %collective-permute-done.8.corner_ref = bf16[2,16,256]{2,1,0:T(8,128)(2,1)S(1)} collective-permute-done((bf16[2,16,256]{2,1,0:T(8,128)(2,1)S(1)}, bf16[2,16,256]{2,1,0:T(8,128)(2,1)S(1)}, u32[]{:S(2)}, u32[]{:S(2)}) %collective-permute-start.8) | collective-permute-done | bytes 16416 | tf_op jit(solution)/shard_map/ppermute | solution.py:547
  58.5 0.0 collective-permute-done.7.past_ref
  58.5 0.5 all-to-all-done.parts_ref
  59.1 0.8 %finish.1 = (bf16[2,64,256]{2,1,0:T(8,128)(2,1)}, f32[64,108]{1,0:T(8,128)}, f32[64,108]{1,0:T(8,128)}) custom-call(bf16[32,112,128]{2,1,0:T(8,128)(2,1)S(1)} %all-to-all-done.parts_ref, f32[2,64,256]{2,1,0:T(8,128)S(1)} %get-tuple-element.39.after_ref.own_ref, bf16[2,16,256]{2,1,0:T(8,128)(2,1)S(1)} %collective-permute-done.6.spill_ref, ...), custom_call_target="tpu_custom_call" | custom-call | flops 1000000 | bytes 10000 | tf_op jit(solution)/shard_map/finish/pallas_call | solution.py:552
  (1 shorter events, 0.0 us)
Async XLA Ops:
  1.5 13.6 %collective-permute-start = (bf16[144,256]{1,0:T(8,128)(2,1)S(1)}, bf16[144,256]{1,0:T(8,128)(2,1)S(1)}, u32[]{:S(2)}, u32[]{:S(2)}) collective-permute-start(bf16[144,256]{1,0:T(8,128)(2,1)S(1)} %pack.1.after_ref.own_ref), channel_id=1, source_target_pairs={{0,64},{64,0},{128,192},{192,128},{1,65},{65,1},{129,193},{193,129... | collective-permute-start | bytes 221192 | tf_op jit(solution)/shard_map/ppermute | solution.py:463
  5.4 9.7 %collective-permute-start.1 = (bf16[144,256]{1,0:T(8,128)(2,1)S(1)}, bf16[144,256]{1,0:T(8,128)(2,1)S(1)}, u32[]{:S(2)}, u32[]{:S(2)}) collective-permute-start(bf16[144,256]{1,0:T(8,128)(2,1)S(1)} %pack.1.after_ref.own_ref), channel_id=1, source_target_pairs={{0,128},{64,192},{128,0},{192,64},{1,129},{65,193},{129,1},{193,65... | collective-permute-start | bytes 221192 | tf_op jit(solution)/shard_map/ppermute | solution.py:463
  10.5 6.0 %collective-permute-start.2 = (bf16[144,256]{1,0:T(8,128)(2,1)S(1)}, bf16[144,256]{1,0:T(8,128)(2,1)S(1)}, u32[]{:S(2)}, u32[]{:S(2)}) collective-permute-start(bf16[144,256]{1,0:T(8,128)(2,1)S(1)} %pack.1.after_ref.own_ref), channel_id=1, source_target_pairs={{0,192},{64,128},{128,64},{192,0},{1,193},{65,129},{129,65},{193,1... | collective-permute-start | bytes 221192 | tf_op jit(solution)/shard_map/ppermute | solution.py:463
  16.5 5.8 %collective-permute-start.3 = (bf16[4,80,256]{2,1,0:T(8,128)(2,1)S(1)}, bf16[4,80,256]{2,1,0:T(8,128)(2,1)S(1)}, u32[]{:S(2)}, u32[]{:S(2)}) collective-permute-start(bf16[4,80,256]{2,1,0:T(8,128)(2,1)S(1)} %head.1.after_ref), channel_id=1, source_target_pairs={{0,56},{8,0},{16,8},{24,16},{32,24},{40,32},{48,40},{56,48},{1,57}... | collective-permute-start | bytes 491528 | tf_op jit(solution)/shard_map/ppermute | solution.py:454
  22.5 6.4 %collective-permute-start.4 = (bf16[8,16,256]{2,1,0:T(8,128)(2,1)S(1)}, bf16[8,16,256]{2,1,0:T(8,128)(2,1)S(1)}, u32[]{:S(2)}, u32[]{:S(2)}) collective-permute-start(bf16[8,16,256]{2,1,0:T(8,128)(2,1)S(1)} %edge.1), channel_id=1, source_target_pairs={{0,7},{1,0},{2,1},{3,2},{4,3},{5,4},{6,5},{7,6},{8,15},{9,8},{10,9... | collective-permute-start | bytes 196616 | tf_op jit(solution)/shard_map/ppermute | solution.py:454
  32.4 2.7 %collective-permute-start.5 = (bf16[3584,128]{1,0:T(8,128)(2,1)S(1)}, bf16[3584,128]{1,0:T(8,128)(2,1)S(1)}, u32[]{:S(2)}, u32[]{:S(2)}) collective-permute-start(bf16[3584,128]{1,0:T(8,128)(2,1)S(1)} %get-tuple-element.38), channel_id=1, source_target_pairs={{0,8},{8,0},{16,24},{24,16},{32,40},{40,32},{48,56},{56,48},{1,9},... | collective-permute-start | bytes 2752520 | tf_op jit(solution)/shard_map/ppermute | solution.py:528
  36.1 23.0 %all-to-all-start = ((bf16[32,112,128]{2,1,0:T(8,128)(2,1)}), bf16[32,112,128]{2,1,0:T(8,128)(2,1)S(1)}, u32[]{:S(2)}, u32[]{:S(2)}) async-start(bf16[32,112,128]{2,1,0:T(8,128)(2,1)} %bitcast.2), calls=%async_computation | async-start | bytes 1835008 | tf_op jit(solution)/shard_map/all_to_all | solution.py:551
  43.3 15.2 %collective-permute-start.7 = (bf16[2,32,256]{2,1,0:T(8,128)(2,1)S(1)}, bf16[2,32,256]{2,1,0:T(8,128)(2,1)S(1)}, u32[]{:S(2)}, u32[]{:S(2)}) collective-permute-start(bf16[2,32,256]{2,1,0:T(8,128)(2,1)S(1)} %get-tuple-element.41), channel_id=1, source_target_pairs={{0,8},{8,16},{16,24},{24,32},{32,40},{40,48},{48,56},{56,0},{1,9},... | collective-permute-start | bytes 98312 | tf_op jit(solution)/shard_map/ppermute | solution.py:454
  45.3 12.3 %collective-permute-start.6 = (bf16[2,16,256]{2,1,0:T(8,128)(2,1)S(1)}, bf16[2,16,256]{2,1,0:T(8,128)(2,1)S(1)}, u32[]{:S(2)}, u32[]{:S(2)}) collective-permute-start(bf16[2,16,256]{2,1,0:T(8,128)(2,1)S(1)} %get-tuple-element.40), channel_id=1, source_target_pairs={{0,1},{1,2},{2,3},{3,4},{4,5},{5,6},{6,7},{7,0},{8,9},{9,10},{10,1... | collective-permute-start | bytes 49160 | tf_op jit(solution)/shard_map/ppermute | solution.py:454
  46.4 12.1 %collective-permute-start.8 = (bf16[2,16,256]{2,1,0:T(8,128)(2,1)S(1)}, bf16[2,16,256]{2,1,0:T(8,128)(2,1)S(1)}, u32[]{:S(2)}, u32[]{:S(2)}) collective-permute-start(bf16[2,16,256]{2,1,0:T(8,128)(2,1)S(1)} %get-tuple-element.40), channel_id=1, source_target_pairs={{0,9},{1,10},{2,11},{3,12},{4,13},{5,14},{6,15},{7,8},{8,17},{9,18... | collective-permute-start | bytes 49160 | tf_op jit(solution)/shard_map/ppermute | solution.py:547
